TPU v7x, 128 devices: a whole 4x4x4 slice. The times are simulated.
128 devices in a mesh: snap: 16 (over x, z_hi, core), span: 8 (over y, z_lo).
Axes of the slice: x: 4, y: 4, z: 4 (z_hi: 2, z_lo: 2; z = z_hi * 2 + z_lo), core: 2. Of those that a mesh axis runs over, the one named last changes fastest.
Arguments:
- snapshots: bfloat16 [3, 12, 1536, 2048], P(None, None, 'span', 'snap'), may hold values from -12 to 12
Outputs:
- gram: float32 [2048, 2048], P('snap', 'span')
- mirror_gram: float32 [2048, 2048], P('snap', 'span')
All inputs are finite; a program needn't handle non-finite values.
Results may differ from a plain program's by a relative error of at most 0.0003.
Values may be sent and summed in bfloat16 or wider, within the bound.
No kernel may reach another device: no remote copies, remote signals or barrier semaphores. Data moves between devices by JAX's collectives and lax.ppermute only.
A program may use at most 128 MiB of HBM per device.

v0:
```python
import jax
import jax.numpy as jnp
from jax import lax
from jax.sharding import PartitionSpec as P

NZ = 1536
NXW = 12


def from_partner(x, axis, distance):
    return lax.ppermute(x, axis, [(i, i ^ 1 << distance) for i in range(lax.axis_size(axis))])


def inner(left, right):
    return lax.dot_general(
        left, right, (((0,), (0,)), ((), ())), preferred_element_type=jnp.float32
    )


def body(snapshots):
    own = snapshots.shape[3]
    span_count = lax.axis_size("span")
    partner = snapshots
    for bit in range(span_count.bit_length() - 1):
        partner = from_partner(partner, "span", bit)
    sign = jnp.array([1.0, 1.0, -1.0], jnp.bfloat16).reshape(3, 1, 1, 1)
    reflected = jnp.flip(partner, 2) * sign
    scale = 1.0 / (NXW * NZ)
    own_flat = snapshots.reshape(-1, own)
    mirror_flat = reflected.reshape(-1, own)
    piece = lax.all_gather(snapshots, "snap", axis=3, tiled=True)
    columns = piece.reshape(-1, piece.shape[3])
    direct = inner(own_flat, columns)
    flipped = inner(mirror_flat, columns)
    gram = direct
    mirror_gram = flipped
    gram, mirror_gram = (
        lax.psum_scatter(gram, "span", scatter_dimension=1, tiled=True),
        lax.psum_scatter(mirror_gram, "span", scatter_dimension=1, tiled=True),
    )
    return (gram * scale, mirror_gram * scale)


def solution(mesh):
    placed = (P(None, None, "span", "snap"),)
    return jax.shard_map(
        body,
        mesh=mesh,
        in_specs=placed,
        out_specs=(P("snap", "span"), P("snap", "span")),
        check_vma=False,
    )
```

profile of v0, /device:TPU:0, one launch (start us, length us, event | category | flops | bytes accessed | tf_op | source)
XLA Modules:
  0.0 311.4 jit_solution(3456378317906895326)
XLA Ops:
  7.2 0.0 copy-start
  7.2 0.0 all-gather.2.cloned.1.call-start
  7.2 0.7 all-gather.2.cloned.1.call-update
  7.9 0.0 copy-start.1
  7.9 0.0 reduce-scatter.5.cloned.1.call-start
  8.0 0.7 copy-done
  8.6 2.0 collective-permute-start
  10.6 57.6 %collective-permute-done = bf16[3,12,192,128]{3,2,1,0:T(8,128)(2,1)S(1)} collective-permute-done((bf16[3,12,192,128]{3,2,1,0:T(8,128)(2,1)S(1)}, bf16[3,12,192,128]{3,2,1,0:T(8,128)(2,1)S(1)}, u32[]{:S(2)}, u32[]{:S(2)}) %collective-permute-start) | collective-permute-done | bytes 1769504 | tf_op jit(solution)/shard_map/ppermute | solution.py:11
  68.2 1.6 collective-permute-start.1
  69.8 38.2 %collective-permute-done.1 = bf16[3,12,192,128]{3,2,1,0:T(8,128)(2,1)S(1)} collective-permute-done((bf16[3,12,192,128]{3,2,1,0:T(8,128)(2,1)S(1)}, bf16[3,12,192,128]{3,2,1,0:T(8,128)(2,1)S(1)}, u32[]{:S(2)}, u32[]{:S(2)}) %collective-permute-start.1) | collective-permute-done | bytes 1769504 | tf_op jit(solution)/shard_map/ppermute | solution.py:11
  108.0 3.1 collective-permute-start.2
  111.1 37.5 %collective-permute-done.2 = bf16[3,12,192,128]{3,2,1,0:T(8,128)(2,1)} collective-permute-done((bf16[3,12,192,128]{3,2,1,0:T(8,128)(2,1)S(1)}, bf16[3,12,192,128]{3,2,1,0:T(8,128)(2,1)}, u32[]{:S(2)}, u32[]{:S(2)}) %collective-permute-start.2) | collective-permute-done | bytes 1769504 | tf_op jit(solution)/shard_map/ppermute | solution.py:11
  148.5 28.9 %rev.4 = bf16[3,12,192,128]{3,2,1,0:T(8,128)(2,1)S(1)} reverse(bf16[3,12,192,128]{3,2,1,0:T(8,128)(2,1)} %collective-permute-done.2), dimensions={2} | reverse | bytes 3538944 | tf_op jit(solution)/shard_map/jit(_flip)/rev | solution.py:27
  177.4 35.6 %all-gather.2.cloned.1.call-done = bf16[3,12,192,2048]{3,2,1,0:T(8,128)(2,1)} async-done(((bf16[3,12,192,128]{3,2,1,0:T(8,128)(2,1)}), bf16[3,12,192,2048]{3,2,1,0:T(8,128)(2,1)}) %all-gather.2.cloned.1.call-update) | async-done | bytes 28311568 | tf_op jit(solution)/shard_map/all_gather | solution.py:31
  213.0 0.0 copy-done.1
  213.0 12.3 %convolution_bitcast_fusion = f32[128,2048]{1,0:T(8,128)} fusion(bf16[3,12,192,2048]{3,2,1,0:T(8,128)(2,1)} %all-gather.2.cloned.1.call-done, bf16[3,12,192,128]{3,2,1,0:T(8,128)(2,1)S(1)} %rev.4, bf16[3]{0:T(256)(128)(2,1)S(1)} %copy-done.1), kind=kOutput, calls=%fused_computation | convolution fusion | flops 3624763392 | bytes 31129606 | tf_op jit(solution)/shard_map/dot_general | solution.py:15
  225.3 0.0 reduce-scatter.5.cloned.1.call-update
  225.3 0.0 reduce-scatter.3.cloned.1.call-start
  225.3 12.3 %convolution_bitcast_fusion.1 = f32[128,2048]{1,0:T(8,128)} fusion(bf16[3,12,192,128]{3,2,1,0:T(8,128)(2,1)S(1)} %copy-done, bf16[3,12,192,2048]{3,2,1,0:T(8,128)(2,1)} %all-gather.2.cloned.1.call-done), kind=kOutput, calls=%fused_computation.1 | convolution fusion | flops 3623878656 | bytes 31129600 | tf_op jit(solution)/shard_map/dot_general | solution.py:15
  237.6 0.0 reduce-scatter.3.cloned.1.call-update
  237.7 24.8 %reduce-scatter.5.cloned.1.call-done = f32[128,256]{1,0:T(8,128)} async-done(((f32[128,2048]{1,0:T(8,128)}), f32[128,256]{1,0:T(8,128)}) %reduce-scatter.5.cloned.1.call-update) | async-done | bytes 131088 | tf_op jit(solution)/shard_map/reduce_scatter | solution.py:39
  262.4 1.6 broadcast_multiply_fusion
  264.0 39.3 %reduce-scatter.3.cloned.1.call-done = f32[128,256]{1,0:T(8,128)} async-done(((f32[128,2048]{1,0:T(8,128)}), f32[128,256]{1,0:T(8,128)}) %reduce-scatter.3.cloned.1.call-update) | async-done | bytes 131088 | tf_op jit(solution)/shard_map/reduce_scatter | solution.py:38
  303.3 1.6 broadcast_multiply_fusion.1
Async XLA Ops:
  7.2 1.5 copy-start
  7.2 205.8 %all-gather.2.cloned.1.call-start = ((), (), s32[]{:S(2)}) async-start(), calls=%async_computation.2 | async-start | bytes 30081024 | tf_op jit(solution)/shard_map/all_gather | solution.py:31
  7.9 205.1 %copy-start.1 = (bf16[3]{0:T(256)(128)(2,1)S(1)}, bf16[3]{0:T(256)(128)(2,1)}, u32[]{:S(2)}) copy-start(bf16[3]{0:T(256)(128)(2,1)} %constant.4.clone) | copy-start | bytes 22
  7.9 254.5 %reduce-scatter.5.cloned.1.call-start = ((), (), s32[]{:S(2)}) async-start(), calls=%async_computation.4 | async-start | bytes 1179648 | tf_op jit(solution)/shard_map/reduce_scatter | solution.py:39
  8.6 59.6 %collective-permute-start = (bf16[3,12,192,128]{3,2,1,0:T(8,128)(2,1)S(1)}, bf16[3,12,192,128]{3,2,1,0:T(8,128)(2,1)S(1)}, u32[]{:S(2)}, u32[]{:S(2)}) collective-permute-start(bf16[3,12,192,128]{3,2,1,0:T(8,128)(2,1)S(1)} %copy-done), channel_id=1, source_target_pairs={{0,1},{1,0},{2,3},{3,2},{4,5},{5,4},{6,7},{7,6},{8,9},{9,8},{10,11... | collective-permute-start | bytes 5308424 | tf_op jit(solution)/shard_map/ppermute | solution.py:11
  68.2 39.8 %collective-permute-start.1 = (bf16[3,12,192,128]{3,2,1,0:T(8,128)(2,1)S(1)}, bf16[3,12,192,128]{3,2,1,0:T(8,128)(2,1)S(1)}, u32[]{:S(2)}, u32[]{:S(2)}) collective-permute-start(bf16[3,12,192,128]{3,2,1,0:T(8,128)(2,1)S(1)} %collective-permute-done), channel_id=1, source_target_pairs={{0,2},{1,3},{2,0},{3,1},{4,6},{5,7},{6,4},{7,5},{8,10},{9,11},{10,... | collective-permute-start | bytes 5308424 | tf_op jit(solution)/shard_map/ppermute | solution.py:11
  108.0 40.6 %collective-permute-start.2 = (bf16[3,12,192,128]{3,2,1,0:T(8,128)(2,1)S(1)}, bf16[3,12,192,128]{3,2,1,0:T(8,128)(2,1)}, u32[]{:S(2)}, u32[]{:S(2)}) collective-permute-start(bf16[3,12,192,128]{3,2,1,0:T(8,128)(2,1)S(1)} %collective-permute-done.1), channel_id=1, source_target_pairs={{0,4},{1,5},{2,6},{3,7},{4,0},{5,1},{6,2},{7,3},{8,12},{9,13},{10,... | collective-permute-start | bytes 5308424 | tf_op jit(solution)/shard_map/ppermute | solution.py:11
  225.3 78.0 %reduce-scatter.3.cloned.1.call-start = ((), (), s32[]{:S(2)}) async-start(), calls=%async_computation.3 | async-start | bytes 1179648 | tf_op jit(solution)/shard_map/reduce_scatter | solution.py:38
Sparse Core Ops, SparseCore 0:
  10.3 202.6 all-gather.1
  225.4 36.9 reduce-scatter.4
  264.8 38.4 reduce-scatter.2
where the time goes:
time: 314 us; the launch traced here: 311 us
  waiting for transfers between devices  234 us (75%)
  local copies, waits for them, and re-layouts  29.5 us (9%)
  matrix products  24.6 us (8%)
  between operations  13.8 us (4%)
  starting transfers between devices  6.79 us (2%)
  other arithmetic  3.14 us (1%)
    ppermute x3, waiting for transfers between devices, from_partner(): lax.ppermute(x, axis, [(i, i ^ 1 << distance) for i in range(lax.axis_siz...  133 us
    reduce_scatter x1, waiting for transfers between devices, body(): lax.psum_scatter(gram, 'span', scatter_dimension=1, tiled=True)  39.3 us
    all_gather x1, waiting for transfers between devices, body(): piece = lax.all_gather(snapshots, 'snap', axis=3, tiled=True)  35.6 us
    rev x1, local copies, waits for them, and re-layouts, body(): reflected = jnp.flip(partner, 2) * sign  28.9 us
    reduce_scatter x1, waiting for transfers between devices, body(): lax.psum_scatter(mirror_gram, 'span', scatter_dimension=1, tiled=True)  24.8 us
    dot_general x2, matrix products, inner(): lax.dot_general(left, right, (((0,), (0,)), ((), ())), preferred_element_...  24.6 us
    ppermute x3, starting transfers between devices, from_partner(): lax.ppermute(x, axis, [(i, i ^ 1 << distance) for i in range(lax.axis_siz...  6.67 us
  transfers between devices with their start and end apart: 6, of which 6 were waited for; matrix products, arithmetic and copies ran while one was open for 14% of the time, Pallas kernels for 0%

commit v1 on v0

v1 whole, which is shorter than its diff:
```python
import functools

import jax
import jax.numpy as jnp
from jax import lax
from jax.sharding import PartitionSpec as P

NZ = 1536
NXW = 12
AXES = ("snap", "span")
COORDS = [
    (x, h, c, y, l)
    for x in range(4) for h in range(2) for c in range(2) for y in range(4) for l in range(2)
]


def place(x, h, c, y, l):
    return (x % 4 * 4 + h * 2 + c) * 8 + y % 4 * 2 + l


def send(value, target):
    pairs = []
    for at in COORDS:
        to = target(*at)
        if to is not None:
            pairs.append((place(*at), place(*to)))
    return lax.ppermute(value, AXES, pairs)


def inner(left, right):
    return lax.dot_general(
        left, right, (((0,), (0,)), ((), ())), preferred_element_type=jnp.float32
    )


def body(snapshots):
    comps, rows, depth, own = snapshots.shape
    quarter = rows // 4
    count = comps * quarter * depth
    snap, span = lax.axis_index("snap"), lax.axis_index("span")
    x, h, c = snap // 4, snap // 2 % 2, snap % 2
    y, l = span // 2, span % 2
    m = y // 2

    def part(side, group):
        return lax.dynamic_slice_in_dim(snapshots, (side * 2 + group) * quarter, quarter, axis=1)

    sign = jnp.array([1.0, 1.0, -1.0], jnp.bfloat16).reshape(3, 1, 1, 1)
    swap = jnp.flip(jnp.eye(depth, dtype=jnp.bfloat16), 0)

    def reflect(piece):
        turned = lax.dot_general(piece, swap, (((2,), (1,)), ((), ())), preferred_element_type=jnp.bfloat16)
        return jnp.swapaxes(turned, 2, 3) * sign

    flat = lambda piece: piece.reshape(count, own)

    with jax.named_scope("rows"):
        s0 = flat(part(m, h))
        t0 = send(flat(reflect(part(1 - m, h))), lambda x, h, c, y, l: (x, h, c, 3 - y, 1 - l))
        s1 = send(flat(part(m, 1 - h)), lambda x, h, c, y, l: (x, 1 - h, c, y, l))
        t1 = send(flat(reflect(part(1 - m, 1 - h))), lambda x, h, c, y, l: (x, 1 - h, c, 3 - y, 1 - l))

    pieces = (s0, t0, s1, t1)
    with jax.named_scope("cores"):
        other = [send(p, lambda x, h, c, y, l: (x, h, 1 - c, y, l)) for p in pieces]
        left_s = jnp.concatenate([s0, s1, other[0], other[2]], axis=1)
        left_t = jnp.concatenate([t0, t1, other[1], other[3]], axis=1)
        left = jnp.concatenate([left_s, left_t], axis=0)

    with jax.named_scope("next"):
        one = [send(p, lambda x, h, c, y, l: (x - 1, h, c, y, l)) for p in pieces]
    with jax.named_scope("opposite"):
        half = count // 2
        two = []
        for q in range(2):
            pair = jnp.stack(
                [lax.dynamic_slice_in_dim(p, (1 - x // 2) * half, half, axis=0) for p in pieces[2 * q:2 * q + 2]]
            )
            pair = send(pair, lambda x, h, c, y, l: (x + 1, h, c, y, l))
            pair = send(pair, lambda x, h, c, y, l: (x + 1, h, c, y, l))
            two += [pair[0], pair[1]]
        mine = (x // 2) * half
        left_half = jnp.concatenate(
            [
                lax.dynamic_slice_in_dim(left_s, mine, half, axis=0),
                lax.dynamic_slice_in_dim(left_t, mine, half, axis=0),
            ],
            axis=0,
        )

    def products(lhs, s, t):
        right = jnp.concatenate(
            [jnp.concatenate([s, t], axis=1), jnp.concatenate([t, s], axis=1)], axis=0
        )
        return inner(lhs, right).reshape(2, 2, own, 2 * own)

    def over_z(first, second):
        both = jnp.stack([first, second])

        def block(k):
            to = (2 * h + l + k) % 4
            piece = lax.dynamic_index_in_dim(both, (to % 2) ^ h, 0, keepdims=False)
            return lax.dynamic_index_in_dim(piece, (to // 2) ^ h, 1, keepdims=False)

        total = block(0)
        for k in (1, 2, 3):
            def target(x, h, c, y, l, k=k):
                to = (2 * h + l + k) % 4
                return (x, to // 2, c, y, to % 2)
            total = total + send(block(k), target)
        return total

    with jax.named_scope("blocks"):
        summed = [
            over_z(products(left, s0, t0), products(left, s1, t1)),
            over_z(products(left, one[0], one[1]), products(left, one[2], one[3])),
            over_z(products(left_half, two[0], two[1]), products(left_half, two[2], two[3])),
        ]

    with jax.named_scope("over_y"):
        stacked = jnp.stack(summed + [jnp.zeros_like(summed[0])])
        pick = lambda k: lax.dynamic_index_in_dim(stacked, (y + k - x) % 4, 0, keepdims=False)
        total = pick(0)
        for k in (1, 2, 3):
            def target(x, h, c, y, l, k=k):
                return (x, h, c, y + k, l) if (y + k - x) % 4 < 3 else None
            total = total + send(pick(k), target)
        total = total * (1.0 / (NXW * NZ))

    with jax.named_scope("place"):
        total = total.reshape(2, own, 2, own)
        received = send(total[1], lambda x, h, c, y, l: (x, h, 1 - c, y, l))
        straight = jnp.where(
            c == 0,
            jnp.stack([total[0], received], axis=2),
            jnp.stack([received, total[0]], axis=2),
        )
        straight = straight.transpose(1, 0, 2, 3).reshape(2, own, 2 * own)
        by_core = jnp.where(c == 0, total, total[::-1])
        turned = by_core.transpose(2, 3, 0, 1).reshape(2, own, 2 * own)

        def transposed(x, h, c, y, l):
            return (y, l, c, x, h) if (y - x) % 4 in (1, 2) else None

        turned = send(turned, transposed)
        d = (y - x) % 4
        result = jnp.where(d == 3, turned, jnp.where(d == 2, straight + turned, straight))
    return result[0], result[1]


def solution(mesh):
    placed = (P(None, None, "span", "snap"),)
    return jax.shard_map(
        body,
        mesh=mesh,
        in_specs=placed,
        out_specs=(P("snap", "span"), P("snap", "span")),
        check_vma=False,
    )
```

time: 314 us -> 161 us (0.51)
  the two profiles are of different devices: /device:TPU:0 before, /device:TPU:25 now
where the time goes in v1:
time: 161 us; the launch traced here: 159 us
  waiting for transfers between devices  94.2 us (59%)
  starting transfers between devices  40.5 us (25%)
  matrix products  10.6 us (7%)
  other arithmetic  8.63 us (5%)
  local copies, waits for them, and re-layouts  3.9 us (2%)
    ppermute x29, waiting for transfers between devices, send(): return lax.ppermute(value, AXES, pairs)  94.2 us
    ppermute x29, starting transfers between devices, send(): return lax.ppermute(value, AXES, pairs)  40.5 us
    dot_general x6, matrix products, inner(): lax.dot_general(left, right, (((0,), (0,)), ((), ())), preferred_element_...  7.24 us
    concatenate x1, other arithmetic, body(): left = jnp.concatenate([left_s, left_t], axis=0)  7.18 us
    dot_general x2, matrix products, reflect(): lax.dot_general(piece, swap, (((2,), (1,)), ((), ())), preferred_element_...  3.37 us
  transfers between devices with their start and end apart: 29, of which 17 were waited for; matrix products, arithmetic and copies ran while one was open for 12% of the time, Pallas kernels for 0%

profile of v1, /device:TPU:25, one launch (start us, length us, event | category | flops | bytes accessed | tf_op | source)
XLA Modules:
  0.0 159.0 jit_solution(9362500602373988794)
XLA Ops:
  3.9 2.1 %convolution_multiply_fusion = bf16[3,3,128,192]{2,3,1,0:T(8,128)(2,1)} fusion(bf16[3,12,192,128]{3,2,1,0:T(8,128)(2,1)} %param.2, s32[]{:T(128)S(6)} %select_n.272, bf16[3]{0:T(256)(128)(2,1)} %constant.575.clone, bf16[192,192]{1,0:T(8,128)(2,1)S(1)} %rev.7), kind=kOutput, calls=%fused_computation.62 | convolution fusion | flops 85155840 | bytes 958980 | tf_op jit(solution)/shard_map/rows/dot_general | solution.py:52
  5.9 4.7 %collective-permute-start.4 = (bf16[1728,128]{1,0:T(8,128)(2,1)}, bf16[1728,128]{1,0:T(8,128)(2,1)S(1)}, u32[]{:S(2)}, u32[]{:S(2)}) collective-permute-start(bf16[1728,128]{1,0:T(8,128)(2,1)} %bitcast.8), channel_id=1, source_target_pairs={{0,23},{1,22},{2,21},{3,20},{4,19},{5,18},{6,17},{7,16},{8,31},{9,... | collective-permute-start | bytes 1327112 | tf_op jit(solution)/shard_map/rows/ppermute | solution.py:27
  12.7 2.5 %collective-permute-start.10 = (bf16[1728,128]{1,0:T(8,128)(2,1)S(1)}, bf16[1728,128]{1,0:T(8,128)(2,1)}, u32[]{:S(2)}, u32[]{:S(2)}) collective-permute-start(bf16[1728,128]{1,0:T(8,128)(2,1)S(1)} %bitcast.125), channel_id=1, source_target_pairs={{0,96},{1,97},{2,98},{3,99},{4,100},{5,101},{6,102},{7,103},{8,104... | collective-permute-start | bytes 1327112 | tf_op jit(solution)/shard_map/next/ppermute | solution.py:27
  17.1 14.9 %collective-permute-done.4 = bf16[1728,128]{1,0:T(8,128)(2,1)S(1)} collective-permute-done((bf16[1728,128]{1,0:T(8,128)(2,1)}, bf16[1728,128]{1,0:T(8,128)(2,1)S(1)}, u32[]{:S(2)}, u32[]{:S(2)}) %collective-permute-start.4) | collective-permute-done | bytes 442400 | tf_op jit(solution)/shard_map/rows/ppermute | solution.py:27
  32.1 5.4 %collective-permute-done = bf16[1728,128]{1,0:T(8,128)(2,1)S(1)} collective-permute-done((bf16[1728,128]{1,0:T(8,128)(2,1)}, bf16[1728,128]{1,0:T(8,128)(2,1)S(1)}, u32[]{:S(2)}, u32[]{:S(2)}) %collective-permute-start) | collective-permute-done | bytes 442400 | tf_op jit(solution)/shard_map/rows/ppermute | solution.py:27
  41.6 1.7 %collective-permute-start.11 = (bf16[1728,128]{1,0:T(8,128)(2,1)S(1)}, bf16[1728,128]{1,0:T(8,128)(2,1)S(1)}, u32[]{:S(2)}, u32[]{:S(2)}) collective-permute-start(bf16[1728,128]{1,0:T(8,128)(2,1)S(1)} %collective-permute-done.3), channel_id=1, source_target_pairs={{0,96},{1,97},{2,98},{3,99},{4,100},{5,101},{6,102},{7,103},{8,104... | collective-permute-start | bytes 1327112 | tf_op jit(solution)/shard_map/next/ppermute | solution.py:27
  44.4 7.2 %pad_maximum_fusion = bf16[3456,512]{1,0:T(8,128)(2,1)S(1)} fusion(bf16[1728,512]{1,0:T(8,128)(2,1)S(1)} %constant_dynamic-update-slice_fusion, bf16[1728,128]{1,0:T(8,128)(2,1)S(1)} %collective-permute-done.2, bf16[1728,128]{1,0:T(8,128)(2,1)S(1)} %collective-permute-done.1, bf16[1728,128]{1,0:T(8,128)(2,1)S(1)} %collective-permute-done, ...), kind=kLoop, calls=%fused_computation | loop fusion | flops 17694720 | bytes 7077888 | tf_op jit(solution)/shard_map/cores/concatenate | solution.py:68
  52.7 2.4 %fusion.16 = f32[512,256]{1,0:T(8,128)S(1)} fusion(bf16[3456,512]{1,0:T(8,128)(2,1)S(1)} %pad_maximum_fusion, bf16[1728,128]{1,0:T(8,128)(2,1)} %collective-permute-done.10, bf16[1728,128]{1,0:T(8,128)(2,1)S(1)} %collective-permute-done.11), kind=kOutput, calls=%fused_computation.21 | convolution fusion | flops 913047552 | bytes 4947968 | tf_op jit(solution)/shard_map/blocks/dot_general | solution.py:31
  55.1 7.1 %collective-permute-done.12 = bf16[1728,128]{1,0:T(8,128)(2,1)S(1)} collective-permute-done((bf16[1728,128]{1,0:T(8,128)(2,1)S(1)}, bf16[1728,128]{1,0:T(8,128)(2,1)S(1)}, u32[]{:S(2)}, u32[]{:S(2)}) %collective-permute-start.12) | collective-permute-done | bytes 442400 | tf_op jit(solution)/shard_map/next/ppermute | solution.py:27
  62.2 9.5 %collective-permute-done.13 = bf16[1728,128]{1,0:T(8,128)(2,1)S(1)} collective-permute-done((bf16[1728,128]{1,0:T(8,128)(2,1)S(1)}, bf16[1728,128]{1,0:T(8,128)(2,1)S(1)}, u32[]{:S(2)}, u32[]{:S(2)}) %collective-permute-start.13) | collective-permute-done | bytes 442400 | tf_op jit(solution)/shard_map/next/ppermute | solution.py:27
  73.1 2.0 %collective-permute-start.15 = (f32[2,128,256]{2,1,0:T(8,128)S(1)}, f32[2,128,256]{2,1,0:T(8,128)S(1)}, u32[]{:S(2)}, u32[]{:S(2)}) collective-permute-start(f32[2,128,256]{2,1,0:T(8,128)S(1)} %get-tuple-element.13), channel_id=1, source_target_pairs={{0,16},{1,17},{2,18},{3,19},{4,20},{5,21},{6,22},{7,23},{8,24},{9,... | collective-permute-start | bytes 786440 | tf_op jit(solution)/shard_map/blocks/ppermute | solution.py:27
  80.0 8.1 %collective-permute-done.18 = bf16[2,864,128]{2,1,0:T(8,128)(2,1)S(1)} collective-permute-done((bf16[2,864,128]{2,1,0:T(8,128)(2,1)S(1)}, bf16[2,864,128]{2,1,0:T(8,128)(2,1)S(1)}, u32[]{:S(2)}, u32[]{:S(2)}) %collective-permute-start.18) | collective-permute-done | bytes 442400 | tf_op jit(solution)/shard_map/opposite/ppermute | solution.py:27
  88.2 2.4 %collective-permute-start.9 = (f32[2,128,256]{2,1,0:T(8,128)S(1)}, f32[2,128,256]{2,1,0:T(8,128)S(1)}, u32[]{:S(2)}, u32[]{:S(2)}) collective-permute-start(f32[2,128,256]{2,1,0:T(8,128)S(1)} %get-tuple-element.11), channel_id=1, source_target_pairs={{0,17},{1,0},{2,19},{3,2},{4,21},{5,4},{6,23},{7,6},{8,25},{9,8},{... | collective-permute-start | bytes 786440 | tf_op jit(solution)/shard_map/blocks/ppermute | solution.py:27
  90.6 7.1 %collective-permute-done.20 = bf16[2,864,128]{2,1,0:T(8,128)(2,1)S(1)} collective-permute-done((bf16[2,864,128]{2,1,0:T(8,128)(2,1)S(1)}, bf16[2,864,128]{2,1,0:T(8,128)(2,1)S(1)}, u32[]{:S(2)}, u32[]{:S(2)}) %collective-permute-start.20) | collective-permute-done | bytes 442400 | tf_op jit(solution)/shard_map/opposite/ppermute | solution.py:27
  97.7 2.2 %collective-permute-start.8 = (f32[2,128,256]{2,1,0:T(8,128)S(1)}, f32[2,128,256]{2,1,0:T(8,128)S(1)}, u32[]{:S(2)}, u32[]{:S(2)}) collective-permute-start(f32[2,128,256]{2,1,0:T(8,128)S(1)} %get-tuple-element.10), channel_id=1, source_target_pairs={{0,16},{1,17},{2,18},{3,19},{4,20},{5,21},{6,22},{7,23},{8,24},{9,... | collective-permute-start | bytes 786440 | tf_op jit(solution)/shard_map/blocks/ppermute | solution.py:27
  102.3 1.9 %collective-permute-start.23 = (f32[2,128,256]{2,1,0:T(8,128)S(1)}, f32[2,128,256]{2,1,0:T(8,128)S(1)}, u32[]{:S(2)}, u32[]{:S(2)}) collective-permute-start(f32[2,128,256]{2,1,0:T(8,128)S(1)} %get-tuple-element.17), channel_id=1, source_target_pairs={{0,17},{1,0},{2,19},{3,2},{4,21},{5,4},{6,23},{7,6},{8,25},{9,8},{... | collective-permute-start | bytes 786440 | tf_op jit(solution)/shard_map/blocks/ppermute | solution.py:27
  105.0 8.4 %collective-permute-done.7 = f32[2,128,256]{2,1,0:T(8,128)S(1)} collective-permute-done((f32[2,128,256]{2,1,0:T(8,128)S(1)}, f32[2,128,256]{2,1,0:T(8,128)S(1)}, u32[]{:S(2)}, u32[]{:S(2)}) %collective-permute-start.7) | collective-permute-done | bytes 262176 | tf_op jit(solution)/shard_map/blocks/ppermute | solution.py:27
  115.2 7.7 %collective-permute-done.21 = f32[2,128,256]{2,1,0:T(8,128)S(1)} collective-permute-done((f32[2,128,256]{2,1,0:T(8,128)S(1)}, f32[2,128,256]{2,1,0:T(8,128)S(1)}, u32[]{:S(2)}, u32[]{:S(2)}) %collective-permute-start.21) | collective-permute-done | bytes 262176 | tf_op jit(solution)/shard_map/blocks/ppermute | solution.py:27
  124.5 3.8 %collective-permute-start.25 = (f32[2,128,256]{2,1,0:T(8,128)S(1)}, f32[2,128,256]{2,1,0:T(8,128)S(1)}, u32[]{:S(2)}, u32[]{:S(2)}) collective-permute-start(f32[2,128,256]{2,1,0:T(8,128)S(1)} %get-tuple-element.8), channel_id=1, source_target_pairs={{0,4},{1,5},{4,0},{5,1},{6,2},{7,3},{8,12},{9,13},{12,8},{13,9},{1... | collective-permute-start | bytes 786440 | tf_op jit(solution)/shard_map/over_y/ppermute | solution.py:27
  128.3 2.5 %collective-permute-start.24 = (f32[2,128,256]{2,1,0:T(8,128)S(1)}, f32[2,128,256]{2,1,0:T(8,128)S(1)}, u32[]{:S(2)}, u32[]{:S(2)}) collective-permute-start(f32[2,128,256]{2,1,0:T(8,128)S(1)} %get-tuple-element.6), channel_id=1, source_target_pairs={{0,2},{1,3},{2,4},{3,5},{6,0},{7,1},{8,10},{9,11},{10,12},{11,13},... | collective-permute-start | bytes 786440 | tf_op jit(solution)/shard_map/over_y/ppermute | solution.py:27
  130.9 3.5 %collective-permute-done.25 = f32[2,128,256]{2,1,0:T(8,128)S(1)} collective-permute-done((f32[2,128,256]{2,1,0:T(8,128)S(1)}, f32[2,128,256]{2,1,0:T(8,128)S(1)}, u32[]{:S(2)}, u32[]{:S(2)}) %collective-permute-start.25) | collective-permute-done | bytes 262176 | tf_op jit(solution)/shard_map/over_y/ppermute | solution.py:27
  134.4 2.3 %collective-permute-done.24 = f32[2,128,256]{2,1,0:T(8,128)S(1)} collective-permute-done((f32[2,128,256]{2,1,0:T(8,128)S(1)}, f32[2,128,256]{2,1,0:T(8,128)S(1)}, u32[]{:S(2)}, u32[]{:S(2)}) %collective-permute-start.24) | collective-permute-done | bytes 262176 | tf_op jit(solution)/shard_map/over_y/ppermute | solution.py:27
  138.5 2.3 %collective-permute-start.28 = (f32[128,2,128]{0,2,1:T(8,128)S(1)}, f32[128,2,128]{0,2,1:T(8,128)S(1)}, u32[]{:S(2)}, u32[]{:S(2)}) collective-permute-start(f32[128,2,128]{0,2,1:T(8,128)S(1)} %bitcast.146), channel_id=1, source_target_pairs={{0,8},{1,9},{2,10},{3,11},{4,12},{5,13},{6,14},{7,15},{8,0},{9,1},... | collective-permute-start | bytes 393224 | tf_op jit(solution)/shard_map/place/ppermute | solution.py:27
  141.8 15.6 %collective-permute-done.27 = f32[2,128,256]{1,2,0:T(8,128)S(1)} collective-permute-done((f32[2,128,256]{1,2,0:T(8,128)S(1)}, f32[2,128,256]{1,2,0:T(8,128)S(1)}, u32[]{:S(2)}, u32[]{:S(2)}) %collective-permute-start.27) | collective-permute-done | bytes 262176 | tf_op jit(solution)/shard_map/place/ppermute | solution.py:27
  (84 shorter events, 30.6 us)
Async XLA Ops:
  2.5 13.2 %collective-permute-start.3 = (bf16[1728,128]{1,0:T(8,128)(2,1)S(1)}, bf16[1728,128]{1,0:T(8,128)(2,1)S(1)}, u32[]{:S(2)}, u32[]{:S(2)}) collective-permute-start(bf16[1728,128]{1,0:T(8,128)(2,1)S(1)} %bitcast.143), channel_id=1, source_target_pairs={{0,7},{1,6},{2,5},{3,4},{4,3},{5,2},{6,1},{7,0},{8,15},{9,14},{10,... | collective-permute-start | bytes 1327112 | tf_op jit(solution)/shard_map/rows/ppermute | solution.py:27
  5.9 26.1 %collective-permute-start.4 = (bf16[1728,128]{1,0:T(8,128)(2,1)}, bf16[1728,128]{1,0:T(8,128)(2,1)S(1)}, u32[]{:S(2)}, u32[]{:S(2)}) collective-permute-start(bf16[1728,128]{1,0:T(8,128)(2,1)} %bitcast.8), channel_id=1, source_target_pairs={{0,23},{1,22},{2,21},{3,20},{4,19},{5,18},{6,17},{7,16},{8,31},{9,... | collective-permute-start | bytes 1327112 | tf_op jit(solution)/shard_map/rows/ppermute | solution.py:27
  11.5 30.1 %collective-permute-start.1 = (bf16[1728,128]{1,0:T(8,128)(2,1)S(1)}, bf16[1728,128]{1,0:T(8,128)(2,1)S(1)}, u32[]{:S(2)}, u32[]{:S(2)}) collective-permute-start(bf16[1728,128]{1,0:T(8,128)(2,1)S(1)} %bitcast.124), channel_id=1, source_target_pairs={{0,8},{1,9},{2,10},{3,11},{4,12},{5,13},{6,14},{7,15},{8,0},{9,1},... | collective-permute-start | bytes 1327112 | tf_op jit(solution)/shard_map/cores/ppermute | solution.py:27
  12.7 38.8 %collective-permute-start.10 = (bf16[1728,128]{1,0:T(8,128)(2,1)S(1)}, bf16[1728,128]{1,0:T(8,128)(2,1)}, u32[]{:S(2)}, u32[]{:S(2)}) collective-permute-start(bf16[1728,128]{1,0:T(8,128)(2,1)S(1)} %bitcast.125), channel_id=1, source_target_pairs={{0,96},{1,97},{2,98},{3,99},{4,100},{5,101},{6,102},{7,103},{8,104... | collective-permute-start | bytes 1327112 | tf_op jit(solution)/shard_map/next/ppermute | solution.py:27
  15.2 22.3 %collective-permute-start = (bf16[1728,128]{1,0:T(8,128)(2,1)}, bf16[1728,128]{1,0:T(8,128)(2,1)S(1)}, u32[]{:S(2)}, u32[]{:S(2)}) collective-permute-start(bf16[1728,128]{1,0:T(8,128)(2,1)} %bitcast.1), channel_id=1, source_target_pairs={{0,16},{1,17},{2,18},{3,19},{4,20},{5,21},{6,22},{7,23},{8,24},{9,... | collective-permute-start | bytes 1327112 | tf_op jit(solution)/shard_map/rows/ppermute | solution.py:27
  15.8 60.5 %collective-permute-start.17 = (bf16[2,864,128]{2,1,0:T(8,128)(2,1)S(1)}, bf16[2,864,128]{2,1,0:T(8,128)(2,1)S(1)}, u32[]{:S(2)}, u32[]{:S(2)}) collective-permute-start(bf16[2,864,128]{2,1,0:T(8,128)(2,1)S(1)} %pad_maximum_fusion.4), channel_id=1, source_target_pairs={{0,32},{1,33},{2,34},{3,35},{4,36},{5,37},{6,38},{7,39},{8,40},{9,... | collective-permute-start | bytes 1327112 | tf_op jit(solution)/shard_map/opposite/ppermute | solution.py:27
  40.5 38.2 %collective-permute-start.19 = (bf16[2,864,128]{2,1,0:T(8,128)(2,1)S(1)}, bf16[2,864,128]{2,1,0:T(8,128)(2,1)S(1)}, u32[]{:S(2)}, u32[]{:S(2)}) collective-permute-start(bf16[2,864,128]{2,1,0:T(8,128)(2,1)S(1)} %pad_maximum_fusion.5), channel_id=1, source_target_pairs={{0,32},{1,33},{2,34},{3,35},{4,36},{5,37},{6,38},{7,39},{8,40},{9,... | collective-permute-start | bytes 1327112 | tf_op jit(solution)/shard_map/opposite/ppermute | solution.py:27
  41.6 11.1 %collective-permute-start.11 = (bf16[1728,128]{1,0:T(8,128)(2,1)S(1)}, bf16[1728,128]{1,0:T(8,128)(2,1)S(1)}, u32[]{:S(2)}, u32[]{:S(2)}) collective-permute-start(bf16[1728,128]{1,0:T(8,128)(2,1)S(1)} %collective-permute-done.3), channel_id=1, source_target_pairs={{0,96},{1,97},{2,98},{3,99},{4,100},{5,101},{6,102},{7,103},{8,104... | collective-permute-start | bytes 1327112 | tf_op jit(solution)/shard_map/next/ppermute | solution.py:27
  43.3 18.9 %collective-permute-start.12 = (bf16[1728,128]{1,0:T(8,128)(2,1)S(1)}, bf16[1728,128]{1,0:T(8,128)(2,1)S(1)}, u32[]{:S(2)}, u32[]{:S(2)}) collective-permute-start(bf16[1728,128]{1,0:T(8,128)(2,1)S(1)} %collective-permute-done), channel_id=1, source_target_pairs={{0,96},{1,97},{2,98},{3,99},{4,100},{5,101},{6,102},{7,103},{8,104... | collective-permute-start | bytes 1327112 | tf_op jit(solution)/shard_map/next/ppermute | solution.py:27
  51.6 20.1 %collective-permute-start.13 = (bf16[1728,128]{1,0:T(8,128)(2,1)S(1)}, bf16[1728,128]{1,0:T(8,128)(2,1)S(1)}, u32[]{:S(2)}, u32[]{:S(2)}) collective-permute-start(bf16[1728,128]{1,0:T(8,128)(2,1)S(1)} %collective-permute-done.4), channel_id=1, source_target_pairs={{0,96},{1,97},{2,98},{3,99},{4,100},{5,101},{6,102},{7,103},{8,104... | collective-permute-start | bytes 1327112 | tf_op jit(solution)/shard_map/next/ppermute | solution.py:27
  73.0 28.2 %collective-permute-start.16 = (f32[2,128,256]{2,1,0:T(8,128)S(1)}, f32[2,128,256]{2,1,0:T(8,128)S(1)}, u32[]{:S(2)}, u32[]{:S(2)}) collective-permute-start(f32[2,128,256]{2,1,0:T(8,128)S(1)} %get-tuple-element.14), channel_id=1, source_target_pairs={{0,17},{1,0},{2,19},{3,2},{4,21},{5,4},{6,23},{7,6},{8,25},{9,8},{... | collective-permute-start | bytes 786440 | tf_op jit(solution)/shard_map/blocks/ppermute | solution.py:27
  73.1 29.2 %collective-permute-start.15 = (f32[2,128,256]{2,1,0:T(8,128)S(1)}, f32[2,128,256]{2,1,0:T(8,128)S(1)}, u32[]{:S(2)}, u32[]{:S(2)}) collective-permute-start(f32[2,128,256]{2,1,0:T(8,128)S(1)} %get-tuple-element.13), channel_id=1, source_target_pairs={{0,16},{1,17},{2,18},{3,19},{4,20},{5,21},{6,22},{7,23},{8,24},{9,... | collective-permute-start | bytes 786440 | tf_op jit(solution)/shard_map/blocks/ppermute | solution.py:27
  75.1 29.1 %collective-permute-start.14 = (f32[2,128,256]{2,1,0:T(8,128)S(1)}, f32[2,128,256]{2,1,0:T(8,128)S(1)}, u32[]{:S(2)}, u32[]{:S(2)}) collective-permute-start(f32[2,128,256]{2,1,0:T(8,128)S(1)} %get-tuple-element.12), channel_id=1, source_target_pairs={{0,1},{1,16},{2,3},{3,18},{4,5},{5,20},{6,7},{7,22},{8,9},{9,24},{... | collective-permute-start | bytes 786440 | tf_op jit(solution)/shard_map/blocks/ppermute | solution.py:27
  76.3 11.9 %collective-permute-start.18 = (bf16[2,864,128]{2,1,0:T(8,128)(2,1)S(1)}, bf16[2,864,128]{2,1,0:T(8,128)(2,1)S(1)}, u32[]{:S(2)}, u32[]{:S(2)}) collective-permute-start(bf16[2,864,128]{2,1,0:T(8,128)(2,1)S(1)} %collective-permute-done.17), channel_id=1, source_target_pairs={{0,32},{1,33},{2,34},{3,35},{4,36},{5,37},{6,38},{7,39},{8,40},{9,... | collective-permute-start | bytes 1327112 | tf_op jit(solution)/shard_map/opposite/ppermute | solution.py:27
  78.7 19.0 %collective-permute-start.20 = (bf16[2,864,128]{2,1,0:T(8,128)(2,1)S(1)}, bf16[2,864,128]{2,1,0:T(8,128)(2,1)S(1)}, u32[]{:S(2)}, u32[]{:S(2)}) collective-permute-start(bf16[2,864,128]{2,1,0:T(8,128)(2,1)S(1)} %collective-permute-done.19), channel_id=1, source_target_pairs={{0,32},{1,33},{2,34},{3,35},{4,36},{5,37},{6,38},{7,39},{8,40},{9,... | collective-permute-start | bytes 1327112 | tf_op jit(solution)/shard_map/opposite/ppermute | solution.py:27
  88.2 16.1 %collective-permute-start.9 = (f32[2,128,256]{2,1,0:T(8,128)S(1)}, f32[2,128,256]{2,1,0:T(8,128)S(1)}, u32[]{:S(2)}, u32[]{:S(2)}) collective-permute-start(f32[2,128,256]{2,1,0:T(8,128)S(1)} %get-tuple-element.11), channel_id=1, source_target_pairs={{0,17},{1,0},{2,19},{3,2},{4,21},{5,4},{6,23},{7,6},{8,25},{9,8},{... | collective-permute-start | bytes 786440 | tf_op jit(solution)/shard_map/blocks/ppermute | solution.py:27
  101.2 12.2 %collective-permute-start.7 = (f32[2,128,256]{2,1,0:T(8,128)S(1)}, f32[2,128,256]{2,1,0:T(8,128)S(1)}, u32[]{:S(2)}, u32[]{:S(2)}) collective-permute-start(f32[2,128,256]{2,1,0:T(8,128)S(1)} %get-tuple-element.9), channel_id=1, source_target_pairs={{0,1},{1,16},{2,3},{3,18},{4,5},{5,20},{6,7},{7,22},{8,9},{9,24},{... | collective-permute-start | bytes 786440 | tf_op jit(solution)/shard_map/blocks/ppermute | solution.py:27
  102.3 11.2 %collective-permute-start.23 = (f32[2,128,256]{2,1,0:T(8,128)S(1)}, f32[2,128,256]{2,1,0:T(8,128)S(1)}, u32[]{:S(2)}, u32[]{:S(2)}) collective-permute-start(f32[2,128,256]{2,1,0:T(8,128)S(1)} %get-tuple-element.17), channel_id=1, source_target_pairs={{0,17},{1,0},{2,19},{3,2},{4,21},{5,4},{6,23},{7,6},{8,25},{9,8},{... | collective-permute-start | bytes 786440 | tf_op jit(solution)/shard_map/blocks/ppermute | solution.py:27
  104.2 10.9 %collective-permute-start.22 = (f32[2,128,256]{2,1,0:T(8,128)S(1)}, f32[2,128,256]{2,1,0:T(8,128)S(1)}, u32[]{:S(2)}, u32[]{:S(2)}) collective-permute-start(f32[2,128,256]{2,1,0:T(8,128)S(1)} %get-tuple-element.16), channel_id=1, source_target_pairs={{0,16},{1,17},{2,18},{3,19},{4,20},{5,21},{6,22},{7,23},{8,24},{9,... | collective-permute-start | bytes 786440 | tf_op jit(solution)/shard_map/blocks/ppermute | solution.py:27
  104.2 18.6 %collective-permute-start.21 = (f32[2,128,256]{2,1,0:T(8,128)S(1)}, f32[2,128,256]{2,1,0:T(8,128)S(1)}, u32[]{:S(2)}, u32[]{:S(2)}) collective-permute-start(f32[2,128,256]{2,1,0:T(8,128)S(1)} %get-tuple-element.15), channel_id=1, source_target_pairs={{0,1},{1,16},{2,3},{3,18},{4,5},{5,20},{6,7},{7,22},{8,9},{9,24},{... | collective-permute-start | bytes 786440 | tf_op jit(solution)/shard_map/blocks/ppermute | solution.py:27
  123.2 7.6 %collective-permute-start.26 = (f32[2,128,256]{2,1,0:T(8,128)S(1)}, f32[2,128,256]{2,1,0:T(8,128)S(1)}, u32[]{:S(2)}, u32[]{:S(2)}) collective-permute-start(f32[2,128,256]{2,1,0:T(8,128)S(1)} %get-tuple-element.7), channel_id=1, source_target_pairs={{2,0},{3,1},{4,2},{5,3},{6,4},{7,5},{10,8},{11,9},{12,10},{13,11},... | collective-permute-start | bytes 786440 | tf_op jit(solution)/shard_map/over_y/ppermute | solution.py:27
  124.5 9.9 %collective-permute-start.25 = (f32[2,128,256]{2,1,0:T(8,128)S(1)}, f32[2,128,256]{2,1,0:T(8,128)S(1)}, u32[]{:S(2)}, u32[]{:S(2)}) collective-permute-start(f32[2,128,256]{2,1,0:T(8,128)S(1)} %get-tuple-element.8), channel_id=1, source_target_pairs={{0,4},{1,5},{4,0},{5,1},{6,2},{7,3},{8,12},{9,13},{12,8},{13,9},{1... | collective-permute-start | bytes 786440 | tf_op jit(solution)/shard_map/over_y/ppermute | solution.py:27
  128.3 8.4 %collective-permute-start.24 = (f32[2,128,256]{2,1,0:T(8,128)S(1)}, f32[2,128,256]{2,1,0:T(8,128)S(1)}, u32[]{:S(2)}, u32[]{:S(2)}) collective-permute-start(f32[2,128,256]{2,1,0:T(8,128)S(1)} %get-tuple-element.6), channel_id=1, source_target_pairs={{0,2},{1,3},{2,4},{3,5},{6,0},{7,1},{8,10},{9,11},{10,12},{11,13},... | collective-permute-start | bytes 786440 | tf_op jit(solution)/shard_map/over_y/ppermute | solution.py:27
  137.0 20.4 %collective-permute-start.27 = (f32[2,128,256]{1,2,0:T(8,128)S(1)}, f32[2,128,256]{1,2,0:T(8,128)S(1)}, u32[]{:S(2)}, u32[]{:S(2)}) collective-permute-start(f32[2,128,256]{1,2,0:T(8,128)S(1)} %bitcast.144), channel_id=1, source_target_pairs={{2,32},{3,48},{4,64},{5,80},{10,40},{11,56},{12,72},{13,88},{18,33... | collective-permute-start | bytes 786440 | tf_op jit(solution)/shard_map/place/ppermute | solution.py:27
  (6 other events, 28.5 us)

commit v2 on v1

v2 whole, which is shorter than its diff:
```python
import functools

import jax
import jax.numpy as jnp
from jax import lax
from jax.sharding import PartitionSpec as P

NZ = 1536
NXW = 12
AXES = ("snap", "span")
SWAPS = ((), (2, 3), (0,))
COORDS = [
    (x, h, c, y, l)
    for x in range(4) for h in range(2) for c in range(2) for y in range(4) for l in range(2)
]


def place(x, h, c, y, l):
    return (x % 4 * 4 + h * 2 + c) * 8 + y % 4 * 2 + l


def after(value, *others):
    return lax.optimization_barrier((value, *others))[0]


def send(value, target, behind=()):
    if behind:
        value = after(value, *behind)
    pairs = []
    for at in COORDS:
        to = target(*at)
        if to is not None:
            pairs.append((place(*at), place(*to)))
    return lax.ppermute(value, AXES, pairs)


def inner(left, right):
    return lax.dot_general(
        left, right, (((0,), (0,)), ((), ())), preferred_element_type=jnp.float32
    )


def up(x, h, c, y, l):
    return x + 1, h, c, y, l


def down(x, h, c, y, l):
    return x - 1, h, c, y, l


def across(x, h, c, y, l):
    return x, h, 1 - c, y, l


def body(snapshots):
    comps, rows, depth, own = snapshots.shape
    quarter = rows // 4
    count = comps * quarter * depth
    snap, span = lax.axis_index("snap"), lax.axis_index("span")
    x, h, c = snap // 4, snap // 2 % 2, snap % 2
    y, l = span // 2, span % 2
    m = y // 2

    def part(side, group):
        return lax.dynamic_slice_in_dim(snapshots, (side * 2 + group) * quarter, quarter, axis=1)

    sign = jnp.array([1.0, 1.0, -1.0], jnp.bfloat16).reshape(3, 1, 1, 1)
    swap = jnp.flip(jnp.eye(depth, dtype=jnp.bfloat16), 0)

    def reflect(piece):
        turned = lax.dot_general(piece, swap, (((2,), (1,)), ((), ())), preferred_element_type=jnp.bfloat16)
        return jnp.swapaxes(turned, 2, 3) * sign

    flat = lambda piece: piece.reshape(count, own)
    def above(x, h, c, y, l):
        return (x + 1, h, c, y, l) if (y - x - 1) % 4 < 2 else None

    with jax.named_scope("rows"):
        s1 = send(flat(part(m, 1 - h)), lambda x, h, c, y, l: (x, 1 - h, c, y, l))
        t0 = send(flat(reflect(part(1 - m, h))), lambda x, h, c, y, l: (x, h, c, 3 - y, 1 - l))
        crossing = flat(reflect(part(1 - m, 1 - h)))
        t1 = send(crossing, lambda x, h, c, y, l: (x, 1 - h, c, 3 - y, 1 - l))
        s0 = flat(part(m, h))
    with jax.named_scope("first"):
        n0 = send(s0, down)
        p0 = send(s0, above)
        n1 = send(t0, down, [n0])
        p1 = send(t0, above, [p0])
    with jax.named_scope("second"):
        pair = jnp.concatenate([s1, t1])
        n2 = send(pair, down)
        p2 = send(pair, above)
        c0, c1, c2 = send(s0, across, [s1, t1, n1, p1]), send(t0, across, [s1, t1, n1, p1]), send(pair, across)
        s0, t0, n1, p0, p1 = after((s0, t0, n1, p0, p1), c0, c1, c2)
        q0, q1 = send(p0, across), send(p1, across)
        p0, p1 = after((p0, p1), q0, q1)

    def columns(name, *cores):
        with jax.named_scope(name):
            result = jnp.zeros((2 * count, 4 * own), jnp.bfloat16)
            for i, (s, t, st) in enumerate(cores):
                result = lax.dynamic_update_slice(result, s, (0, 2 * i * own))
                result = lax.dynamic_update_slice(result, t, (count, 2 * i * own))
                result = lax.dynamic_update_slice(result, st[:count], (0, (2 * i + 1) * own))
                result = lax.dynamic_update_slice(result, st[count:], (count, (2 * i + 1) * own))
            return result

    left = columns("left", (s0, t0, pair), (c0, c1, c2))

    def products(lhs, s, t):
        right = jnp.concatenate(
            [jnp.concatenate([s, t], axis=1), jnp.concatenate([t, s], axis=1)], axis=0
        )
        return inner(lhs, right).reshape(2, 2, own, 2 * own)

    d = (y - x) % 4

    def over_z(first, second, behind, active=lambda *at: True, swaps=()):
        swap = functools.reduce(jnp.logical_or, [d == at for at in swaps], jnp.zeros((), bool))

        def block(k):
            to = (2 * h + l + k) % 4
            row, column = jnp.where(swap, to % 2, to // 2), jnp.where(swap, to // 2, to % 2)
            pick = lambda both: lax.dynamic_index_in_dim(both, row ^ h, 1, keepdims=False)
            return jnp.where(column ^ h == 0, pick(first), pick(second))

        total = block(0)
        for k in (1, 2, 3):
            def target(x, h, c, y, l, k=k):
                to = (2 * h + l + k) % 4
                return (x, to // 2, c, y, to % 2) if active(x, h, c, y, l) else None
            total = total + send(block(k), target, behind)
        return total

    with jax.named_scope("same"):
        same = over_z(products(left, s0, t0), products(left, pair[:count], pair[count:]), [q0, q1])
    with jax.named_scope("beside"):
        n2 = after(n2, same)
        beside = over_z(products(left, n0, n1), products(left, n2[:count], n2[count:]), [], swaps=SWAPS[1])
    with jax.named_scope("around"):
        p2 = after(p2, same)
        q2 = send(p2, across)
        previous = columns("previous", (p0, p1, p2), (q0, q1, q2))
        around = over_z(
            products(previous, n0, n1),
            products(previous, n2[:count], n2[count:]),
            [],
            lambda x, h, c, y, l: (y - x) % 4 < 2,
            SWAPS[2],
        )

    rounds = (
        ((1, True), (2, False), (1, False), (0, False)),
        ((1, False), (2, True), (0, False), (1, True)),
        ((2, False), (0, False), (1, True), (1, False)),
        ((2, True), (1, True), None, None),
    )
    with jax.named_scope("over_y"):
        got = []
        for plan in rounds:
            def target(x, h, c, y, l, plan=plan):
                if plan[(y - x) % 4] is None:
                    return None
                block, turn = plan[(y - x) % 4]
                row, column = ((x, x), (x, x + 1), (x - 1, x + 1))[block]
                if turn:
                    row, column = column, row
                if turn != ((y - x) % 4 in SWAPS[block]):
                    h, l = l, h
                return row % 4, h, c, column, l
            value = beside
            for at, step in enumerate(plan):
                if step is not None and step[0] != 1:
                    value = jnp.where(d == at, (same, beside, around)[step[0]], value)
            got.append(send(value, target))
        own_block = jnp.where(d == 0, same, beside)
        odd = got[0] + got[2]
        straight = odd + jnp.where(d == 2, 0, own_block + got[1])
        turned = jnp.where(d == 2, 0, odd) + got[1] + got[3]

    with jax.named_scope("place"):
        scale = 1.0 / (NXW * NZ)
        total = (straight * scale).reshape(2, own, 2, own)
        turned = (turned * scale).reshape(2, own, 2, own)
        received = send(total[1], across)
        straight = jnp.where(
            c == 0,
            jnp.stack([total[0], received], axis=2),
            jnp.stack([received, total[0]], axis=2),
        )
        straight = straight.transpose(1, 0, 2, 3).reshape(2, own, 2 * own)
        by_core = jnp.where(c == 0, turned, turned[::-1])
        turned = by_core.transpose(2, 3, 0, 1).reshape(2, own, 2 * own)
        result = jnp.where(d == 3, turned, jnp.where(d == 2, straight + turned, straight))
    return result[0], result[1]


def solution(mesh):
    placed = (P(None, None, "span", "snap"),)
    return jax.shard_map(
        body,
        mesh=mesh,
        in_specs=placed,
        out_specs=(P("snap", "span"), P("snap", "span")),
        check_vma=False,
    )
```

time: 161 us -> 129 us (0.80); the launches traced: 159 us -> 129 us
  waiting for transfers between devices: 94.2 us -> 51.4 us
  starting transfers between devices: 40.5 us -> 51.5 us
  local copies, waits for them, and re-layouts: 3.9 us -> 10.4 us
  other arithmetic: 8.63 us -> 4.84 us
    ppermute x29, waiting for transfers between devices: 94.2 us -> 51.4 us  [send(): return lax.ppermute(value, AXES, pairs)]
    ppermute x29, starting transfers between devices: 40.5 us -> 51.5 us  [send(): return lax.ppermute(value, AXES, pairs)]
    concatenate x2 -> x0, other arithmetic: 7.3 us -> none  [the longest x1 7.18 us: body(): left = jnp.concatenate([left_s, left_t], axis=0)]
    select_n x0 -> x5, other arithmetic: none -> 4.08 us  [the longest x2 2.19 us: body(): value = jnp.where(d == at, (same, beside, around)[step[0]], value)]
    dynamic_update_slice x0 -> x16, local copies, waits for them, and re-layouts: none -> 4.03 us  [the longest x4 1.74 us: columns(): result = lax.dynamic_update_slice(result, s, (0, 2 * i * own))]
  transfers between devices with their start and end apart: 29 -> 29, of which waited for: 17 -> 11; matrix products, arithmetic and copies ran while one was open for 12% -> 14% of each run, Pallas kernels for 0% -> 0%
where the time goes in v2:
time: 129 us
  starting transfers between devices  51.5 us (40%)
  waiting for transfers between devices  51.4 us (40%)
  local copies, waits for them, and re-layouts  10.4 us (8%)
  matrix products  9.55 us (7%)
  other arithmetic  4.84 us (4%)
    ppermute x29, starting transfers between devices, send(): return lax.ppermute(value, AXES, pairs)  51.5 us
    ppermute x29, waiting for transfers between devices, send(): return lax.ppermute(value, AXES, pairs)  51.4 us
    dot_general x6, matrix products, inner(): lax.dot_general(left, right, (((0,), (0,)), ((), ())), preferred_element_...  6.94 us
    dot_general x2, matrix products, reflect(): lax.dot_general(piece, swap, (((2,), (1,)), ((), ())), preferred_element_...  2.61 us
  transfers between devices with their start and end apart: 29, of which 11 were waited for; matrix products, arithmetic and copies ran while one was open for 14% of the time, Pallas kernels for 0%

profile of v2, /device:TPU:25, one launch (start us, length us, event | category | flops | bytes accessed | tf_op | source)
XLA Modules:
  0.0 128.8 jit_solution(13982805162452296298)
XLA Ops:
  1.9 2.5 %collective-permute-start.1 = (bf16[1728,128]{1,0:T(8,128)(2,1)S(1)}, bf16[1728,128]{1,0:T(8,128)(2,1)S(1)}, u32[]{:S(2)}, u32[]{:S(2)}) collective-permute-start(bf16[1728,128]{1,0:T(8,128)(2,1)S(1)} %bitcast.189), channel_id=1, source_target_pairs={{0,96},{1,97},{2,98},{3,99},{4,100},{5,101},{6,102},{7,103},{8,104... | collective-permute-start | bytes 1327112 | tf_op jit(solution)/shard_map/first/ppermute | solution.py:34
  5.6 1.3 %convolution_multiply_fusion.1 = bf16[3,3,128,192]{2,3,1,0:T(8,128)(2,1)S(1)} fusion(bf16[3,12,192,128]{3,2,1,0:T(8,128)(2,1)} %param.2, s32[]{:T(128)S(6)} %select_n.464, bf16[3]{0:T(256)(128)(2,1)} %constant.301.clone, bf16[192,192]{1,0:T(8,128)(2,1)S(1)} %rev.7), kind=kOutput, calls=%fused_computation.19 | convolution fusion | flops 85155840 | bytes 958980 | tf_op jit(solution)/shard_map/rows/dot_general | solution.py:71
  6.9 2.0 %collective-permute-start = (bf16[1728,128]{1,0:T(8,128)(2,1)S(1)}, bf16[1728,128]{1,0:T(8,128)(2,1)S(1)}, u32[]{:S(2)}, u32[]{:S(2)}) collective-permute-start(bf16[1728,128]{1,0:T(8,128)(2,1)S(1)} %bitcast.195), channel_id=1, source_target_pairs={{0,7},{1,6},{2,5},{3,4},{4,3},{5,2},{6,1},{7,0},{8,15},{9,14},{10,... | collective-permute-start | bytes 1327112 | tf_op jit(solution)/shard_map/rows/ppermute | solution.py:34
  8.9 3.3 %collective-permute-start.5 = (bf16[1728,128]{1,0:T(8,128)(2,1)S(1)}, bf16[1728,128]{1,0:T(8,128)(2,1)S(1)}, u32[]{:S(2)}, u32[]{:S(2)}) collective-permute-start(bf16[1728,128]{1,0:T(8,128)(2,1)S(1)} %bitcast.194), channel_id=1, source_target_pairs={{0,16},{1,17},{2,18},{3,19},{4,20},{5,21},{6,22},{7,23},{8,24},{9,... | collective-permute-start | bytes 1327112 | tf_op jit(solution)/shard_map/rows/ppermute | solution.py:34
  14.4 5.5 %collective-permute-done = bf16[1728,128]{1,0:T(8,128)(2,1)S(1)} collective-permute-done((bf16[1728,128]{1,0:T(8,128)(2,1)S(1)}, bf16[1728,128]{1,0:T(8,128)(2,1)S(1)}, u32[]{:S(2)}, u32[]{:S(2)}) %collective-permute-start) | collective-permute-done | bytes 442400 | tf_op jit(solution)/shard_map/rows/ppermute | solution.py:34
  19.9 1.6 %collective-permute-start.2 = (bf16[1728,128]{1,0:T(8,128)(2,1)S(1)}, bf16[1728,128]{1,0:T(8,128)(2,1)S(1)}, u32[]{:S(2)}, u32[]{:S(2)}) collective-permute-start(bf16[1728,128]{1,0:T(8,128)(2,1)S(1)} %collective-permute-done), channel_id=1, source_target_pairs={{0,96},{1,97},{2,98},{3,99},{4,100},{5,101},{6,102},{7,103},{8,104... | collective-permute-start | bytes 1327112 | tf_op jit(solution)/shard_map/first/ppermute | solution.py:34
  22.2 15.8 %collective-permute-done.5 = bf16[1728,128]{1,0:T(8,128)(2,1)S(1)} collective-permute-done((bf16[1728,128]{1,0:T(8,128)(2,1)S(1)}, bf16[1728,128]{1,0:T(8,128)(2,1)S(1)}, u32[]{:S(2)}, u32[]{:S(2)}) %collective-permute-start.5) | collective-permute-done | bytes 442400 | tf_op jit(solution)/shard_map/rows/ppermute | solution.py:34
  39.6 2.3 %collective-permute-start.9 = (bf16[3456,128]{1,0:T(8,128)(2,1)}, bf16[3456,128]{1,0:T(8,128)(2,1)S(1)}, u32[]{:S(2)}, u32[]{:S(2)}) collective-permute-start(bf16[3456,128]{1,0:T(8,128)(2,1)} %constant_dynamic-update-slice_fusion.5), channel_id=1, source_target_pairs={{0,8},{1,9},{2,10},{3,11},{4,12},{5,13},{6,14},{7,15},{8,0},{9,1},... | collective-permute-start | bytes 2654216 | tf_op jit(solution)/shard_map/second/ppermute | solution.py:34
  43.2 3.1 %collective-permute-start.17 = (bf16[3456,128]{1,0:T(8,128)(2,1)}, bf16[3456,128]{1,0:T(8,128)(2,1)S(1)}, u32[]{:S(2)}, u32[]{:S(2)}) collective-permute-start(bf16[3456,128]{1,0:T(8,128)(2,1)} %constant_dynamic-update-slice_fusion.5), channel_id=1, source_target_pairs={{0,96},{1,97},{2,98},{3,99},{4,100},{5,101},{6,102},{7,103},{8,104... | collective-permute-start | bytes 2654216 | tf_op jit(solution)/shard_map/second/ppermute | solution.py:34
  53.8 1.9 %collective-permute-start.13 = (f32[2,128,256]{2,1,0:T(8,128)S(1)}, f32[2,128,256]{2,1,0:T(8,128)S(1)}, u32[]{:S(2)}, u32[]{:S(2)}) collective-permute-start(f32[2,128,256]{2,1,0:T(8,128)S(1)} %get-tuple-element.27), channel_id=1, source_target_pairs={{0,16},{1,17},{2,18},{3,19},{4,20},{5,21},{6,22},{7,23},{8,24},{9,... | collective-permute-start | bytes 786440 | tf_op jit(solution)/shard_map/same/ppermute | solution.py:34
  57.3 4.2 %collective-permute-done.14 = f32[2,128,256]{2,1,0:T(8,128)S(1)} collective-permute-done((f32[2,128,256]{2,1,0:T(8,128)S(1)}, f32[2,128,256]{2,1,0:T(8,128)S(1)}, u32[]{:S(2)}, u32[]{:S(2)}) %collective-permute-start.14) | collective-permute-done | bytes 262176 | tf_op jit(solution)/shard_map/same/ppermute | solution.py:34
  62.8 6.4 %collective-permute-done.12 = f32[2,128,256]{2,1,0:T(8,128)S(1)} collective-permute-done((f32[2,128,256]{2,1,0:T(8,128)S(1)}, f32[2,128,256]{2,1,0:T(8,128)S(1)}, u32[]{:S(2)}, u32[]{:S(2)}) %collective-permute-start.12) | collective-permute-done | bytes 262176 | tf_op jit(solution)/shard_map/same/ppermute | solution.py:34
  73.2 1.8 %collective-permute-start.16 = (bf16[3456,128]{1,0:T(8,128)(2,1)S(1)}, bf16[3456,128]{1,0:T(8,128)(2,1)S(1)}, u32[]{:S(2)}, u32[]{:S(2)}) collective-permute-start(bf16[3456,128]{1,0:T(8,128)(2,1)S(1)} %collective-permute-done.15), channel_id=1, source_target_pairs={{0,8},{1,9},{2,10},{3,11},{4,12},{5,13},{6,14},{7,15},{8,0},{9,1},... | collective-permute-start | bytes 2654216 | tf_op jit(solution)/shard_map/around/ppermute | solution.py:34
  75.5 1.6 %collective-permute-done.16 = bf16[3456,128]{1,0:T(8,128)(2,1)S(1)} collective-permute-done((bf16[3456,128]{1,0:T(8,128)(2,1)S(1)}, bf16[3456,128]{1,0:T(8,128)(2,1)S(1)}, u32[]{:S(2)}, u32[]{:S(2)}) %collective-permute-start.16) | collective-permute-done | bytes 884768 | tf_op jit(solution)/shard_map/around/ppermute | solution.py:34
  80.5 1.3 %collective-permute-start.20 = (f32[2,128,256]{2,1,0:T(8,128)}, f32[2,128,256]{2,1,0:T(8,128)}, u32[]{:S(2)}, u32[]{:S(2)}) collective-permute-start(f32[2,128,256]{2,1,0:T(8,128)} %get-tuple-element.42), channel_id=1, source_target_pairs={{0,17},{1,0},{2,19},{3,2},{8,25},{9,8},{10,27},{11,10},{16,1},{17,... | collective-permute-start | bytes 786440 | tf_op jit(solution)/shard_map/around/ppermute | solution.py:34
  81.9 1.4 %collective-permute-start.19 = (f32[2,128,256]{2,1,0:T(8,128)}, f32[2,128,256]{2,1,0:T(8,128)}, u32[]{:S(2)}, u32[]{:S(2)}) collective-permute-start(f32[2,128,256]{2,1,0:T(8,128)} %get-tuple-element.41), channel_id=1, source_target_pairs={{0,16},{1,17},{2,18},{3,19},{8,24},{9,25},{10,26},{11,27},{16,0},{... | collective-permute-start | bytes 786440 | tf_op jit(solution)/shard_map/around/ppermute | solution.py:34
  83.2 1.4 %collective-permute-start.18 = (f32[2,128,256]{2,1,0:T(8,128)}, f32[2,128,256]{2,1,0:T(8,128)}, u32[]{:S(2)}, u32[]{:S(2)}) collective-permute-start(f32[2,128,256]{2,1,0:T(8,128)} %get-tuple-element.40), channel_id=1, source_target_pairs={{0,1},{1,16},{2,3},{3,18},{8,9},{9,24},{10,11},{11,26},{16,17},{17... | collective-permute-start | bytes 786440 | tf_op jit(solution)/shard_map/around/ppermute | solution.py:34
  84.6 2.6 %collective-permute-done.21 = f32[2,128,256]{2,1,0:T(8,128)S(1)} collective-permute-done((f32[2,128,256]{2,1,0:T(8,128)S(1)}, f32[2,128,256]{2,1,0:T(8,128)S(1)}, u32[]{:S(2)}, u32[]{:S(2)}) %collective-permute-start.21) | collective-permute-done | bytes 262176 | tf_op jit(solution)/shard_map/beside/ppermute | solution.py:34
  87.2 2.1 %broadcast_select_fusion.1 = (f32[2,128,256]{2,1,0:T(8,128)}, f32[2,128,256]{2,1,0:T(8,128)}, f32[2,128,256]{2,1,0:T(8,128)S(1)}, f32[2,128,256]{2,1,0:T(8,128)S(1)}) fusion(f32[2,128,256]{2,1,0:T(8,128)S(1)} %fusion.44, pred[]{:T(512)S(6)} %eq.115, pred[]{:T(512)S(6)} %eq.116, f32[2,128,256]{2,1,0:T(8,128)S(1)} %collective-permute-done.23, ...), kind=kLoop, calls=%fused_computation.77 | loop fusion | flops 655360 | bytes 3932172 | tf_op jit(solution)/shard_map/over_y/jit(_where)/select_n | solution.py:174
  90.2 16.8 %collective-permute-start.24 = (f32[2,128,256]{2,1,0:T(8,128)S(1)}, f32[2,128,256]{2,1,0:T(8,128)S(1)}, u32[]{:S(2)}, u32[]{:S(2)}) collective-permute-start(f32[2,128,256]{2,1,0:T(8,128)S(1)} %get-tuple-element.53), channel_id=1, source_target_pairs={{0,32},{1,48},{2,98},{3,99},{4,2},{5,18},{6,0},{7,1},{8,40},{9,56}... | collective-permute-start | bytes 786440 | tf_op jit(solution)/shard_map/over_y/ppermute | solution.py:34
  107.1 2.2 %collective-permute-start.25 = (f32[2,128,256]{2,1,0:T(8,128)}, f32[2,128,256]{2,1,0:T(8,128)S(1)}, u32[]{:S(2)}, u32[]{:S(2)}) collective-permute-start(f32[2,128,256]{2,1,0:T(8,128)} %get-tuple-element.34), channel_id=1, source_target_pairs={{0,98},{1,114},{2,0},{3,1},{4,32},{5,33},{6,2},{7,18},{8,106},{9,1... | collective-permute-start | bytes 786440 | tf_op jit(solution)/shard_map/over_y/ppermute | solution.py:34
  110.5 7.5 %collective-permute-done.24 = f32[2,128,256]{2,1,0:T(8,128)S(1)} collective-permute-done((f32[2,128,256]{2,1,0:T(8,128)S(1)}, f32[2,128,256]{2,1,0:T(8,128)S(1)}, u32[]{:S(2)}, u32[]{:S(2)}) %collective-permute-start.24) | collective-permute-done | bytes 262176 | tf_op jit(solution)/shard_map/over_y/ppermute | solution.py:34
  118.0 5.5 %collective-permute-done.27 = f32[2,128,256]{2,1,0:T(8,128)S(1)} collective-permute-done((f32[2,128,256]{2,1,0:T(8,128)}, f32[2,128,256]{2,1,0:T(8,128)S(1)}, u32[]{:S(2)}, u32[]{:S(2)}) %collective-permute-start.27) | collective-permute-done | bytes 262176 | tf_op jit(solution)/shard_map/over_y/ppermute | solution.py:34
  124.6 1.9 %collective-permute-start.28 = (f32[128,2,128]{2,0,1:T(8,128)S(1)}, f32[128,2,128]{2,0,1:T(8,128)S(1)}, u32[]{:S(2)}, u32[]{:S(2)}) collective-permute-start(f32[128,2,128]{2,0,1:T(8,128)S(1)} %copy.30), channel_id=1, source_target_pairs={{0,8},{1,9},{2,10},{3,11},{4,12},{5,13},{6,14},{7,15},{8,0},{9,1},... | collective-permute-start | bytes 393224 | tf_op jit(solution)/shard_map/place/ppermute | solution.py:34
  (92 shorter events, 31.7 us)
Async XLA Ops:
  1.9 18.0 %collective-permute-start.1 = (bf16[1728,128]{1,0:T(8,128)(2,1)S(1)}, bf16[1728,128]{1,0:T(8,128)(2,1)S(1)}, u32[]{:S(2)}, u32[]{:S(2)}) collective-permute-start(bf16[1728,128]{1,0:T(8,128)(2,1)S(1)} %bitcast.189), channel_id=1, source_target_pairs={{0,96},{1,97},{2,98},{3,99},{4,100},{5,101},{6,102},{7,103},{8,104... | collective-permute-start | bytes 1327112 | tf_op jit(solution)/shard_map/first/ppermute | solution.py:34
  4.5 17.1 %collective-permute-start.3 = (bf16[1728,128]{1,0:T(8,128)(2,1)S(1)}, bf16[1728,128]{1,0:T(8,128)(2,1)S(1)}, u32[]{:S(2)}, u32[]{:S(2)}) collective-permute-start(bf16[1728,128]{1,0:T(8,128)(2,1)S(1)} %bitcast.190), channel_id=1, source_target_pairs={{2,34},{3,35},{4,36},{5,37},{10,42},{11,43},{12,44},{13,45},{18,50... | collective-permute-start | bytes 1327112 | tf_op jit(solution)/shard_map/first/ppermute | solution.py:34
  6.9 12.9 %collective-permute-start = (bf16[1728,128]{1,0:T(8,128)(2,1)S(1)}, bf16[1728,128]{1,0:T(8,128)(2,1)S(1)}, u32[]{:S(2)}, u32[]{:S(2)}) collective-permute-start(bf16[1728,128]{1,0:T(8,128)(2,1)S(1)} %bitcast.195), channel_id=1, source_target_pairs={{0,7},{1,6},{2,5},{3,4},{4,3},{5,2},{6,1},{7,0},{8,15},{9,14},{10,... | collective-permute-start | bytes 1327112 | tf_op jit(solution)/shard_map/rows/ppermute | solution.py:34
  8.9 29.1 %collective-permute-start.5 = (bf16[1728,128]{1,0:T(8,128)(2,1)S(1)}, bf16[1728,128]{1,0:T(8,128)(2,1)S(1)}, u32[]{:S(2)}, u32[]{:S(2)}) collective-permute-start(bf16[1728,128]{1,0:T(8,128)(2,1)S(1)} %bitcast.194), channel_id=1, source_target_pairs={{0,16},{1,17},{2,18},{3,19},{4,20},{5,21},{6,22},{7,23},{8,24},{9,... | collective-permute-start | bytes 1327112 | tf_op jit(solution)/shard_map/rows/ppermute | solution.py:34
  13.5 25.3 %collective-permute-start.6 = (bf16[1728,128]{1,0:T(8,128)(2,1)S(1)}, bf16[1728,128]{1,0:T(8,128)(2,1)S(1)}, u32[]{:S(2)}, u32[]{:S(2)}) collective-permute-start(bf16[1728,128]{1,0:T(8,128)(2,1)S(1)} %bitcast.196), channel_id=1, source_target_pairs={{0,23},{1,22},{2,21},{3,20},{4,19},{5,18},{6,17},{7,16},{8,31},{9,... | collective-permute-start | bytes 1327112 | tf_op jit(solution)/shard_map/rows/ppermute | solution.py:34
  19.9 22.0 %collective-permute-start.2 = (bf16[1728,128]{1,0:T(8,128)(2,1)S(1)}, bf16[1728,128]{1,0:T(8,128)(2,1)S(1)}, u32[]{:S(2)}, u32[]{:S(2)}) collective-permute-start(bf16[1728,128]{1,0:T(8,128)(2,1)S(1)} %collective-permute-done), channel_id=1, source_target_pairs={{0,96},{1,97},{2,98},{3,99},{4,100},{5,101},{6,102},{7,103},{8,104... | collective-permute-start | bytes 1327112 | tf_op jit(solution)/shard_map/first/ppermute | solution.py:34
  21.5 20.4 %collective-permute-start.4 = (bf16[1728,128]{1,0:T(8,128)(2,1)S(1)}, bf16[1728,128]{1,0:T(8,128)(2,1)S(1)}, u32[]{:S(2)}, u32[]{:S(2)}) collective-permute-start(bf16[1728,128]{1,0:T(8,128)(2,1)S(1)} %collective-permute-done), channel_id=1, source_target_pairs={{2,34},{3,35},{4,36},{5,37},{10,42},{11,43},{12,44},{13,45},{18,50... | collective-permute-start | bytes 1327112 | tf_op jit(solution)/shard_map/first/ppermute | solution.py:34
  39.6 7.4 %collective-permute-start.9 = (bf16[3456,128]{1,0:T(8,128)(2,1)}, bf16[3456,128]{1,0:T(8,128)(2,1)S(1)}, u32[]{:S(2)}, u32[]{:S(2)}) collective-permute-start(bf16[3456,128]{1,0:T(8,128)(2,1)} %constant_dynamic-update-slice_fusion.5), channel_id=1, source_target_pairs={{0,8},{1,9},{2,10},{3,11},{4,12},{5,13},{6,14},{7,15},{8,0},{9,1},... | collective-permute-start | bytes 2654216 | tf_op jit(solution)/shard_map/second/ppermute | solution.py:34
  42.7 4.3 %collective-permute-start.7 = (bf16[1728,128]{1,0:T(8,128)(2,1)S(1)}, bf16[1728,128]{1,0:T(8,128)(2,1)}, u32[]{:S(2)}, u32[]{:S(2)}) collective-permute-start(bf16[1728,128]{1,0:T(8,128)(2,1)S(1)} %bitcast.191), channel_id=1, source_target_pairs={{0,8},{1,9},{2,10},{3,11},{4,12},{5,13},{6,14},{7,15},{8,0},{9,1},... | collective-permute-start | bytes 1327112 | tf_op jit(solution)/shard_map/second/ppermute | solution.py:34
  42.7 4.3 %collective-permute-start.8 = (bf16[1728,128]{1,0:T(8,128)(2,1)S(1)}, bf16[1728,128]{1,0:T(8,128)(2,1)}, u32[]{:S(2)}, u32[]{:S(2)}) collective-permute-start(bf16[1728,128]{1,0:T(8,128)(2,1)S(1)} %collective-permute-done), channel_id=1, source_target_pairs={{0,8},{1,9},{2,10},{3,11},{4,12},{5,13},{6,14},{7,15},{8,0},{9,1},... | collective-permute-start | bytes 1327112 | tf_op jit(solution)/shard_map/second/ppermute | solution.py:34
  43.2 26.1 %collective-permute-start.17 = (bf16[3456,128]{1,0:T(8,128)(2,1)}, bf16[3456,128]{1,0:T(8,128)(2,1)S(1)}, u32[]{:S(2)}, u32[]{:S(2)}) collective-permute-start(bf16[3456,128]{1,0:T(8,128)(2,1)} %constant_dynamic-update-slice_fusion.5), channel_id=1, source_target_pairs={{0,96},{1,97},{2,98},{3,99},{4,100},{5,101},{6,102},{7,103},{8,104... | collective-permute-start | bytes 2654216 | tf_op jit(solution)/shard_map/second/ppermute | solution.py:34
  46.3 26.9 %collective-permute-start.15 = (bf16[3456,128]{1,0:T(8,128)(2,1)}, bf16[3456,128]{1,0:T(8,128)(2,1)S(1)}, u32[]{:S(2)}, u32[]{:S(2)}) collective-permute-start(bf16[3456,128]{1,0:T(8,128)(2,1)} %constant_dynamic-update-slice_fusion.5), channel_id=1, source_target_pairs={{2,34},{3,35},{4,36},{5,37},{10,42},{11,43},{12,44},{13,45},{18,50... | collective-permute-start | bytes 2654216 | tf_op jit(solution)/shard_map/second/ppermute | solution.py:34
  53.8 7.6 %collective-permute-start.14 = (f32[2,128,256]{2,1,0:T(8,128)S(1)}, f32[2,128,256]{2,1,0:T(8,128)S(1)}, u32[]{:S(2)}, u32[]{:S(2)}) collective-permute-start(f32[2,128,256]{2,1,0:T(8,128)S(1)} %get-tuple-element.28), channel_id=1, source_target_pairs={{0,17},{1,0},{2,19},{3,2},{4,21},{5,4},{6,23},{7,6},{8,25},{9,8},{... | collective-permute-start | bytes 786440 | tf_op jit(solution)/shard_map/same/ppermute | solution.py:34
  53.8 8.9 %collective-permute-start.13 = (f32[2,128,256]{2,1,0:T(8,128)S(1)}, f32[2,128,256]{2,1,0:T(8,128)S(1)}, u32[]{:S(2)}, u32[]{:S(2)}) collective-permute-start(f32[2,128,256]{2,1,0:T(8,128)S(1)} %get-tuple-element.27), channel_id=1, source_target_pairs={{0,16},{1,17},{2,18},{3,19},{4,20},{5,21},{6,22},{7,23},{8,24},{9,... | collective-permute-start | bytes 786440 | tf_op jit(solution)/shard_map/same/ppermute | solution.py:34
  55.8 13.4 %collective-permute-start.12 = (f32[2,128,256]{2,1,0:T(8,128)S(1)}, f32[2,128,256]{2,1,0:T(8,128)S(1)}, u32[]{:S(2)}, u32[]{:S(2)}) collective-permute-start(f32[2,128,256]{2,1,0:T(8,128)S(1)} %get-tuple-element.26), channel_id=1, source_target_pairs={{0,1},{1,16},{2,3},{3,18},{4,5},{5,20},{6,7},{7,22},{8,9},{9,24},{... | collective-permute-start | bytes 786440 | tf_op jit(solution)/shard_map/same/ppermute | solution.py:34
  71.3 11.9 %collective-permute-start.23 = (f32[2,128,256]{2,1,0:T(8,128)S(1)}, f32[2,128,256]{2,1,0:T(8,128)S(1)}, u32[]{:S(2)}, u32[]{:S(2)}) collective-permute-start(f32[2,128,256]{2,1,0:T(8,128)S(1)} %get-tuple-element.45), channel_id=1, source_target_pairs={{0,17},{1,0},{2,19},{3,2},{4,21},{5,4},{6,23},{7,6},{8,25},{9,8},{... | collective-permute-start | bytes 786440 | tf_op jit(solution)/shard_map/beside/ppermute | solution.py:34
  71.6 13.0 %collective-permute-start.22 = (f32[2,128,256]{2,1,0:T(8,128)}, f32[2,128,256]{2,1,0:T(8,128)S(1)}, u32[]{:S(2)}, u32[]{:S(2)}) collective-permute-start(f32[2,128,256]{2,1,0:T(8,128)} %get-tuple-element.44), channel_id=1, source_target_pairs={{0,16},{1,17},{2,18},{3,19},{4,20},{5,21},{6,22},{7,23},{8,24},{9,... | collective-permute-start | bytes 786440 | tf_op jit(solution)/shard_map/beside/ppermute | solution.py:34
  72.7 14.5 %collective-permute-start.21 = (f32[2,128,256]{2,1,0:T(8,128)S(1)}, f32[2,128,256]{2,1,0:T(8,128)S(1)}, u32[]{:S(2)}, u32[]{:S(2)}) collective-permute-start(f32[2,128,256]{2,1,0:T(8,128)S(1)} %get-tuple-element.43), channel_id=1, source_target_pairs={{0,1},{1,16},{2,3},{3,18},{4,5},{5,20},{6,7},{7,22},{8,9},{9,24},{... | collective-permute-start | bytes 786440 | tf_op jit(solution)/shard_map/beside/ppermute | solution.py:34
  80.5 6.6 %collective-permute-start.20 = (f32[2,128,256]{2,1,0:T(8,128)}, f32[2,128,256]{2,1,0:T(8,128)}, u32[]{:S(2)}, u32[]{:S(2)}) collective-permute-start(f32[2,128,256]{2,1,0:T(8,128)} %get-tuple-element.42), channel_id=1, source_target_pairs={{0,17},{1,0},{2,19},{3,2},{8,25},{9,8},{10,27},{11,10},{16,1},{17,... | collective-permute-start | bytes 786440 | tf_op jit(solution)/shard_map/around/ppermute | solution.py:34
  81.9 5.3 %collective-permute-start.19 = (f32[2,128,256]{2,1,0:T(8,128)}, f32[2,128,256]{2,1,0:T(8,128)}, u32[]{:S(2)}, u32[]{:S(2)}) collective-permute-start(f32[2,128,256]{2,1,0:T(8,128)} %get-tuple-element.41), channel_id=1, source_target_pairs={{0,16},{1,17},{2,18},{3,19},{8,24},{9,25},{10,26},{11,27},{16,0},{... | collective-permute-start | bytes 786440 | tf_op jit(solution)/shard_map/around/ppermute | solution.py:34
  89.4 21.1 %collective-permute-start.26 = (f32[2,128,256]{2,1,0:T(8,128)S(1)}, f32[2,128,256]{2,1,0:T(8,128)S(1)}, u32[]{:S(2)}, u32[]{:S(2)}) collective-permute-start(f32[2,128,256]{2,1,0:T(8,128)S(1)} %get-tuple-element.54), channel_id=1, source_target_pairs={{0,2},{1,3},{2,38},{3,54},{4,0},{5,1},{6,32},{7,33},{8,10},{9,11},... | collective-permute-start | bytes 786440 | tf_op jit(solution)/shard_map/over_y/ppermute | solution.py:34
  90.2 27.8 %collective-permute-start.24 = (f32[2,128,256]{2,1,0:T(8,128)S(1)}, f32[2,128,256]{2,1,0:T(8,128)S(1)}, u32[]{:S(2)}, u32[]{:S(2)}) collective-permute-start(f32[2,128,256]{2,1,0:T(8,128)S(1)} %get-tuple-element.53), channel_id=1, source_target_pairs={{0,32},{1,48},{2,98},{3,99},{4,2},{5,18},{6,0},{7,1},{8,40},{9,56}... | collective-permute-start | bytes 786440 | tf_op jit(solution)/shard_map/over_y/ppermute | solution.py:34
  107.1 10.9 %collective-permute-start.25 = (f32[2,128,256]{2,1,0:T(8,128)}, f32[2,128,256]{2,1,0:T(8,128)S(1)}, u32[]{:S(2)}, u32[]{:S(2)}) collective-permute-start(f32[2,128,256]{2,1,0:T(8,128)} %get-tuple-element.34), channel_id=1, source_target_pairs={{0,98},{1,114},{2,0},{3,1},{4,32},{5,33},{6,2},{7,18},{8,106},{9,1... | collective-permute-start | bytes 786440 | tf_op jit(solution)/shard_map/over_y/ppermute | solution.py:34
  109.2 14.3 %collective-permute-start.27 = (f32[2,128,256]{2,1,0:T(8,128)}, f32[2,128,256]{2,1,0:T(8,128)S(1)}, u32[]{:S(2)}, u32[]{:S(2)}) collective-permute-start(f32[2,128,256]{2,1,0:T(8,128)} %get-tuple-element.35), channel_id=1, source_target_pairs={{0,38},{1,39},{2,32},{3,48},{8,46},{9,47},{10,40},{11,56},{16,54},... | collective-permute-start | bytes 786440 | tf_op jit(solution)/shard_map/over_y/ppermute | solution.py:34
  (9 other events, 26.0 us)

commit v3 on v2

--- a/solution.py
+++ b/solution.py
@@ -76,11 +76,11 @@
         return (x + 1, h, c, y, l) if (y - x - 1) % 4 < 2 else None
 
     with jax.named_scope("rows"):
-        s1 = send(flat(part(m, 1 - h)), lambda x, h, c, y, l: (x, 1 - h, c, y, l))
-        t0 = send(flat(reflect(part(1 - m, h))), lambda x, h, c, y, l: (x, h, c, 3 - y, 1 - l))
-        crossing = flat(reflect(part(1 - m, 1 - h)))
-        t1 = send(crossing, lambda x, h, c, y, l: (x, 1 - h, c, 3 - y, 1 - l))
-        s0 = flat(part(m, h))
+        s1 = flat(send(part(m, 1 - h), lambda x, h, c, y, l: (x, 1 - h, c, y, l)))
+        t0 = send(part(1 - m, h), lambda x, h, c, y, l: (x, h, c, 3 - y, 1 - l))
+        t1 = send(part(1 - m, 1 - h), lambda x, h, c, y, l: (x, 1 - h, c, 3 - y, 1 - l))
+        t0, t1 = flat(reflect(t0)), flat(reflect(t1))
+        s0 = after(flat(part(m, h)), swap)
     with jax.named_scope("first"):
         n0 = send(s0, down)
         p0 = send(s0, above)
@@ -125,7 +125,7 @@
             return jnp.where(column ^ h == 0, pick(first), pick(second))
 
         total = block(0)
-        for k in (1, 2, 3):
+        for k in (3, 1, 2):
             def target(x, h, c, y, l, k=k):
                 to = (2 * h + l + k) % 4
                 return (x, to // 2, c, y, to % 2) if active(x, h, c, y, l) else None
@@ -133,7 +133,7 @@
         return total
 
     with jax.named_scope("same"):
-        same = over_z(products(left, s0, t0), products(left, pair[:count], pair[count:]), [q0, q1])
+        same = over_z(products(left, s0, t0), products(left, pair[:count], pair[count:]), [])
     with jax.named_scope("beside"):
         n2 = after(n2, same)
         beside = over_z(products(left, n0, n1), products(left, n2[:count], n2[count:]), [], swaps=SWAPS[1])
@@ -148,6 +148,8 @@
             lambda x, h, c, y, l: (y - x) % 4 < 2,
             SWAPS[2],
         )
+
+    same, beside = lax.optimization_barrier((same, beside))
 
     rounds = (
         ((1, True), (2, False), (1, False), (0, False)),

time: 129 us -> 118 us (0.915)
  waiting for transfers between devices: 51.4 us -> 44 us
  matrix products: 9.55 us -> 7.51 us
    ppermute x29, waiting for transfers between devices: 51.4 us -> 44 us  [send(): return lax.ppermute(value, AXES, pairs)]
    dot_general x2, matrix products: 2.61 us -> 0.57 us  [reflect(): lax.dot_general(piece, swap, (((2,), (1,)), ((), ())), preferred_element_...]
  transfers between devices with their start and end apart: 29 -> 29, of which waited for: 11 -> 10; matrix products, arithmetic and copies ran while one was open for 14% -> 13% of each run, Pallas kernels for 0% -> 0%
where the time goes in v3:
time: 118 us
  starting transfers between devices  50.5 us (43%)
  waiting for transfers between devices  44 us (37%)
  local copies, waits for them, and re-layouts  10 us (8%)
  matrix products  7.51 us (6%)
  other arithmetic  4.46 us (4%)
  between operations  1.22 us (1%)
    ppermute x29, starting transfers between devices, send(): return lax.ppermute(value, AXES, pairs)  50.5 us
    ppermute x29, waiting for transfers between devices, send(): return lax.ppermute(value, AXES, pairs)  44 us
    dot_general x6, matrix products, inner(): lax.dot_general(left, right, (((0,), (0,)), ((), ())), preferred_element_...  6.94 us
  transfers between devices with their start and end apart: 29, of which 10 were waited for; matrix products, arithmetic and copies ran while one was open for 13% of the time, Pallas kernels for 0%

profile of v3, /device:TPU:25, one launch (start us, length us, event | category | flops | bytes accessed | tf_op | source)
XLA Modules:
  0.0 117.8 jit_solution(4693662463247269282)
XLA Ops:
  0.7 1.6 %constant_dynamic-slice_fusion = (bf16[3,3,192,128]{3,2,1,0:T(8,128)(2,1)S(1)}, bf16[3,3,192,128]{3,2,1,0:T(8,128)(2,1)S(1)}, bf16[3,3,192,128]{3,2,1,0:T(8,128)(2,1)S(1)}, bf16[3,3,192,128]{3,2,1,0:T(8,128)(2,1)S(1)}) fusion(bf16[3,12,192,128]{3,2,1,0:T(8,128)(2,1)} %param.2, s32[]{:T(128)S(6)} %select_n.466, s32[]{:T(128)S(6)} %select_n.464, ...), kind=kLoop, calls=%fused_computation.87 | loop fusion | bytes 3538960 | tf_op jit(solution)/shard_map/rows/dynamic_slice | solution.py:65
  2.3 1.4 %collective-permute-start = (bf16[3,3,192,128]{3,2,1,0:T(8,128)(2,1)S(1)}, bf16[3,3,192,128]{3,2,1,0:T(8,128)(2,1)S(1)}, u32[]{:S(2)}, u32[]{:S(2)}) collective-permute-start(bf16[3,3,192,128]{3,2,1,0:T(8,128)(2,1)S(1)} %get-tuple-element.38), channel_id=1, source_target_pairs={{0,7},{1,6},{2,5},{3,4},{4,3},{5,2},{6,1},{7,0},{8,15},{9,14},{10,... | collective-permute-start | bytes 1327112 | tf_op jit(solution)/shard_map/rows/ppermute | solution.py:34
  4.1 2.5 %collective-permute-start.1 = (bf16[1728,128]{1,0:T(8,128)(2,1)S(1)}, bf16[1728,128]{1,0:T(8,128)(2,1)S(1)}, u32[]{:S(2)}, u32[]{:S(2)}) collective-permute-start(bf16[1728,128]{1,0:T(8,128)(2,1)S(1)} %bitcast.191), channel_id=1, source_target_pairs={{0,96},{1,97},{2,98},{3,99},{4,100},{5,101},{6,102},{7,103},{8,104... | collective-permute-start | bytes 1327112 | tf_op jit(solution)/shard_map/first/ppermute | solution.py:34
  7.4 5.4 %collective-permute-start.6 = (bf16[3,3,192,128]{3,2,1,0:T(8,128)(2,1)S(1)}, bf16[3,3,192,128]{3,2,1,0:T(8,128)(2,1)S(1)}, u32[]{:S(2)}, u32[]{:S(2)}) collective-permute-start(bf16[3,3,192,128]{3,2,1,0:T(8,128)(2,1)S(1)} %get-tuple-element.37), channel_id=1, source_target_pairs={{0,23},{1,22},{2,21},{3,20},{4,19},{5,18},{6,17},{7,16},{8,31},{9,... | collective-permute-start | bytes 1327112 | tf_op jit(solution)/shard_map/rows/ppermute | solution.py:34
  12.7 2.8 %collective-permute-done = bf16[3,3,192,128]{3,2,1,0:T(8,128)(2,1)S(1)} collective-permute-done((bf16[3,3,192,128]{3,2,1,0:T(8,128)(2,1)S(1)}, bf16[3,3,192,128]{3,2,1,0:T(8,128)(2,1)S(1)}, u32[]{:S(2)}, u32[]{:S(2)}) %collective-permute-start) | collective-permute-done | bytes 442400 | tf_op jit(solution)/shard_map/rows/ppermute | solution.py:34
  15.8 2.8 %collective-permute-start.2 = (bf16[1728,128]{1,0:T(8,128)(2,1)S(1)}, bf16[1728,128]{1,0:T(8,128)(2,1)S(1)}, u32[]{:S(2)}, u32[]{:S(2)}) collective-permute-start(bf16[1728,128]{1,0:T(8,128)(2,1)S(1)} %bitcast.199), channel_id=1, source_target_pairs={{0,96},{1,97},{2,98},{3,99},{4,100},{5,101},{6,102},{7,103},{8,104... | collective-permute-start | bytes 1327112 | tf_op jit(solution)/shard_map/first/ppermute | solution.py:34
  19.4 12.5 %collective-permute-done.6 = bf16[3,3,192,128]{3,2,1,0:T(8,128)(2,1)S(1)} collective-permute-done((bf16[3,3,192,128]{3,2,1,0:T(8,128)(2,1)S(1)}, bf16[3,3,192,128]{3,2,1,0:T(8,128)(2,1)S(1)}, u32[]{:S(2)}, u32[]{:S(2)}) %collective-permute-start.6) | collective-permute-done | bytes 442400 | tf_op jit(solution)/shard_map/rows/ppermute | solution.py:34
  32.1 5.2 %collective-permute-done.5 = bf16[3,3,192,128]{3,2,1,0:T(8,128)(2,1)S(1)} collective-permute-done((bf16[3,3,192,128]{3,2,1,0:T(8,128)(2,1)S(1)}, bf16[3,3,192,128]{3,2,1,0:T(8,128)(2,1)S(1)}, u32[]{:S(2)}, u32[]{:S(2)}) %collective-permute-start.5) | collective-permute-done | bytes 442400 | tf_op jit(solution)/shard_map/rows/ppermute | solution.py:34
  39.3 2.5 %collective-permute-start.13 = (bf16[3456,128]{1,0:T(8,128)(2,1)S(1)}, bf16[3456,128]{1,0:T(8,128)(2,1)S(1)}, u32[]{:S(2)}, u32[]{:S(2)}) collective-permute-start(bf16[3456,128]{1,0:T(8,128)(2,1)S(1)} %pad_maximum_fusion), channel_id=1, source_target_pairs={{0,96},{1,97},{2,98},{3,99},{4,100},{5,101},{6,102},{7,103},{8,104... | collective-permute-start | bytes 2654216 | tf_op jit(solution)/shard_map/second/ppermute | solution.py:34
  48.6 2.4 %collective-permute-start.10 = (f32[2,128,256]{2,1,0:T(8,128)S(1)}, f32[2,128,256]{2,1,0:T(8,128)S(1)}, u32[]{:S(2)}, u32[]{:S(2)}) collective-permute-start(f32[2,128,256]{2,1,0:T(8,128)S(1)} %get-tuple-element.47), channel_id=1, source_target_pairs={{0,17},{1,0},{2,19},{3,2},{4,21},{5,4},{6,23},{7,6},{8,25},{9,8},{... | collective-permute-start | bytes 786440 | tf_op jit(solution)/shard_map/same/ppermute | solution.py:34
  52.1 5.2 %collective-permute-done.12 = f32[2,128,256]{2,1,0:T(8,128)S(1)} collective-permute-done((f32[2,128,256]{2,1,0:T(8,128)S(1)}, f32[2,128,256]{2,1,0:T(8,128)S(1)}, u32[]{:S(2)}, u32[]{:S(2)}) %collective-permute-start.12) | collective-permute-done | bytes 262176 | tf_op jit(solution)/shard_map/same/ppermute | solution.py:34
  57.3 2.0 %collective-permute-start.17 = (bf16[1728,128]{1,0:T(8,128)(2,1)S(1)}, bf16[1728,128]{1,0:T(8,128)(2,1)S(1)}, u32[]{:S(2)}, u32[]{:S(2)}) collective-permute-start(bf16[1728,128]{1,0:T(8,128)(2,1)S(1)} %copy-done.1), channel_id=1, source_target_pairs={{0,8},{1,9},{2,10},{3,11},{4,12},{5,13},{6,14},{7,15},{8,0},{9,1},... | collective-permute-start | bytes 1327112 | tf_op jit(solution)/shard_map/second/ppermute | solution.py:34
  59.3 3.9 %collective-permute-done.11 = f32[2,128,256]{2,1,0:T(8,128)S(1)} collective-permute-done((f32[2,128,256]{2,1,0:T(8,128)S(1)}, f32[2,128,256]{2,1,0:T(8,128)S(1)}, u32[]{:S(2)}, u32[]{:S(2)}) %collective-permute-start.11) | collective-permute-done | bytes 262176 | tf_op jit(solution)/shard_map/same/ppermute | solution.py:34
  66.5 1.8 %collective-permute-start.14 = (f32[2,128,256]{2,1,0:T(8,128)S(1)}, f32[2,128,256]{2,1,0:T(8,128)}, u32[]{:S(2)}, u32[]{:S(2)}) collective-permute-start(f32[2,128,256]{2,1,0:T(8,128)S(1)} %get-tuple-element.44), channel_id=1, source_target_pairs={{0,17},{1,0},{2,19},{3,2},{4,21},{5,4},{6,23},{7,6},{8,25},{9,8},{... | collective-permute-start | bytes 786440 | tf_op jit(solution)/shard_map/beside/ppermute | solution.py:34
  68.3 1.6 %collective-permute-start.20 = (bf16[3456,128]{1,0:T(8,128)(2,1)S(1)}, bf16[3456,128]{1,0:T(8,128)(2,1)S(1)}, u32[]{:S(2)}, u32[]{:S(2)}) collective-permute-start(bf16[3456,128]{1,0:T(8,128)(2,1)S(1)} %collective-permute-done.19), channel_id=1, source_target_pairs={{0,8},{1,9},{2,10},{3,11},{4,12},{5,13},{6,14},{7,15},{8,0},{9,1},... | collective-permute-start | bytes 2654216 | tf_op jit(solution)/shard_map/around/ppermute | solution.py:34
  75.4 1.4 %collective-permute-start.23 = (f32[2,128,256]{2,1,0:T(8,128)}, f32[2,128,256]{2,1,0:T(8,128)}, u32[]{:S(2)}, u32[]{:S(2)}) collective-permute-start(f32[2,128,256]{2,1,0:T(8,128)} %get-tuple-element.43), channel_id=1, source_target_pairs={{0,16},{1,17},{2,18},{3,19},{8,24},{9,25},{10,26},{11,27},{16,0},{... | collective-permute-start | bytes 786440 | tf_op jit(solution)/shard_map/around/ppermute | solution.py:34
  76.8 1.4 %collective-permute-start.22 = (f32[2,128,256]{2,1,0:T(8,128)}, f32[2,128,256]{2,1,0:T(8,128)}, u32[]{:S(2)}, u32[]{:S(2)}) collective-permute-start(f32[2,128,256]{2,1,0:T(8,128)} %get-tuple-element.42), channel_id=1, source_target_pairs={{0,1},{1,16},{2,3},{3,18},{8,9},{9,24},{10,11},{11,26},{16,17},{17... | collective-permute-start | bytes 786440 | tf_op jit(solution)/shard_map/around/ppermute | solution.py:34
  78.9 1.4 %collective-permute-start.21 = (f32[2,128,256]{2,1,0:T(8,128)S(1)}, f32[2,128,256]{2,1,0:T(8,128)}, u32[]{:S(2)}, u32[]{:S(2)}) collective-permute-start(f32[2,128,256]{2,1,0:T(8,128)S(1)} %get-tuple-element.41), channel_id=1, source_target_pairs={{0,17},{1,0},{2,19},{3,2},{8,25},{9,8},{10,27},{11,10},{16,1},{17,... | collective-permute-start | bytes 786440 | tf_op jit(solution)/shard_map/around/ppermute | solution.py:34
  83.7 12.6 %collective-permute-start.24 = (f32[2,128,256]{2,1,0:T(8,128)S(1)}, f32[2,128,256]{2,1,0:T(8,128)S(1)}, u32[]{:S(2)}, u32[]{:S(2)}) collective-permute-start(f32[2,128,256]{2,1,0:T(8,128)S(1)} %get-tuple-element.54), channel_id=1, source_target_pairs={{0,32},{1,48},{2,98},{3,99},{4,2},{5,18},{6,0},{7,1},{8,40},{9,56}... | collective-permute-start | bytes 786440 | tf_op jit(solution)/shard_map/over_y/ppermute | solution.py:34
  96.2 2.4 %collective-permute-start.25 = (f32[2,128,256]{2,1,0:T(8,128)S(1)}, f32[2,128,256]{2,1,0:T(8,128)S(1)}, u32[]{:S(2)}, u32[]{:S(2)}) collective-permute-start(f32[2,128,256]{2,1,0:T(8,128)S(1)} %get-tuple-element.34), channel_id=1, source_target_pairs={{0,98},{1,114},{2,0},{3,1},{4,32},{5,33},{6,2},{7,18},{8,106},{9,1... | collective-permute-start | bytes 786440 | tf_op jit(solution)/shard_map/over_y/ppermute | solution.py:34
  98.6 1.3 %collective-permute-start.27 = (f32[2,128,256]{2,1,0:T(8,128)S(1)}, f32[2,128,256]{2,1,0:T(8,128)S(1)}, u32[]{:S(2)}, u32[]{:S(2)}) collective-permute-start(f32[2,128,256]{2,1,0:T(8,128)S(1)} %get-tuple-element.35), channel_id=1, source_target_pairs={{0,38},{1,39},{2,32},{3,48},{8,46},{9,47},{10,40},{11,56},{16,54},... | collective-permute-start | bytes 786440 | tf_op jit(solution)/shard_map/over_y/ppermute | solution.py:34
  99.9 7.8 %collective-permute-done.24 = f32[2,128,256]{2,1,0:T(8,128)S(1)} collective-permute-done((f32[2,128,256]{2,1,0:T(8,128)S(1)}, f32[2,128,256]{2,1,0:T(8,128)S(1)}, u32[]{:S(2)}, u32[]{:S(2)}) %collective-permute-start.24) | collective-permute-done | bytes 262176 | tf_op jit(solution)/shard_map/over_y/ppermute | solution.py:34
  107.7 4.7 %collective-permute-done.27 = f32[2,128,256]{2,1,0:T(8,128)S(1)} collective-permute-done((f32[2,128,256]{2,1,0:T(8,128)S(1)}, f32[2,128,256]{2,1,0:T(8,128)S(1)}, u32[]{:S(2)}, u32[]{:S(2)}) %collective-permute-start.27) | collective-permute-done | bytes 262176 | tf_op jit(solution)/shard_map/over_y/ppermute | solution.py:34
  113.5 1.9 %collective-permute-start.28 = (f32[128,2,128]{2,0,1:T(8,128)S(1)}, f32[128,2,128]{2,0,1:T(8,128)S(1)}, u32[]{:S(2)}, u32[]{:S(2)}) collective-permute-start(f32[128,2,128]{2,0,1:T(8,128)S(1)} %copy.30), channel_id=1, source_target_pairs={{0,8},{1,9},{2,10},{3,11},{4,12},{5,13},{6,14},{7,15},{8,0},{9,1},... | collective-permute-start | bytes 393224 | tf_op jit(solution)/shard_map/place/ppermute | solution.py:34
  (104 shorter events, 28.5 us)
Async XLA Ops:
  2.3 13.2 %collective-permute-start = (bf16[3,3,192,128]{3,2,1,0:T(8,128)(2,1)S(1)}, bf16[3,3,192,128]{3,2,1,0:T(8,128)(2,1)S(1)}, u32[]{:S(2)}, u32[]{:S(2)}) collective-permute-start(bf16[3,3,192,128]{3,2,1,0:T(8,128)(2,1)S(1)} %get-tuple-element.38), channel_id=1, source_target_pairs={{0,7},{1,6},{2,5},{3,4},{4,3},{5,2},{6,1},{7,0},{8,15},{9,14},{10,... | collective-permute-start | bytes 1327112 | tf_op jit(solution)/shard_map/rows/ppermute | solution.py:34
  4.1 11.7 %collective-permute-start.1 = (bf16[1728,128]{1,0:T(8,128)(2,1)S(1)}, bf16[1728,128]{1,0:T(8,128)(2,1)S(1)}, u32[]{:S(2)}, u32[]{:S(2)}) collective-permute-start(bf16[1728,128]{1,0:T(8,128)(2,1)S(1)} %bitcast.191), channel_id=1, source_target_pairs={{0,96},{1,97},{2,98},{3,99},{4,100},{5,101},{6,102},{7,103},{8,104... | collective-permute-start | bytes 1327112 | tf_op jit(solution)/shard_map/first/ppermute | solution.py:34
  6.7 11.9 %collective-permute-start.3 = (bf16[1728,128]{1,0:T(8,128)(2,1)S(1)}, bf16[1728,128]{1,0:T(8,128)(2,1)S(1)}, u32[]{:S(2)}, u32[]{:S(2)}) collective-permute-start(bf16[1728,128]{1,0:T(8,128)(2,1)S(1)} %bitcast.192), channel_id=1, source_target_pairs={{2,34},{3,35},{4,36},{5,37},{10,42},{11,43},{12,44},{13,45},{18,50... | collective-permute-start | bytes 1327112 | tf_op jit(solution)/shard_map/first/ppermute | solution.py:34
  7.4 24.5 %collective-permute-start.6 = (bf16[3,3,192,128]{3,2,1,0:T(8,128)(2,1)S(1)}, bf16[3,3,192,128]{3,2,1,0:T(8,128)(2,1)S(1)}, u32[]{:S(2)}, u32[]{:S(2)}) collective-permute-start(bf16[3,3,192,128]{3,2,1,0:T(8,128)(2,1)S(1)} %get-tuple-element.37), channel_id=1, source_target_pairs={{0,23},{1,22},{2,21},{3,20},{4,19},{5,18},{6,17},{7,16},{8,31},{9,... | collective-permute-start | bytes 1327112 | tf_op jit(solution)/shard_map/rows/ppermute | solution.py:34
  12.7 24.5 %collective-permute-start.5 = (bf16[3,3,192,128]{3,2,1,0:T(8,128)(2,1)S(1)}, bf16[3,3,192,128]{3,2,1,0:T(8,128)(2,1)S(1)}, u32[]{:S(2)}, u32[]{:S(2)}) collective-permute-start(bf16[3,3,192,128]{3,2,1,0:T(8,128)(2,1)S(1)} %get-tuple-element.40), channel_id=1, source_target_pairs={{0,16},{1,17},{2,18},{3,19},{4,20},{5,21},{6,22},{7,23},{8,24},{9,... | collective-permute-start | bytes 1327112 | tf_op jit(solution)/shard_map/rows/ppermute | solution.py:34
  15.8 22.1 %collective-permute-start.2 = (bf16[1728,128]{1,0:T(8,128)(2,1)S(1)}, bf16[1728,128]{1,0:T(8,128)(2,1)S(1)}, u32[]{:S(2)}, u32[]{:S(2)}) collective-permute-start(bf16[1728,128]{1,0:T(8,128)(2,1)S(1)} %bitcast.199), channel_id=1, source_target_pairs={{0,96},{1,97},{2,98},{3,99},{4,100},{5,101},{6,102},{7,103},{8,104... | collective-permute-start | bytes 1327112 | tf_op jit(solution)/shard_map/first/ppermute | solution.py:34
  18.6 19.4 %collective-permute-start.4 = (bf16[1728,128]{1,0:T(8,128)(2,1)S(1)}, bf16[1728,128]{1,0:T(8,128)(2,1)S(1)}, u32[]{:S(2)}, u32[]{:S(2)}) collective-permute-start(bf16[1728,128]{1,0:T(8,128)(2,1)S(1)} %bitcast.200), channel_id=1, source_target_pairs={{2,34},{3,35},{4,36},{5,37},{10,42},{11,43},{12,44},{13,45},{18,50... | collective-permute-start | bytes 1327112 | tf_op jit(solution)/shard_map/first/ppermute | solution.py:34
  37.3 5.2 %collective-permute-start.9 = (bf16[3456,128]{1,0:T(8,128)(2,1)S(1)}, bf16[3456,128]{1,0:T(8,128)(2,1)S(1)}, u32[]{:S(2)}, u32[]{:S(2)}) collective-permute-start(bf16[3456,128]{1,0:T(8,128)(2,1)S(1)} %pad_maximum_fusion), channel_id=1, source_target_pairs={{0,8},{1,9},{2,10},{3,11},{4,12},{5,13},{6,14},{7,15},{8,0},{9,1},... | collective-permute-start | bytes 2654216 | tf_op jit(solution)/shard_map/second/ppermute | solution.py:34
  39.3 24.7 %collective-permute-start.13 = (bf16[3456,128]{1,0:T(8,128)(2,1)S(1)}, bf16[3456,128]{1,0:T(8,128)(2,1)S(1)}, u32[]{:S(2)}, u32[]{:S(2)}) collective-permute-start(bf16[3456,128]{1,0:T(8,128)(2,1)S(1)} %pad_maximum_fusion), channel_id=1, source_target_pairs={{0,96},{1,97},{2,98},{3,99},{4,100},{5,101},{6,102},{7,103},{8,104... | collective-permute-start | bytes 2654216 | tf_op jit(solution)/shard_map/second/ppermute | solution.py:34
  41.8 24.7 %collective-permute-start.19 = (bf16[3456,128]{1,0:T(8,128)(2,1)S(1)}, bf16[3456,128]{1,0:T(8,128)(2,1)S(1)}, u32[]{:S(2)}, u32[]{:S(2)}) collective-permute-start(bf16[3456,128]{1,0:T(8,128)(2,1)S(1)} %pad_maximum_fusion), channel_id=1, source_target_pairs={{2,34},{3,35},{4,36},{5,37},{10,42},{11,43},{12,44},{13,45},{18,50... | collective-permute-start | bytes 2654216 | tf_op jit(solution)/shard_map/second/ppermute | solution.py:34
  48.1 9.2 %collective-permute-start.12 = (f32[2,128,256]{2,1,0:T(8,128)S(1)}, f32[2,128,256]{2,1,0:T(8,128)S(1)}, u32[]{:S(2)}, u32[]{:S(2)}) collective-permute-start(f32[2,128,256]{2,1,0:T(8,128)S(1)} %get-tuple-element.49), channel_id=1, source_target_pairs={{0,16},{1,17},{2,18},{3,19},{4,20},{5,21},{6,22},{7,23},{8,24},{9,... | collective-permute-start | bytes 786440 | tf_op jit(solution)/shard_map/same/ppermute | solution.py:34
  48.2 14.9 %collective-permute-start.11 = (f32[2,128,256]{2,1,0:T(8,128)S(1)}, f32[2,128,256]{2,1,0:T(8,128)S(1)}, u32[]{:S(2)}, u32[]{:S(2)}) collective-permute-start(f32[2,128,256]{2,1,0:T(8,128)S(1)} %get-tuple-element.48), channel_id=1, source_target_pairs={{0,1},{1,16},{2,3},{3,18},{4,5},{5,20},{6,7},{7,22},{8,9},{9,24},{... | collective-permute-start | bytes 786440 | tf_op jit(solution)/shard_map/same/ppermute | solution.py:34
  48.6 15.2 %collective-permute-start.10 = (f32[2,128,256]{2,1,0:T(8,128)S(1)}, f32[2,128,256]{2,1,0:T(8,128)S(1)}, u32[]{:S(2)}, u32[]{:S(2)}) collective-permute-start(f32[2,128,256]{2,1,0:T(8,128)S(1)} %get-tuple-element.47), channel_id=1, source_target_pairs={{0,17},{1,0},{2,19},{3,2},{4,21},{5,4},{6,23},{7,6},{8,25},{9,8},{... | collective-permute-start | bytes 786440 | tf_op jit(solution)/shard_map/same/ppermute | solution.py:34
  57.3 11.0 %collective-permute-start.17 = (bf16[1728,128]{1,0:T(8,128)(2,1)S(1)}, bf16[1728,128]{1,0:T(8,128)(2,1)S(1)}, u32[]{:S(2)}, u32[]{:S(2)}) collective-permute-start(bf16[1728,128]{1,0:T(8,128)(2,1)S(1)} %copy-done.1), channel_id=1, source_target_pairs={{0,8},{1,9},{2,10},{3,11},{4,12},{5,13},{6,14},{7,15},{8,0},{9,1},... | collective-permute-start | bytes 1327112 | tf_op jit(solution)/shard_map/second/ppermute | solution.py:34
  63.1 6.8 %collective-permute-start.18 = (bf16[1728,128]{1,0:T(8,128)(2,1)S(1)}, bf16[1728,128]{1,0:T(8,128)(2,1)S(1)}, u32[]{:S(2)}, u32[]{:S(2)}) collective-permute-start(bf16[1728,128]{1,0:T(8,128)(2,1)S(1)} %copy-done.3), channel_id=1, source_target_pairs={{0,8},{1,9},{2,10},{3,11},{4,12},{5,13},{6,14},{7,15},{8,0},{9,1},... | collective-permute-start | bytes 1327112 | tf_op jit(solution)/shard_map/second/ppermute | solution.py:34
  65.3 12.8 %collective-permute-start.16 = (f32[2,128,256]{2,1,0:T(8,128)S(1)}, f32[2,128,256]{2,1,0:T(8,128)S(1)}, u32[]{:S(2)}, u32[]{:S(2)}) collective-permute-start(f32[2,128,256]{2,1,0:T(8,128)S(1)} %get-tuple-element.46), channel_id=1, source_target_pairs={{0,16},{1,17},{2,18},{3,19},{4,20},{5,21},{6,22},{7,23},{8,24},{9,... | collective-permute-start | bytes 786440 | tf_op jit(solution)/shard_map/beside/ppermute | solution.py:34
  65.6 15.1 %collective-permute-start.15 = (f32[2,128,256]{2,1,0:T(8,128)S(1)}, f32[2,128,256]{2,1,0:T(8,128)}, u32[]{:S(2)}, u32[]{:S(2)}) collective-permute-start(f32[2,128,256]{2,1,0:T(8,128)S(1)} %get-tuple-element.45), channel_id=1, source_target_pairs={{0,1},{1,16},{2,3},{3,18},{4,5},{5,20},{6,7},{7,22},{8,9},{9,24},{... | collective-permute-start | bytes 786440 | tf_op jit(solution)/shard_map/beside/ppermute | solution.py:34
  66.5 14.2 %collective-permute-start.14 = (f32[2,128,256]{2,1,0:T(8,128)S(1)}, f32[2,128,256]{2,1,0:T(8,128)}, u32[]{:S(2)}, u32[]{:S(2)}) collective-permute-start(f32[2,128,256]{2,1,0:T(8,128)S(1)} %get-tuple-element.44), channel_id=1, source_target_pairs={{0,17},{1,0},{2,19},{3,2},{4,21},{5,4},{6,23},{7,6},{8,25},{9,8},{... | collective-permute-start | bytes 786440 | tf_op jit(solution)/shard_map/beside/ppermute | solution.py:34
  75.4 6.5 %collective-permute-start.23 = (f32[2,128,256]{2,1,0:T(8,128)}, f32[2,128,256]{2,1,0:T(8,128)}, u32[]{:S(2)}, u32[]{:S(2)}) collective-permute-start(f32[2,128,256]{2,1,0:T(8,128)} %get-tuple-element.43), channel_id=1, source_target_pairs={{0,16},{1,17},{2,18},{3,19},{8,24},{9,25},{10,26},{11,27},{16,0},{... | collective-permute-start | bytes 786440 | tf_op jit(solution)/shard_map/around/ppermute | solution.py:34
  76.8 5.1 %collective-permute-start.22 = (f32[2,128,256]{2,1,0:T(8,128)}, f32[2,128,256]{2,1,0:T(8,128)}, u32[]{:S(2)}, u32[]{:S(2)}) collective-permute-start(f32[2,128,256]{2,1,0:T(8,128)} %get-tuple-element.42), channel_id=1, source_target_pairs={{0,1},{1,16},{2,3},{3,18},{8,9},{9,24},{10,11},{11,26},{16,17},{17... | collective-permute-start | bytes 786440 | tf_op jit(solution)/shard_map/around/ppermute | solution.py:34
  83.2 16.7 %collective-permute-start.26 = (f32[2,128,256]{2,1,0:T(8,128)S(1)}, f32[2,128,256]{2,1,0:T(8,128)S(1)}, u32[]{:S(2)}, u32[]{:S(2)}) collective-permute-start(f32[2,128,256]{2,1,0:T(8,128)S(1)} %get-tuple-element.55), channel_id=1, source_target_pairs={{0,2},{1,3},{2,38},{3,54},{4,0},{5,1},{6,32},{7,33},{8,10},{9,11},... | collective-permute-start | bytes 786440 | tf_op jit(solution)/shard_map/over_y/ppermute | solution.py:34
  83.7 24.1 %collective-permute-start.24 = (f32[2,128,256]{2,1,0:T(8,128)S(1)}, f32[2,128,256]{2,1,0:T(8,128)S(1)}, u32[]{:S(2)}, u32[]{:S(2)}) collective-permute-start(f32[2,128,256]{2,1,0:T(8,128)S(1)} %get-tuple-element.54), channel_id=1, source_target_pairs={{0,32},{1,48},{2,98},{3,99},{4,2},{5,18},{6,0},{7,1},{8,40},{9,56}... | collective-permute-start | bytes 786440 | tf_op jit(solution)/shard_map/over_y/ppermute | solution.py:34
  96.2 11.5 %collective-permute-start.25 = (f32[2,128,256]{2,1,0:T(8,128)S(1)}, f32[2,128,256]{2,1,0:T(8,128)S(1)}, u32[]{:S(2)}, u32[]{:S(2)}) collective-permute-start(f32[2,128,256]{2,1,0:T(8,128)S(1)} %get-tuple-element.34), channel_id=1, source_target_pairs={{0,98},{1,114},{2,0},{3,1},{4,32},{5,33},{6,2},{7,18},{8,106},{9,1... | collective-permute-start | bytes 786440 | tf_op jit(solution)/shard_map/over_y/ppermute | solution.py:34
  98.6 13.8 %collective-permute-start.27 = (f32[2,128,256]{2,1,0:T(8,128)S(1)}, f32[2,128,256]{2,1,0:T(8,128)S(1)}, u32[]{:S(2)}, u32[]{:S(2)}) collective-permute-start(f32[2,128,256]{2,1,0:T(8,128)S(1)} %get-tuple-element.35), channel_id=1, source_target_pairs={{0,38},{1,39},{2,32},{3,48},{8,46},{9,47},{10,40},{11,56},{16,54},... | collective-permute-start | bytes 786440 | tf_op jit(solution)/shard_map/over_y/ppermute | solution.py:34
  (15 other events, 88.1 us)

commit v4 on v3

--- a/solution.py
+++ b/solution.py
@@ -125,7 +125,7 @@
             return jnp.where(column ^ h == 0, pick(first), pick(second))
 
         total = block(0)
-        for k in (3, 1, 2):
+        for k in (1, 3, 2):
             def target(x, h, c, y, l, k=k):
                 to = (2 * h + l + k) % 4
                 return (x, to // 2, c, y, to % 2) if active(x, h, c, y, l) else None
@@ -182,18 +182,16 @@
 
     with jax.named_scope("place"):
         scale = 1.0 / (NXW * NZ)
-        total = (straight * scale).reshape(2, own, 2, own)
-        turned = (turned * scale).reshape(2, own, 2, own)
-        received = send(total[1], across)
-        straight = jnp.where(
-            c == 0,
-            jnp.stack([total[0], received], axis=2),
-            jnp.stack([received, total[0]], axis=2),
-        )
-        straight = straight.transpose(1, 0, 2, 3).reshape(2, own, 2 * own)
-        by_core = jnp.where(c == 0, turned, turned[::-1])
-        turned = by_core.transpose(2, 3, 0, 1).reshape(2, own, 2 * own)
-        result = jnp.where(d == 3, turned, jnp.where(d == 2, straight + turned, straight))
+        mine, theirs = straight[0] * scale, straight[1] * scale
+        received = send(theirs, across)
+        turned = turned * scale
+        first, second = jnp.where(c == 0, turned[0], turned[1]), jnp.where(c == 0, turned[1], turned[0])
+        result = []
+        for part in (slice(0, own), slice(own, 2 * own)):
+            across_cores = jnp.concatenate([first[:, part].T, second[:, part].T], axis=1)
+            lower, upper = mine[:, part], received[:, part]
+            along = jnp.concatenate([jnp.where(c == 0, lower, upper), jnp.where(c == 0, upper, lower)], axis=1)
+            result.append(jnp.where(d == 3, across_cores, jnp.where(d == 2, along + across_cores, along)))
     return result[0], result[1]
 
 

time: 118 us -> 116 us (0.983)
  local copies, waits for them, and re-layouts: 10 us -> 8.06 us
  transfers between devices with their start and end apart: 29 -> 29, of which waited for: 10 -> 11; matrix products, arithmetic and copies ran while one was open for 13% -> 13% of each run, Pallas kernels for 0% -> 0%
where the time goes in v4:
time: 116 us; the launch traced here: 115 us
  starting transfers between devices  50 us (43%)
  waiting for transfers between devices  43.7 us (38%)
  local copies, waits for them, and re-layouts  8.06 us (7%)
  matrix products  7.52 us (6%)
  other arithmetic  4.7 us (4%)
  between operations  1.21 us (1%)
    ppermute x29, starting transfers between devices, send(): return lax.ppermute(value, AXES, pairs)  50 us
    ppermute x29, waiting for transfers between devices, send(): return lax.ppermute(value, AXES, pairs)  43.7 us
    dot_general x6, matrix products, inner(): lax.dot_general(left, right, (((0,), (0,)), ((), ())), preferred_element_...  6.94 us
  transfers between devices with their start and end apart: 29, of which 11 were waited for; matrix products, arithmetic and copies ran while one was open for 13% of the time, Pallas kernels for 0%

profile of v4, /device:TPU:25, one launch (start us, length us, event | category | flops | bytes accessed | tf_op | source)
XLA Modules:
  0.0 115.2 jit_solution(7172208776228196277)
XLA Ops:
  0.7 1.6 %constant_dynamic-slice_fusion = (bf16[3,3,192,128]{3,2,1,0:T(8,128)(2,1)S(1)}, bf16[3,3,192,128]{3,2,1,0:T(8,128)(2,1)S(1)}, bf16[3,3,192,128]{3,2,1,0:T(8,128)(2,1)S(1)}, bf16[3,3,192,128]{3,2,1,0:T(8,128)(2,1)S(1)}) fusion(bf16[3,12,192,128]{3,2,1,0:T(8,128)(2,1)} %param.2, s32[]{:T(128)S(6)} %select_n.501, s32[]{:T(128)S(6)} %select_n.499, ...), kind=kLoop, calls=%fused_computation.98 | loop fusion | bytes 3538960 | tf_op jit(solution)/shard_map/rows/dynamic_slice | solution.py:65
  2.3 1.4 %collective-permute-start = (bf16[3,3,192,128]{3,2,1,0:T(8,128)(2,1)S(1)}, bf16[3,3,192,128]{3,2,1,0:T(8,128)(2,1)S(1)}, u32[]{:S(2)}, u32[]{:S(2)}) collective-permute-start(bf16[3,3,192,128]{3,2,1,0:T(8,128)(2,1)S(1)} %get-tuple-element.38), channel_id=1, source_target_pairs={{0,7},{1,6},{2,5},{3,4},{4,3},{5,2},{6,1},{7,0},{8,15},{9,14},{10,... | collective-permute-start | bytes 1327112 | tf_op jit(solution)/shard_map/rows/ppermute | solution.py:34
  4.1 2.5 %collective-permute-start.1 = (bf16[1728,128]{1,0:T(8,128)(2,1)S(1)}, bf16[1728,128]{1,0:T(8,128)(2,1)S(1)}, u32[]{:S(2)}, u32[]{:S(2)}) collective-permute-start(bf16[1728,128]{1,0:T(8,128)(2,1)S(1)} %bitcast.194), channel_id=1, source_target_pairs={{0,96},{1,97},{2,98},{3,99},{4,100},{5,101},{6,102},{7,103},{8,104... | collective-permute-start | bytes 1327112 | tf_op jit(solution)/shard_map/first/ppermute | solution.py:34
  7.4 5.4 %collective-permute-start.6 = (bf16[3,3,192,128]{3,2,1,0:T(8,128)(2,1)S(1)}, bf16[3,3,192,128]{3,2,1,0:T(8,128)(2,1)S(1)}, u32[]{:S(2)}, u32[]{:S(2)}) collective-permute-start(bf16[3,3,192,128]{3,2,1,0:T(8,128)(2,1)S(1)} %get-tuple-element.37), channel_id=1, source_target_pairs={{0,23},{1,22},{2,21},{3,20},{4,19},{5,18},{6,17},{7,16},{8,31},{9,... | collective-permute-start | bytes 1327112 | tf_op jit(solution)/shard_map/rows/ppermute | solution.py:34
  12.7 2.8 %collective-permute-done = bf16[3,3,192,128]{3,2,1,0:T(8,128)(2,1)S(1)} collective-permute-done((bf16[3,3,192,128]{3,2,1,0:T(8,128)(2,1)S(1)}, bf16[3,3,192,128]{3,2,1,0:T(8,128)(2,1)S(1)}, u32[]{:S(2)}, u32[]{:S(2)}) %collective-permute-start) | collective-permute-done | bytes 442400 | tf_op jit(solution)/shard_map/rows/ppermute | solution.py:34
  15.8 2.8 %collective-permute-start.2 = (bf16[1728,128]{1,0:T(8,128)(2,1)S(1)}, bf16[1728,128]{1,0:T(8,128)(2,1)S(1)}, u32[]{:S(2)}, u32[]{:S(2)}) collective-permute-start(bf16[1728,128]{1,0:T(8,128)(2,1)S(1)} %bitcast.202), channel_id=1, source_target_pairs={{0,96},{1,97},{2,98},{3,99},{4,100},{5,101},{6,102},{7,103},{8,104... | collective-permute-start | bytes 1327112 | tf_op jit(solution)/shard_map/first/ppermute | solution.py:34
  19.4 12.4 %collective-permute-done.6 = bf16[3,3,192,128]{3,2,1,0:T(8,128)(2,1)S(1)} collective-permute-done((bf16[3,3,192,128]{3,2,1,0:T(8,128)(2,1)S(1)}, bf16[3,3,192,128]{3,2,1,0:T(8,128)(2,1)S(1)}, u32[]{:S(2)}, u32[]{:S(2)}) %collective-permute-start.6) | collective-permute-done | bytes 442400 | tf_op jit(solution)/shard_map/rows/ppermute | solution.py:34
  32.1 5.2 %collective-permute-done.5 = bf16[3,3,192,128]{3,2,1,0:T(8,128)(2,1)S(1)} collective-permute-done((bf16[3,3,192,128]{3,2,1,0:T(8,128)(2,1)S(1)}, bf16[3,3,192,128]{3,2,1,0:T(8,128)(2,1)S(1)}, u32[]{:S(2)}, u32[]{:S(2)}) %collective-permute-start.5) | collective-permute-done | bytes 442400 | tf_op jit(solution)/shard_map/rows/ppermute | solution.py:34
  39.3 2.5 %collective-permute-start.13 = (bf16[3456,128]{1,0:T(8,128)(2,1)S(1)}, bf16[3456,128]{1,0:T(8,128)(2,1)S(1)}, u32[]{:S(2)}, u32[]{:S(2)}) collective-permute-start(bf16[3456,128]{1,0:T(8,128)(2,1)S(1)} %pad_maximum_fusion), channel_id=1, source_target_pairs={{0,96},{1,97},{2,98},{3,99},{4,100},{5,101},{6,102},{7,103},{8,104... | collective-permute-start | bytes 2654216 | tf_op jit(solution)/shard_map/second/ppermute | solution.py:34
  48.2 2.5 %collective-permute-start.11 = (f32[2,128,256]{2,1,0:T(8,128)S(1)}, f32[2,128,256]{2,1,0:T(8,128)S(1)}, u32[]{:S(2)}, u32[]{:S(2)}) collective-permute-start(f32[2,128,256]{2,1,0:T(8,128)S(1)} %get-tuple-element.48), channel_id=1, source_target_pairs={{0,17},{1,0},{2,19},{3,2},{4,21},{5,4},{6,23},{7,6},{8,25},{9,8},{... | collective-permute-start | bytes 786440 | tf_op jit(solution)/shard_map/same/ppermute | solution.py:34
  51.9 5.3 %collective-permute-done.12 = f32[2,128,256]{2,1,0:T(8,128)S(1)} collective-permute-done((f32[2,128,256]{2,1,0:T(8,128)S(1)}, f32[2,128,256]{2,1,0:T(8,128)S(1)}, u32[]{:S(2)}, u32[]{:S(2)}) %collective-permute-start.12) | collective-permute-done | bytes 262176 | tf_op jit(solution)/shard_map/same/ppermute | solution.py:34
  57.2 2.1 %collective-permute-start.17 = (bf16[1728,128]{1,0:T(8,128)(2,1)S(1)}, bf16[1728,128]{1,0:T(8,128)(2,1)S(1)}, u32[]{:S(2)}, u32[]{:S(2)}) collective-permute-start(bf16[1728,128]{1,0:T(8,128)(2,1)S(1)} %copy-done.1), channel_id=1, source_target_pairs={{0,8},{1,9},{2,10},{3,11},{4,12},{5,13},{6,14},{7,15},{8,0},{9,1},... | collective-permute-start | bytes 1327112 | tf_op jit(solution)/shard_map/second/ppermute | solution.py:34
  61.5 2.0 %collective-permute-done.10 = f32[2,128,256]{2,1,0:T(8,128)S(1)} collective-permute-done((f32[2,128,256]{2,1,0:T(8,128)S(1)}, f32[2,128,256]{2,1,0:T(8,128)S(1)}, u32[]{:S(2)}, u32[]{:S(2)}) %collective-permute-start.10) | collective-permute-done | bytes 262176 | tf_op jit(solution)/shard_map/same/ppermute | solution.py:34
  65.0 1.4 %collective-permute-start.16 = (f32[2,128,256]{2,1,0:T(8,128)S(1)}, f32[2,128,256]{2,1,0:T(8,128)S(1)}, u32[]{:S(2)}, u32[]{:S(2)}) collective-permute-start(f32[2,128,256]{2,1,0:T(8,128)S(1)} %get-tuple-element.46), channel_id=1, source_target_pairs={{0,16},{1,17},{2,18},{3,19},{4,20},{5,21},{6,22},{7,23},{8,24},{9,... | collective-permute-start | bytes 786440 | tf_op jit(solution)/shard_map/beside/ppermute | solution.py:34
  66.3 1.3 %collective-permute-start.15 = (f32[2,128,256]{2,1,0:T(8,128)S(1)}, f32[2,128,256]{2,1,0:T(8,128)}, u32[]{:S(2)}, u32[]{:S(2)}) collective-permute-start(f32[2,128,256]{2,1,0:T(8,128)S(1)} %get-tuple-element.45), channel_id=1, source_target_pairs={{0,17},{1,0},{2,19},{3,2},{4,21},{5,4},{6,23},{7,6},{8,25},{9,8},{... | collective-permute-start | bytes 786440 | tf_op jit(solution)/shard_map/beside/ppermute | solution.py:34
  74.2 1.4 %collective-permute-start.23 = (f32[2,128,256]{2,1,0:T(8,128)}, f32[2,128,256]{2,1,0:T(8,128)}, u32[]{:S(2)}, u32[]{:S(2)}) collective-permute-start(f32[2,128,256]{2,1,0:T(8,128)} %get-tuple-element.43), channel_id=1, source_target_pairs={{0,16},{1,17},{2,18},{3,19},{8,24},{9,25},{10,26},{11,27},{16,0},{... | collective-permute-start | bytes 786440 | tf_op jit(solution)/shard_map/around/ppermute | solution.py:34
  75.5 1.4 %collective-permute-start.22 = (f32[2,128,256]{2,1,0:T(8,128)}, f32[2,128,256]{2,1,0:T(8,128)}, u32[]{:S(2)}, u32[]{:S(2)}) collective-permute-start(f32[2,128,256]{2,1,0:T(8,128)} %get-tuple-element.42), channel_id=1, source_target_pairs={{0,17},{1,0},{2,19},{3,2},{8,25},{9,8},{10,27},{11,10},{16,1},{17,... | collective-permute-start | bytes 786440 | tf_op jit(solution)/shard_map/around/ppermute | solution.py:34
  77.6 1.4 %collective-permute-start.21 = (f32[2,128,256]{2,1,0:T(8,128)S(1)}, f32[2,128,256]{2,1,0:T(8,128)}, u32[]{:S(2)}, u32[]{:S(2)}) collective-permute-start(f32[2,128,256]{2,1,0:T(8,128)S(1)} %get-tuple-element.41), channel_id=1, source_target_pairs={{0,1},{1,16},{2,3},{3,18},{8,9},{9,24},{10,11},{11,26},{16,17},{17... | collective-permute-start | bytes 786440 | tf_op jit(solution)/shard_map/around/ppermute | solution.py:34
  79.0 1.6 %collective-permute-done.14 = f32[2,128,256]{2,1,0:T(8,128)} collective-permute-done((f32[2,128,256]{2,1,0:T(8,128)S(1)}, f32[2,128,256]{2,1,0:T(8,128)}, u32[]{:S(2)}, u32[]{:S(2)}) %collective-permute-start.14) | collective-permute-done | bytes 262176 | tf_op jit(solution)/shard_map/beside/ppermute | solution.py:34
  83.1 11.8 %collective-permute-start.24 = (f32[2,128,256]{2,1,0:T(8,128)S(1)}, f32[2,128,256]{2,1,0:T(8,128)S(1)}, u32[]{:S(2)}, u32[]{:S(2)}) collective-permute-start(f32[2,128,256]{2,1,0:T(8,128)S(1)} %get-tuple-element.54), channel_id=1, source_target_pairs={{0,32},{1,48},{2,98},{3,99},{4,2},{5,18},{6,0},{7,1},{8,40},{9,56}... | collective-permute-start | bytes 786440 | tf_op jit(solution)/shard_map/over_y/ppermute | solution.py:34
  94.9 2.1 %collective-permute-start.25 = (f32[2,128,256]{2,1,0:T(8,128)S(1)}, f32[2,128,256]{2,1,0:T(8,128)S(1)}, u32[]{:S(2)}, u32[]{:S(2)}) collective-permute-start(f32[2,128,256]{2,1,0:T(8,128)S(1)} %get-tuple-element.34), channel_id=1, source_target_pairs={{0,98},{1,114},{2,0},{3,1},{4,32},{5,33},{6,2},{7,18},{8,106},{9,1... | collective-permute-start | bytes 786440 | tf_op jit(solution)/shard_map/over_y/ppermute | solution.py:34
  98.3 7.6 %collective-permute-done.24 = f32[2,128,256]{2,1,0:T(8,128)S(1)} collective-permute-done((f32[2,128,256]{2,1,0:T(8,128)S(1)}, f32[2,128,256]{2,1,0:T(8,128)S(1)}, u32[]{:S(2)}, u32[]{:S(2)}) %collective-permute-start.24) | collective-permute-done | bytes 262176 | tf_op jit(solution)/shard_map/over_y/ppermute | solution.py:34
  105.9 3.9 %collective-permute-done.27 = f32[2,128,256]{2,1,0:T(8,128)S(1)} collective-permute-done((f32[2,128,256]{2,1,0:T(8,128)S(1)}, f32[2,128,256]{2,1,0:T(8,128)S(1)}, u32[]{:S(2)}, u32[]{:S(2)}) %collective-permute-start.27) | collective-permute-done | bytes 262176 | tf_op jit(solution)/shard_map/over_y/ppermute | solution.py:34
  110.2 3.3 %collective-permute-start.28 = (f32[128,256]{1,0:T(8,128)S(1)}, f32[128,256]{1,0:T(8,128)S(1)}, u32[]{:S(2)}, u32[]{:S(2)}) collective-permute-start(f32[128,256]{1,0:T(8,128)S(1)} %get-tuple-element.61), channel_id=1, source_target_pairs={{0,8},{1,9},{2,10},{3,11},{4,12},{5,13},{6,14},{7,15},{8,0},{9,1},... | collective-permute-start | bytes 393224 | tf_op jit(solution)/shard_map/place/ppermute | solution.py:34
  (100 shorter events, 28.6 us)
Async XLA Ops:
  2.3 13.2 %collective-permute-start = (bf16[3,3,192,128]{3,2,1,0:T(8,128)(2,1)S(1)}, bf16[3,3,192,128]{3,2,1,0:T(8,128)(2,1)S(1)}, u32[]{:S(2)}, u32[]{:S(2)}) collective-permute-start(bf16[3,3,192,128]{3,2,1,0:T(8,128)(2,1)S(1)} %get-tuple-element.38), channel_id=1, source_target_pairs={{0,7},{1,6},{2,5},{3,4},{4,3},{5,2},{6,1},{7,0},{8,15},{9,14},{10,... | collective-permute-start | bytes 1327112 | tf_op jit(solution)/shard_map/rows/ppermute | solution.py:34
  4.1 11.7 %collective-permute-start.1 = (bf16[1728,128]{1,0:T(8,128)(2,1)S(1)}, bf16[1728,128]{1,0:T(8,128)(2,1)S(1)}, u32[]{:S(2)}, u32[]{:S(2)}) collective-permute-start(bf16[1728,128]{1,0:T(8,128)(2,1)S(1)} %bitcast.194), channel_id=1, source_target_pairs={{0,96},{1,97},{2,98},{3,99},{4,100},{5,101},{6,102},{7,103},{8,104... | collective-permute-start | bytes 1327112 | tf_op jit(solution)/shard_map/first/ppermute | solution.py:34
  6.7 11.9 %collective-permute-start.3 = (bf16[1728,128]{1,0:T(8,128)(2,1)S(1)}, bf16[1728,128]{1,0:T(8,128)(2,1)S(1)}, u32[]{:S(2)}, u32[]{:S(2)}) collective-permute-start(bf16[1728,128]{1,0:T(8,128)(2,1)S(1)} %bitcast.195), channel_id=1, source_target_pairs={{2,34},{3,35},{4,36},{5,37},{10,42},{11,43},{12,44},{13,45},{18,50... | collective-permute-start | bytes 1327112 | tf_op jit(solution)/shard_map/first/ppermute | solution.py:34
  7.4 24.5 %collective-permute-start.6 = (bf16[3,3,192,128]{3,2,1,0:T(8,128)(2,1)S(1)}, bf16[3,3,192,128]{3,2,1,0:T(8,128)(2,1)S(1)}, u32[]{:S(2)}, u32[]{:S(2)}) collective-permute-start(bf16[3,3,192,128]{3,2,1,0:T(8,128)(2,1)S(1)} %get-tuple-element.37), channel_id=1, source_target_pairs={{0,23},{1,22},{2,21},{3,20},{4,19},{5,18},{6,17},{7,16},{8,31},{9,... | collective-permute-start | bytes 1327112 | tf_op jit(solution)/shard_map/rows/ppermute | solution.py:34
  12.7 24.5 %collective-permute-start.5 = (bf16[3,3,192,128]{3,2,1,0:T(8,128)(2,1)S(1)}, bf16[3,3,192,128]{3,2,1,0:T(8,128)(2,1)S(1)}, u32[]{:S(2)}, u32[]{:S(2)}) collective-permute-start(bf16[3,3,192,128]{3,2,1,0:T(8,128)(2,1)S(1)} %get-tuple-element.40), channel_id=1, source_target_pairs={{0,16},{1,17},{2,18},{3,19},{4,20},{5,21},{6,22},{7,23},{8,24},{9,... | collective-permute-start | bytes 1327112 | tf_op jit(solution)/shard_map/rows/ppermute | solution.py:34
  15.8 22.1 %collective-permute-start.2 = (bf16[1728,128]{1,0:T(8,128)(2,1)S(1)}, bf16[1728,128]{1,0:T(8,128)(2,1)S(1)}, u32[]{:S(2)}, u32[]{:S(2)}) collective-permute-start(bf16[1728,128]{1,0:T(8,128)(2,1)S(1)} %bitcast.202), channel_id=1, source_target_pairs={{0,96},{1,97},{2,98},{3,99},{4,100},{5,101},{6,102},{7,103},{8,104... | collective-permute-start | bytes 1327112 | tf_op jit(solution)/shard_map/first/ppermute | solution.py:34
  18.6 19.4 %collective-permute-start.4 = (bf16[1728,128]{1,0:T(8,128)(2,1)S(1)}, bf16[1728,128]{1,0:T(8,128)(2,1)S(1)}, u32[]{:S(2)}, u32[]{:S(2)}) collective-permute-start(bf16[1728,128]{1,0:T(8,128)(2,1)S(1)} %bitcast.203), channel_id=1, source_target_pairs={{2,34},{3,35},{4,36},{5,37},{10,42},{11,43},{12,44},{13,45},{18,50... | collective-permute-start | bytes 1327112 | tf_op jit(solution)/shard_map/first/ppermute | solution.py:34
  37.3 5.2 %collective-permute-start.9 = (bf16[3456,128]{1,0:T(8,128)(2,1)S(1)}, bf16[3456,128]{1,0:T(8,128)(2,1)S(1)}, u32[]{:S(2)}, u32[]{:S(2)}) collective-permute-start(bf16[3456,128]{1,0:T(8,128)(2,1)S(1)} %pad_maximum_fusion), channel_id=1, source_target_pairs={{0,8},{1,9},{2,10},{3,11},{4,12},{5,13},{6,14},{7,15},{8,0},{9,1},... | collective-permute-start | bytes 2654216 | tf_op jit(solution)/shard_map/second/ppermute | solution.py:34
  39.3 24.3 %collective-permute-start.13 = (bf16[3456,128]{1,0:T(8,128)(2,1)S(1)}, bf16[3456,128]{1,0:T(8,128)(2,1)S(1)}, u32[]{:S(2)}, u32[]{:S(2)}) collective-permute-start(bf16[3456,128]{1,0:T(8,128)(2,1)S(1)} %pad_maximum_fusion), channel_id=1, source_target_pairs={{0,96},{1,97},{2,98},{3,99},{4,100},{5,101},{6,102},{7,103},{8,104... | collective-permute-start | bytes 2654216 | tf_op jit(solution)/shard_map/second/ppermute | solution.py:34
  41.8 25.9 %collective-permute-start.19 = (bf16[3456,128]{1,0:T(8,128)(2,1)S(1)}, bf16[3456,128]{1,0:T(8,128)(2,1)S(1)}, u32[]{:S(2)}, u32[]{:S(2)}) collective-permute-start(bf16[3456,128]{1,0:T(8,128)(2,1)S(1)} %pad_maximum_fusion), channel_id=1, source_target_pairs={{2,34},{3,35},{4,36},{5,37},{10,42},{11,43},{12,44},{13,45},{18,50... | collective-permute-start | bytes 2654216 | tf_op jit(solution)/shard_map/second/ppermute | solution.py:34
  48.1 9.1 %collective-permute-start.12 = (f32[2,128,256]{2,1,0:T(8,128)S(1)}, f32[2,128,256]{2,1,0:T(8,128)S(1)}, u32[]{:S(2)}, u32[]{:S(2)}) collective-permute-start(f32[2,128,256]{2,1,0:T(8,128)S(1)} %get-tuple-element.49), channel_id=1, source_target_pairs={{0,16},{1,17},{2,18},{3,19},{4,20},{5,21},{6,22},{7,23},{8,24},{9,... | collective-permute-start | bytes 786440 | tf_op jit(solution)/shard_map/same/ppermute | solution.py:34
  48.2 12.0 %collective-permute-start.11 = (f32[2,128,256]{2,1,0:T(8,128)S(1)}, f32[2,128,256]{2,1,0:T(8,128)S(1)}, u32[]{:S(2)}, u32[]{:S(2)}) collective-permute-start(f32[2,128,256]{2,1,0:T(8,128)S(1)} %get-tuple-element.48), channel_id=1, source_target_pairs={{0,17},{1,0},{2,19},{3,2},{4,21},{5,4},{6,23},{7,6},{8,25},{9,8},{... | collective-permute-start | bytes 786440 | tf_op jit(solution)/shard_map/same/ppermute | solution.py:34
  50.7 12.8 %collective-permute-start.10 = (f32[2,128,256]{2,1,0:T(8,128)S(1)}, f32[2,128,256]{2,1,0:T(8,128)S(1)}, u32[]{:S(2)}, u32[]{:S(2)}) collective-permute-start(f32[2,128,256]{2,1,0:T(8,128)S(1)} %get-tuple-element.47), channel_id=1, source_target_pairs={{0,1},{1,16},{2,3},{3,18},{4,5},{5,20},{6,7},{7,22},{8,9},{9,24},{... | collective-permute-start | bytes 786440 | tf_op jit(solution)/shard_map/same/ppermute | solution.py:34
  57.2 10.6 %collective-permute-start.17 = (bf16[1728,128]{1,0:T(8,128)(2,1)S(1)}, bf16[1728,128]{1,0:T(8,128)(2,1)S(1)}, u32[]{:S(2)}, u32[]{:S(2)}) collective-permute-start(bf16[1728,128]{1,0:T(8,128)(2,1)S(1)} %copy-done.1), channel_id=1, source_target_pairs={{0,8},{1,9},{2,10},{3,11},{4,12},{5,13},{6,14},{7,15},{8,0},{9,1},... | collective-permute-start | bytes 1327112 | tf_op jit(solution)/shard_map/second/ppermute | solution.py:34
  60.2 8.5 %collective-permute-start.18 = (bf16[1728,128]{1,0:T(8,128)(2,1)S(1)}, bf16[1728,128]{1,0:T(8,128)(2,1)S(1)}, u32[]{:S(2)}, u32[]{:S(2)}) collective-permute-start(bf16[1728,128]{1,0:T(8,128)(2,1)S(1)} %copy-done.3), channel_id=1, source_target_pairs={{0,8},{1,9},{2,10},{3,11},{4,12},{5,13},{6,14},{7,15},{8,0},{9,1},... | collective-permute-start | bytes 1327112 | tf_op jit(solution)/shard_map/second/ppermute | solution.py:34
  65.0 11.9 %collective-permute-start.16 = (f32[2,128,256]{2,1,0:T(8,128)S(1)}, f32[2,128,256]{2,1,0:T(8,128)S(1)}, u32[]{:S(2)}, u32[]{:S(2)}) collective-permute-start(f32[2,128,256]{2,1,0:T(8,128)S(1)} %get-tuple-element.46), channel_id=1, source_target_pairs={{0,16},{1,17},{2,18},{3,19},{4,20},{5,21},{6,22},{7,23},{8,24},{9,... | collective-permute-start | bytes 786440 | tf_op jit(solution)/shard_map/beside/ppermute | solution.py:34
  66.3 12.6 %collective-permute-start.15 = (f32[2,128,256]{2,1,0:T(8,128)S(1)}, f32[2,128,256]{2,1,0:T(8,128)}, u32[]{:S(2)}, u32[]{:S(2)}) collective-permute-start(f32[2,128,256]{2,1,0:T(8,128)S(1)} %get-tuple-element.45), channel_id=1, source_target_pairs={{0,17},{1,0},{2,19},{3,2},{4,21},{5,4},{6,23},{7,6},{8,25},{9,8},{... | collective-permute-start | bytes 786440 | tf_op jit(solution)/shard_map/beside/ppermute | solution.py:34
  67.6 12.9 %collective-permute-start.14 = (f32[2,128,256]{2,1,0:T(8,128)S(1)}, f32[2,128,256]{2,1,0:T(8,128)}, u32[]{:S(2)}, u32[]{:S(2)}) collective-permute-start(f32[2,128,256]{2,1,0:T(8,128)S(1)} %get-tuple-element.44), channel_id=1, source_target_pairs={{0,1},{1,16},{2,3},{3,18},{4,5},{5,20},{6,7},{7,22},{8,9},{9,24},{... | collective-permute-start | bytes 786440 | tf_op jit(solution)/shard_map/beside/ppermute | solution.py:34
  74.2 7.6 %collective-permute-start.23 = (f32[2,128,256]{2,1,0:T(8,128)}, f32[2,128,256]{2,1,0:T(8,128)}, u32[]{:S(2)}, u32[]{:S(2)}) collective-permute-start(f32[2,128,256]{2,1,0:T(8,128)} %get-tuple-element.43), channel_id=1, source_target_pairs={{0,16},{1,17},{2,18},{3,19},{8,24},{9,25},{10,26},{11,27},{16,0},{... | collective-permute-start | bytes 786440 | tf_op jit(solution)/shard_map/around/ppermute | solution.py:34
  75.5 6.2 %collective-permute-start.22 = (f32[2,128,256]{2,1,0:T(8,128)}, f32[2,128,256]{2,1,0:T(8,128)}, u32[]{:S(2)}, u32[]{:S(2)}) collective-permute-start(f32[2,128,256]{2,1,0:T(8,128)} %get-tuple-element.42), channel_id=1, source_target_pairs={{0,17},{1,0},{2,19},{3,2},{8,25},{9,8},{10,27},{11,10},{16,1},{17,... | collective-permute-start | bytes 786440 | tf_op jit(solution)/shard_map/around/ppermute | solution.py:34
  83.0 15.3 %collective-permute-start.26 = (f32[2,128,256]{2,1,0:T(8,128)S(1)}, f32[2,128,256]{2,1,0:T(8,128)S(1)}, u32[]{:S(2)}, u32[]{:S(2)}) collective-permute-start(f32[2,128,256]{2,1,0:T(8,128)S(1)} %get-tuple-element.55), channel_id=1, source_target_pairs={{0,2},{1,3},{2,38},{3,54},{4,0},{5,1},{6,32},{7,33},{8,10},{9,11},... | collective-permute-start | bytes 786440 | tf_op jit(solution)/shard_map/over_y/ppermute | solution.py:34
  83.1 22.8 %collective-permute-start.24 = (f32[2,128,256]{2,1,0:T(8,128)S(1)}, f32[2,128,256]{2,1,0:T(8,128)S(1)}, u32[]{:S(2)}, u32[]{:S(2)}) collective-permute-start(f32[2,128,256]{2,1,0:T(8,128)S(1)} %get-tuple-element.54), channel_id=1, source_target_pairs={{0,32},{1,48},{2,98},{3,99},{4,2},{5,18},{6,0},{7,1},{8,40},{9,56}... | collective-permute-start | bytes 786440 | tf_op jit(solution)/shard_map/over_y/ppermute | solution.py:34
  94.9 11.0 %collective-permute-start.25 = (f32[2,128,256]{2,1,0:T(8,128)S(1)}, f32[2,128,256]{2,1,0:T(8,128)S(1)}, u32[]{:S(2)}, u32[]{:S(2)}) collective-permute-start(f32[2,128,256]{2,1,0:T(8,128)S(1)} %get-tuple-element.34), channel_id=1, source_target_pairs={{0,98},{1,114},{2,0},{3,1},{4,32},{5,33},{6,2},{7,18},{8,106},{9,1... | collective-permute-start | bytes 786440 | tf_op jit(solution)/shard_map/over_y/ppermute | solution.py:34
  97.0 12.8 %collective-permute-start.27 = (f32[2,128,256]{2,1,0:T(8,128)S(1)}, f32[2,128,256]{2,1,0:T(8,128)S(1)}, u32[]{:S(2)}, u32[]{:S(2)}) collective-permute-start(f32[2,128,256]{2,1,0:T(8,128)S(1)} %get-tuple-element.35), channel_id=1, source_target_pairs={{0,38},{1,39},{2,32},{3,48},{8,46},{9,47},{10,40},{11,56},{16,54},... | collective-permute-start | bytes 786440 | tf_op jit(solution)/shard_map/over_y/ppermute | solution.py:34
  (15 other events, 82.0 us)

commit v5 on v4

--- a/solution.py
+++ b/solution.py
@@ -150,6 +150,7 @@
         )
 
     same, beside = lax.optimization_barrier((same, beside))
+    mixed = lax.optimization_barrier(tuple(jnp.where(d == at, same, beside) for at in (3, 2, 1)))
 
     rounds = (
         ((1, True), (2, False), (1, False), (0, False)),
@@ -170,10 +171,10 @@
                 if turn != ((y - x) % 4 in SWAPS[block]):
                     h, l = l, h
                 return row % 4, h, c, column, l
-            value = beside
+            value = (mixed + (beside,))[len(got)]
             for at, step in enumerate(plan):
-                if step is not None and step[0] != 1:
-                    value = jnp.where(d == at, (same, beside, around)[step[0]], value)
+                if step is not None and step[0] == 2:
+                    value = jnp.where(d == at, around, value)
             got.append(send(value, target))
         own_block = jnp.where(d == 0, same, beside)
         odd = got[0] + got[2]

time: 116 us -> 114 us (0.983)
  other arithmetic: 4.7 us -> 1.78 us
  waiting for transfers between devices: 43.7 us -> 46.6 us
  starting transfers between devices: 50 us -> 48.5 us
    ppermute x29, waiting for transfers between devices: 43.7 us -> 46.6 us  [send(): return lax.ppermute(value, AXES, pairs)]
    ppermute x29, starting transfers between devices: 50 us -> 48.5 us  [send(): return lax.ppermute(value, AXES, pairs)]
  transfers between devices with their start and end apart: 29 -> 29, of which waited for: 11 -> 12; matrix products, arithmetic and copies ran while one was open for 13% -> 11% of each run, Pallas kernels for 0% -> 0%
where the time goes in v5:
time: 114 us; the launch traced here: 113 us
  starting transfers between devices  48.5 us (43%)
  waiting for transfers between devices  46.6 us (41%)
  matrix products  7.53 us (7%)
  local copies, waits for them, and re-layouts  7.26 us (6%)
  other arithmetic  1.78 us (2%)
  between operations  1.25 us (1%)
    ppermute x29, starting transfers between devices, send(): return lax.ppermute(value, AXES, pairs)  48.5 us
    ppermute x29, waiting for transfers between devices, send(): return lax.ppermute(value, AXES, pairs)  46.6 us
    dot_general x6, matrix products, inner(): lax.dot_general(left, right, (((0,), (0,)), ((), ())), preferred_element_...  6.95 us
  transfers between devices with their start and end apart: 29, of which 12 were waited for; matrix products, arithmetic and copies ran while one was open for 11% of the time, Pallas kernels for 0%

profile of v5, /device:TPU:25, one launch (start us, length us, event | category | flops | bytes accessed | tf_op | source)
XLA Modules:
  0.0 112.9 jit_solution(15448877845296208500)
XLA Ops:
  0.7 1.5 %constant_dynamic-slice_fusion = (bf16[3,3,192,128]{3,2,1,0:T(8,128)(2,1)S(1)}, bf16[3,3,192,128]{3,2,1,0:T(8,128)(2,1)S(1)}, bf16[3,3,192,128]{3,2,1,0:T(8,128)(2,1)S(1)}, bf16[3,3,192,128]{3,2,1,0:T(8,128)(2,1)S(1)}) fusion(bf16[3,12,192,128]{3,2,1,0:T(8,128)(2,1)} %param.2, s32[]{:T(128)S(6)} %select_n.507, s32[]{:T(128)S(6)} %select_n.505, ...), kind=kLoop, calls=%fused_computation.100 | loop fusion | bytes 3538960 | tf_op jit(solution)/shard_map/rows/dynamic_slice | solution.py:65
  2.3 1.4 %collective-permute-start = (bf16[3,3,192,128]{3,2,1,0:T(8,128)(2,1)S(1)}, bf16[3,3,192,128]{3,2,1,0:T(8,128)(2,1)S(1)}, u32[]{:S(2)}, u32[]{:S(2)}) collective-permute-start(bf16[3,3,192,128]{3,2,1,0:T(8,128)(2,1)S(1)} %get-tuple-element.43), channel_id=1, source_target_pairs={{0,7},{1,6},{2,5},{3,4},{4,3},{5,2},{6,1},{7,0},{8,15},{9,14},{10,... | collective-permute-start | bytes 1327112 | tf_op jit(solution)/shard_map/rows/ppermute | solution.py:34
  4.1 2.5 %collective-permute-start.1 = (bf16[1728,128]{1,0:T(8,128)(2,1)S(1)}, bf16[1728,128]{1,0:T(8,128)(2,1)S(1)}, u32[]{:S(2)}, u32[]{:S(2)}) collective-permute-start(bf16[1728,128]{1,0:T(8,128)(2,1)S(1)} %bitcast.194), channel_id=1, source_target_pairs={{0,96},{1,97},{2,98},{3,99},{4,100},{5,101},{6,102},{7,103},{8,104... | collective-permute-start | bytes 1327112 | tf_op jit(solution)/shard_map/first/ppermute | solution.py:34
  7.3 5.4 %collective-permute-start.6 = (bf16[3,3,192,128]{3,2,1,0:T(8,128)(2,1)S(1)}, bf16[3,3,192,128]{3,2,1,0:T(8,128)(2,1)S(1)}, u32[]{:S(2)}, u32[]{:S(2)}) collective-permute-start(bf16[3,3,192,128]{3,2,1,0:T(8,128)(2,1)S(1)} %get-tuple-element.42), channel_id=1, source_target_pairs={{0,23},{1,22},{2,21},{3,20},{4,19},{5,18},{6,17},{7,16},{8,31},{9,... | collective-permute-start | bytes 1327112 | tf_op jit(solution)/shard_map/rows/ppermute | solution.py:34
  12.7 2.8 %collective-permute-done = bf16[3,3,192,128]{3,2,1,0:T(8,128)(2,1)S(1)} collective-permute-done((bf16[3,3,192,128]{3,2,1,0:T(8,128)(2,1)S(1)}, bf16[3,3,192,128]{3,2,1,0:T(8,128)(2,1)S(1)}, u32[]{:S(2)}, u32[]{:S(2)}) %collective-permute-start) | collective-permute-done | bytes 442400 | tf_op jit(solution)/shard_map/rows/ppermute | solution.py:34
  15.8 2.8 %collective-permute-start.2 = (bf16[1728,128]{1,0:T(8,128)(2,1)S(1)}, bf16[1728,128]{1,0:T(8,128)(2,1)S(1)}, u32[]{:S(2)}, u32[]{:S(2)}) collective-permute-start(bf16[1728,128]{1,0:T(8,128)(2,1)S(1)} %bitcast.202), channel_id=1, source_target_pairs={{0,96},{1,97},{2,98},{3,99},{4,100},{5,101},{6,102},{7,103},{8,104... | collective-permute-start | bytes 1327112 | tf_op jit(solution)/shard_map/first/ppermute | solution.py:34
  19.3 12.5 %collective-permute-done.6 = bf16[3,3,192,128]{3,2,1,0:T(8,128)(2,1)S(1)} collective-permute-done((bf16[3,3,192,128]{3,2,1,0:T(8,128)(2,1)S(1)}, bf16[3,3,192,128]{3,2,1,0:T(8,128)(2,1)S(1)}, u32[]{:S(2)}, u32[]{:S(2)}) %collective-permute-start.6) | collective-permute-done | bytes 442400 | tf_op jit(solution)/shard_map/rows/ppermute | solution.py:34
  32.1 5.2 %collective-permute-done.5 = bf16[3,3,192,128]{3,2,1,0:T(8,128)(2,1)S(1)} collective-permute-done((bf16[3,3,192,128]{3,2,1,0:T(8,128)(2,1)S(1)}, bf16[3,3,192,128]{3,2,1,0:T(8,128)(2,1)S(1)}, u32[]{:S(2)}, u32[]{:S(2)}) %collective-permute-start.5) | collective-permute-done | bytes 442400 | tf_op jit(solution)/shard_map/rows/ppermute | solution.py:34
  39.3 2.5 %collective-permute-start.17 = (bf16[3456,128]{1,0:T(8,128)(2,1)S(1)}, bf16[3456,128]{1,0:T(8,128)(2,1)S(1)}, u32[]{:S(2)}, u32[]{:S(2)}) collective-permute-start(bf16[3456,128]{1,0:T(8,128)(2,1)S(1)} %pad_maximum_fusion), channel_id=1, source_target_pairs={{0,96},{1,97},{2,98},{3,99},{4,100},{5,101},{6,102},{7,103},{8,104... | collective-permute-start | bytes 2654216 | tf_op jit(solution)/shard_map/second/ppermute | solution.py:34
  48.2 2.5 %collective-permute-start.14 = (f32[2,128,256]{2,1,0:T(8,128)S(1)}, f32[2,128,256]{2,1,0:T(8,128)S(1)}, u32[]{:S(2)}, u32[]{:S(2)}) collective-permute-start(f32[2,128,256]{2,1,0:T(8,128)S(1)} %get-tuple-element.53), channel_id=1, source_target_pairs={{0,17},{1,0},{2,19},{3,2},{4,21},{5,4},{6,23},{7,6},{8,25},{9,8},{... | collective-permute-start | bytes 786440 | tf_op jit(solution)/shard_map/same/ppermute | solution.py:34
  51.9 5.3 %collective-permute-done.15 = f32[2,128,256]{2,1,0:T(8,128)S(1)} collective-permute-done((f32[2,128,256]{2,1,0:T(8,128)S(1)}, f32[2,128,256]{2,1,0:T(8,128)S(1)}, u32[]{:S(2)}, u32[]{:S(2)}) %collective-permute-start.15) | collective-permute-done | bytes 262176 | tf_op jit(solution)/shard_map/same/ppermute | solution.py:34
  57.2 2.1 %collective-permute-start.10 = (bf16[1728,128]{1,0:T(8,128)(2,1)S(1)}, bf16[1728,128]{1,0:T(8,128)(2,1)S(1)}, u32[]{:S(2)}, u32[]{:S(2)}) collective-permute-start(bf16[1728,128]{1,0:T(8,128)(2,1)S(1)} %copy-done.1), channel_id=1, source_target_pairs={{0,8},{1,9},{2,10},{3,11},{4,12},{5,13},{6,14},{7,15},{8,0},{9,1},... | collective-permute-start | bytes 1327112 | tf_op jit(solution)/shard_map/second/ppermute | solution.py:34
  60.2 1.3 %collective-permute-start.11 = (bf16[1728,128]{1,0:T(8,128)(2,1)S(1)}, bf16[1728,128]{1,0:T(8,128)(2,1)S(1)}, u32[]{:S(2)}, u32[]{:S(2)}) collective-permute-start(bf16[1728,128]{1,0:T(8,128)(2,1)S(1)} %copy-done.3), channel_id=1, source_target_pairs={{0,8},{1,9},{2,10},{3,11},{4,12},{5,13},{6,14},{7,15},{8,0},{9,1},... | collective-permute-start | bytes 1327112 | tf_op jit(solution)/shard_map/second/ppermute | solution.py:34
  61.5 2.0 %collective-permute-done.13 = f32[2,128,256]{2,1,0:T(8,128)S(1)} collective-permute-done((f32[2,128,256]{2,1,0:T(8,128)S(1)}, f32[2,128,256]{2,1,0:T(8,128)S(1)}, u32[]{:S(2)}, u32[]{:S(2)}) %collective-permute-start.13) | collective-permute-done | bytes 262176 | tf_op jit(solution)/shard_map/same/ppermute | solution.py:34
  65.0 1.4 %collective-permute-start.23 = (f32[2,128,256]{2,1,0:T(8,128)S(1)}, f32[2,128,256]{2,1,0:T(8,128)S(1)}, u32[]{:S(2)}, u32[]{:S(2)}) collective-permute-start(f32[2,128,256]{2,1,0:T(8,128)S(1)} %get-tuple-element.51), channel_id=1, source_target_pairs={{0,16},{1,17},{2,18},{3,19},{4,20},{5,21},{6,22},{7,23},{8,24},{9,... | collective-permute-start | bytes 786440 | tf_op jit(solution)/shard_map/beside/ppermute | solution.py:34
  66.3 1.3 %collective-permute-start.22 = (f32[2,128,256]{2,1,0:T(8,128)S(1)}, f32[2,128,256]{2,1,0:T(8,128)S(1)}, u32[]{:S(2)}, u32[]{:S(2)}) collective-permute-start(f32[2,128,256]{2,1,0:T(8,128)S(1)} %get-tuple-element.50), channel_id=1, source_target_pairs={{0,17},{1,0},{2,19},{3,2},{4,21},{5,4},{6,23},{7,6},{8,25},{9,8},{... | collective-permute-start | bytes 786440 | tf_op jit(solution)/shard_map/beside/ppermute | solution.py:34
  75.4 2.1 %collective-permute-done.22 = f32[2,128,256]{2,1,0:T(8,128)S(1)} collective-permute-done((f32[2,128,256]{2,1,0:T(8,128)S(1)}, f32[2,128,256]{2,1,0:T(8,128)S(1)}, u32[]{:S(2)}, u32[]{:S(2)}) %collective-permute-start.22) | collective-permute-done | bytes 262176 | tf_op jit(solution)/shard_map/beside/ppermute | solution.py:34
  77.5 2.9 %collective-permute-done.21 = f32[2,128,256]{2,1,0:T(8,128)S(1)} collective-permute-done((f32[2,128,256]{2,1,0:T(8,128)S(1)}, f32[2,128,256]{2,1,0:T(8,128)S(1)}, u32[]{:S(2)}, u32[]{:S(2)}) %collective-permute-start.21) | collective-permute-done | bytes 262176 | tf_op jit(solution)/shard_map/beside/ppermute | solution.py:34
  80.9 11.7 %collective-permute-start.24 = (f32[2,128,256]{2,1,0:T(8,128)S(1)}, f32[2,128,256]{2,1,0:T(8,128)S(1)}, u32[]{:S(2)}, u32[]{:S(2)}) collective-permute-start(f32[2,128,256]{2,1,0:T(8,128)S(1)} %get-tuple-element.70), channel_id=1, source_target_pairs={{0,32},{1,48},{2,98},{3,99},{4,2},{5,18},{6,0},{7,1},{8,40},{9,56}... | collective-permute-start | bytes 786440 | tf_op jit(solution)/shard_map/over_y/ppermute | solution.py:34
  92.6 3.2 %collective-permute-start.25 = (f32[2,128,256]{2,1,0:T(8,128)S(1)}, f32[2,128,256]{2,1,0:T(8,128)S(1)}, u32[]{:S(2)}, u32[]{:S(2)}) collective-permute-start(f32[2,128,256]{2,1,0:T(8,128)S(1)} %get-tuple-element.40), channel_id=1, source_target_pairs={{0,98},{1,114},{2,0},{3,1},{4,32},{5,33},{6,2},{7,18},{8,106},{9,1... | collective-permute-start | bytes 786440 | tf_op jit(solution)/shard_map/over_y/ppermute | solution.py:34
  95.8 1.3 %collective-permute-start.27 = (f32[2,128,256]{2,1,0:T(8,128)S(1)}, f32[2,128,256]{2,1,0:T(8,128)S(1)}, u32[]{:S(2)}, u32[]{:S(2)}) collective-permute-start(f32[2,128,256]{2,1,0:T(8,128)S(1)} %get-tuple-element.72), channel_id=1, source_target_pairs={{0,38},{1,39},{2,32},{3,48},{8,46},{9,47},{10,40},{11,56},{16,54},... | collective-permute-start | bytes 786440 | tf_op jit(solution)/shard_map/over_y/ppermute | solution.py:34
  97.1 6.7 %collective-permute-done.24 = f32[2,128,256]{2,1,0:T(8,128)S(1)} collective-permute-done((f32[2,128,256]{2,1,0:T(8,128)S(1)}, f32[2,128,256]{2,1,0:T(8,128)S(1)}, u32[]{:S(2)}, u32[]{:S(2)}) %collective-permute-start.24) | collective-permute-done | bytes 262176 | tf_op jit(solution)/shard_map/over_y/ppermute | solution.py:34
  103.8 4.1 %collective-permute-done.27 = f32[2,128,256]{2,1,0:T(8,128)S(1)} collective-permute-done((f32[2,128,256]{2,1,0:T(8,128)S(1)}, f32[2,128,256]{2,1,0:T(8,128)S(1)}, u32[]{:S(2)}, u32[]{:S(2)}) %collective-permute-start.27) | collective-permute-done | bytes 262176 | tf_op jit(solution)/shard_map/over_y/ppermute | solution.py:34
  108.3 2.8 %collective-permute-start.28 = (f32[128,256]{1,0:T(8,128)S(1)}, f32[128,256]{1,0:T(8,128)S(1)}, u32[]{:S(2)}, u32[]{:S(2)}) collective-permute-start(f32[128,256]{1,0:T(8,128)S(1)} %get-tuple-element.67), channel_id=1, source_target_pairs={{0,8},{1,9},{2,10},{3,11},{4,12},{5,13},{6,14},{7,15},{8,0},{9,1},... | collective-permute-start | bytes 393224 | tf_op jit(solution)/shard_map/place/ppermute | solution.py:34
  (99 shorter events, 24.4 us)
Async XLA Ops:
  2.3 13.2 %collective-permute-start = (bf16[3,3,192,128]{3,2,1,0:T(8,128)(2,1)S(1)}, bf16[3,3,192,128]{3,2,1,0:T(8,128)(2,1)S(1)}, u32[]{:S(2)}, u32[]{:S(2)}) collective-permute-start(bf16[3,3,192,128]{3,2,1,0:T(8,128)(2,1)S(1)} %get-tuple-element.43), channel_id=1, source_target_pairs={{0,7},{1,6},{2,5},{3,4},{4,3},{5,2},{6,1},{7,0},{8,15},{9,14},{10,... | collective-permute-start | bytes 1327112 | tf_op jit(solution)/shard_map/rows/ppermute | solution.py:34
  4.1 11.7 %collective-permute-start.1 = (bf16[1728,128]{1,0:T(8,128)(2,1)S(1)}, bf16[1728,128]{1,0:T(8,128)(2,1)S(1)}, u32[]{:S(2)}, u32[]{:S(2)}) collective-permute-start(bf16[1728,128]{1,0:T(8,128)(2,1)S(1)} %bitcast.194), channel_id=1, source_target_pairs={{0,96},{1,97},{2,98},{3,99},{4,100},{5,101},{6,102},{7,103},{8,104... | collective-permute-start | bytes 1327112 | tf_op jit(solution)/shard_map/first/ppermute | solution.py:34
  6.7 11.9 %collective-permute-start.3 = (bf16[1728,128]{1,0:T(8,128)(2,1)S(1)}, bf16[1728,128]{1,0:T(8,128)(2,1)S(1)}, u32[]{:S(2)}, u32[]{:S(2)}) collective-permute-start(bf16[1728,128]{1,0:T(8,128)(2,1)S(1)} %bitcast.195), channel_id=1, source_target_pairs={{2,34},{3,35},{4,36},{5,37},{10,42},{11,43},{12,44},{13,45},{18,50... | collective-permute-start | bytes 1327112 | tf_op jit(solution)/shard_map/first/ppermute | solution.py:34
  7.3 24.5 %collective-permute-start.6 = (bf16[3,3,192,128]{3,2,1,0:T(8,128)(2,1)S(1)}, bf16[3,3,192,128]{3,2,1,0:T(8,128)(2,1)S(1)}, u32[]{:S(2)}, u32[]{:S(2)}) collective-permute-start(bf16[3,3,192,128]{3,2,1,0:T(8,128)(2,1)S(1)} %get-tuple-element.42), channel_id=1, source_target_pairs={{0,23},{1,22},{2,21},{3,20},{4,19},{5,18},{6,17},{7,16},{8,31},{9,... | collective-permute-start | bytes 1327112 | tf_op jit(solution)/shard_map/rows/ppermute | solution.py:34
  12.7 24.5 %collective-permute-start.5 = (bf16[3,3,192,128]{3,2,1,0:T(8,128)(2,1)S(1)}, bf16[3,3,192,128]{3,2,1,0:T(8,128)(2,1)S(1)}, u32[]{:S(2)}, u32[]{:S(2)}) collective-permute-start(bf16[3,3,192,128]{3,2,1,0:T(8,128)(2,1)S(1)} %get-tuple-element.45), channel_id=1, source_target_pairs={{0,16},{1,17},{2,18},{3,19},{4,20},{5,21},{6,22},{7,23},{8,24},{9,... | collective-permute-start | bytes 1327112 | tf_op jit(solution)/shard_map/rows/ppermute | solution.py:34
  15.8 22.1 %collective-permute-start.2 = (bf16[1728,128]{1,0:T(8,128)(2,1)S(1)}, bf16[1728,128]{1,0:T(8,128)(2,1)S(1)}, u32[]{:S(2)}, u32[]{:S(2)}) collective-permute-start(bf16[1728,128]{1,0:T(8,128)(2,1)S(1)} %bitcast.202), channel_id=1, source_target_pairs={{0,96},{1,97},{2,98},{3,99},{4,100},{5,101},{6,102},{7,103},{8,104... | collective-permute-start | bytes 1327112 | tf_op jit(solution)/shard_map/first/ppermute | solution.py:34
  18.6 19.4 %collective-permute-start.4 = (bf16[1728,128]{1,0:T(8,128)(2,1)S(1)}, bf16[1728,128]{1,0:T(8,128)(2,1)S(1)}, u32[]{:S(2)}, u32[]{:S(2)}) collective-permute-start(bf16[1728,128]{1,0:T(8,128)(2,1)S(1)} %bitcast.203), channel_id=1, source_target_pairs={{2,34},{3,35},{4,36},{5,37},{10,42},{11,43},{12,44},{13,45},{18,50... | collective-permute-start | bytes 1327112 | tf_op jit(solution)/shard_map/first/ppermute | solution.py:34
  39.3 24.3 %collective-permute-start.17 = (bf16[3456,128]{1,0:T(8,128)(2,1)S(1)}, bf16[3456,128]{1,0:T(8,128)(2,1)S(1)}, u32[]{:S(2)}, u32[]{:S(2)}) collective-permute-start(bf16[3456,128]{1,0:T(8,128)(2,1)S(1)} %pad_maximum_fusion), channel_id=1, source_target_pairs={{0,96},{1,97},{2,98},{3,99},{4,100},{5,101},{6,102},{7,103},{8,104... | collective-permute-start | bytes 2654216 | tf_op jit(solution)/shard_map/second/ppermute | solution.py:34
  41.7 25.9 %collective-permute-start.12 = (bf16[3456,128]{1,0:T(8,128)(2,1)S(1)}, bf16[3456,128]{1,0:T(8,128)(2,1)S(1)}, u32[]{:S(2)}, u32[]{:S(2)}) collective-permute-start(bf16[3456,128]{1,0:T(8,128)(2,1)S(1)} %pad_maximum_fusion), channel_id=1, source_target_pairs={{2,34},{3,35},{4,36},{5,37},{10,42},{11,43},{12,44},{13,45},{18,50... | collective-permute-start | bytes 2654216 | tf_op jit(solution)/shard_map/second/ppermute | solution.py:34
  48.1 9.1 %collective-permute-start.15 = (f32[2,128,256]{2,1,0:T(8,128)S(1)}, f32[2,128,256]{2,1,0:T(8,128)S(1)}, u32[]{:S(2)}, u32[]{:S(2)}) collective-permute-start(f32[2,128,256]{2,1,0:T(8,128)S(1)} %get-tuple-element.54), channel_id=1, source_target_pairs={{0,16},{1,17},{2,18},{3,19},{4,20},{5,21},{6,22},{7,23},{8,24},{9,... | collective-permute-start | bytes 786440 | tf_op jit(solution)/shard_map/same/ppermute | solution.py:34
  48.2 12.0 %collective-permute-start.14 = (f32[2,128,256]{2,1,0:T(8,128)S(1)}, f32[2,128,256]{2,1,0:T(8,128)S(1)}, u32[]{:S(2)}, u32[]{:S(2)}) collective-permute-start(f32[2,128,256]{2,1,0:T(8,128)S(1)} %get-tuple-element.53), channel_id=1, source_target_pairs={{0,17},{1,0},{2,19},{3,2},{4,21},{5,4},{6,23},{7,6},{8,25},{9,8},{... | collective-permute-start | bytes 786440 | tf_op jit(solution)/shard_map/same/ppermute | solution.py:34
  50.7 12.8 %collective-permute-start.13 = (f32[2,128,256]{2,1,0:T(8,128)S(1)}, f32[2,128,256]{2,1,0:T(8,128)S(1)}, u32[]{:S(2)}, u32[]{:S(2)}) collective-permute-start(f32[2,128,256]{2,1,0:T(8,128)S(1)} %get-tuple-element.52), channel_id=1, source_target_pairs={{0,1},{1,16},{2,3},{3,18},{4,5},{5,20},{6,7},{7,22},{8,9},{9,24},{... | collective-permute-start | bytes 786440 | tf_op jit(solution)/shard_map/same/ppermute | solution.py:34
  57.2 10.6 %collective-permute-start.10 = (bf16[1728,128]{1,0:T(8,128)(2,1)S(1)}, bf16[1728,128]{1,0:T(8,128)(2,1)S(1)}, u32[]{:S(2)}, u32[]{:S(2)}) collective-permute-start(bf16[1728,128]{1,0:T(8,128)(2,1)S(1)} %copy-done.1), channel_id=1, source_target_pairs={{0,8},{1,9},{2,10},{3,11},{4,12},{5,13},{6,14},{7,15},{8,0},{9,1},... | collective-permute-start | bytes 1327112 | tf_op jit(solution)/shard_map/second/ppermute | solution.py:34
  60.2 8.5 %collective-permute-start.11 = (bf16[1728,128]{1,0:T(8,128)(2,1)S(1)}, bf16[1728,128]{1,0:T(8,128)(2,1)S(1)}, u32[]{:S(2)}, u32[]{:S(2)}) collective-permute-start(bf16[1728,128]{1,0:T(8,128)(2,1)S(1)} %copy-done.3), channel_id=1, source_target_pairs={{0,8},{1,9},{2,10},{3,11},{4,12},{5,13},{6,14},{7,15},{8,0},{9,1},... | collective-permute-start | bytes 1327112 | tf_op jit(solution)/shard_map/second/ppermute | solution.py:34
  65.0 9.8 %collective-permute-start.23 = (f32[2,128,256]{2,1,0:T(8,128)S(1)}, f32[2,128,256]{2,1,0:T(8,128)S(1)}, u32[]{:S(2)}, u32[]{:S(2)}) collective-permute-start(f32[2,128,256]{2,1,0:T(8,128)S(1)} %get-tuple-element.51), channel_id=1, source_target_pairs={{0,16},{1,17},{2,18},{3,19},{4,20},{5,21},{6,22},{7,23},{8,24},{9,... | collective-permute-start | bytes 786440 | tf_op jit(solution)/shard_map/beside/ppermute | solution.py:34
  66.3 11.2 %collective-permute-start.22 = (f32[2,128,256]{2,1,0:T(8,128)S(1)}, f32[2,128,256]{2,1,0:T(8,128)S(1)}, u32[]{:S(2)}, u32[]{:S(2)}) collective-permute-start(f32[2,128,256]{2,1,0:T(8,128)S(1)} %get-tuple-element.50), channel_id=1, source_target_pairs={{0,17},{1,0},{2,19},{3,2},{4,21},{5,4},{6,23},{7,6},{8,25},{9,8},{... | collective-permute-start | bytes 786440 | tf_op jit(solution)/shard_map/beside/ppermute | solution.py:34
  67.6 12.8 %collective-permute-start.21 = (f32[2,128,256]{2,1,0:T(8,128)S(1)}, f32[2,128,256]{2,1,0:T(8,128)S(1)}, u32[]{:S(2)}, u32[]{:S(2)}) collective-permute-start(f32[2,128,256]{2,1,0:T(8,128)S(1)} %get-tuple-element.49), channel_id=1, source_target_pairs={{0,1},{1,16},{2,3},{3,18},{4,5},{5,20},{6,7},{7,22},{8,9},{9,24},{... | collective-permute-start | bytes 786440 | tf_op jit(solution)/shard_map/beside/ppermute | solution.py:34
  73.4 7.2 %collective-permute-start.20 = (f32[2,128,256]{2,1,0:T(8,128)S(1)}, f32[2,128,256]{2,1,0:T(8,128)S(1)}, u32[]{:S(2)}, u32[]{:S(2)}) collective-permute-start(f32[2,128,256]{2,1,0:T(8,128)S(1)} %get-tuple-element.48), channel_id=1, source_target_pairs={{0,16},{1,17},{2,18},{3,19},{8,24},{9,25},{10,26},{11,27},{16,0},{... | collective-permute-start | bytes 786440 | tf_op jit(solution)/shard_map/around/ppermute | solution.py:34
  74.1 6.5 %collective-permute-start.19 = (f32[2,128,256]{2,1,0:T(8,128)S(1)}, f32[2,128,256]{2,1,0:T(8,128)S(1)}, u32[]{:S(2)}, u32[]{:S(2)}) collective-permute-start(f32[2,128,256]{2,1,0:T(8,128)S(1)} %get-tuple-element.47), channel_id=1, source_target_pairs={{0,17},{1,0},{2,19},{3,2},{8,25},{9,8},{10,27},{11,10},{16,1},{17,... | collective-permute-start | bytes 786440 | tf_op jit(solution)/shard_map/around/ppermute | solution.py:34
  74.7 5.8 %collective-permute-start.18 = (f32[2,128,256]{2,1,0:T(8,128)S(1)}, f32[2,128,256]{2,1,0:T(8,128)S(1)}, u32[]{:S(2)}, u32[]{:S(2)}) collective-permute-start(f32[2,128,256]{2,1,0:T(8,128)S(1)} %get-tuple-element.46), channel_id=1, source_target_pairs={{0,1},{1,16},{2,3},{3,18},{8,9},{9,24},{10,11},{11,26},{16,17},{17... | collective-permute-start | bytes 786440 | tf_op jit(solution)/shard_map/around/ppermute | solution.py:34
  80.8 16.3 %collective-permute-start.26 = (f32[2,128,256]{2,1,0:T(8,128)S(1)}, f32[2,128,256]{2,1,0:T(8,128)S(1)}, u32[]{:S(2)}, u32[]{:S(2)}) collective-permute-start(f32[2,128,256]{2,1,0:T(8,128)S(1)} %get-tuple-element.71), channel_id=1, source_target_pairs={{0,2},{1,3},{2,38},{3,54},{4,0},{5,1},{6,32},{7,33},{8,10},{9,11},... | collective-permute-start | bytes 786440 | tf_op jit(solution)/shard_map/over_y/ppermute | solution.py:34
  80.9 22.9 %collective-permute-start.24 = (f32[2,128,256]{2,1,0:T(8,128)S(1)}, f32[2,128,256]{2,1,0:T(8,128)S(1)}, u32[]{:S(2)}, u32[]{:S(2)}) collective-permute-start(f32[2,128,256]{2,1,0:T(8,128)S(1)} %get-tuple-element.70), channel_id=1, source_target_pairs={{0,32},{1,48},{2,98},{3,99},{4,2},{5,18},{6,0},{7,1},{8,40},{9,56}... | collective-permute-start | bytes 786440 | tf_op jit(solution)/shard_map/over_y/ppermute | solution.py:34
  92.6 11.2 %collective-permute-start.25 = (f32[2,128,256]{2,1,0:T(8,128)S(1)}, f32[2,128,256]{2,1,0:T(8,128)S(1)}, u32[]{:S(2)}, u32[]{:S(2)}) collective-permute-start(f32[2,128,256]{2,1,0:T(8,128)S(1)} %get-tuple-element.40), channel_id=1, source_target_pairs={{0,98},{1,114},{2,0},{3,1},{4,32},{5,33},{6,2},{7,18},{8,106},{9,1... | collective-permute-start | bytes 786440 | tf_op jit(solution)/shard_map/over_y/ppermute | solution.py:34
  95.8 12.1 %collective-permute-start.27 = (f32[2,128,256]{2,1,0:T(8,128)S(1)}, f32[2,128,256]{2,1,0:T(8,128)S(1)}, u32[]{:S(2)}, u32[]{:S(2)}) collective-permute-start(f32[2,128,256]{2,1,0:T(8,128)S(1)} %get-tuple-element.72), channel_id=1, source_target_pairs={{0,38},{1,39},{2,32},{3,48},{8,46},{9,47},{10,40},{11,56},{16,54},... | collective-permute-start | bytes 786440 | tf_op jit(solution)/shard_map/over_y/ppermute | solution.py:34
  (14 other events, 99.8 us)

commit v6 on v5

--- a/solution.py
+++ b/solution.py
@@ -113,6 +113,14 @@
         )
         return inner(lhs, right).reshape(2, 2, own, 2 * own)
 
+    def both_products(lhs, first, second):
+        (s, t), (u, v) = first, second
+        right = jnp.concatenate(
+            [jnp.concatenate([s, t, u, v], axis=1), jnp.concatenate([t, s, v, u], axis=1)], axis=0
+        )
+        out = inner(lhs, right)
+        return [out[:, q * 2 * own:(q + 1) * 2 * own].reshape(2, 2, own, 2 * own) for q in range(2)]
+
     d = (y - x) % 4
 
     def over_z(first, second, behind, active=lambda *at: True, swaps=()):
@@ -142,8 +150,7 @@
         q2 = send(p2, across)
         previous = columns("previous", (p0, p1, p2), (q0, q1, q2))
         around = over_z(
-            products(previous, n0, n1),
-            products(previous, n2[:count], n2[count:]),
+            *both_products(previous, (n0, n1), (n2[:count], n2[count:])),
             [],
             lambda x, h, c, y, l: (y - x) % 4 < 2,
             SWAPS[2],

time: 114 us -> 114 us (level)
    dot_general x6 -> x5, matrix products: 6.95 us -> 6.74 us  [inner(): lax.dot_general(left, right, (((0,), (0,)), ((), ())), preferred_element_...]
where the time goes in v6:
time: 114 us; the launch traced here: 113 us
  starting transfers between devices  48.4 us (42%)
  waiting for transfers between devices  46.6 us (41%)
  local copies, waits for them, and re-layouts  7.32 us (6%)
  matrix products  7.32 us (6%)
  other arithmetic  1.77 us (2%)
  between operations  1.25 us (1%)
    ppermute x29, starting transfers between devices, send(): return lax.ppermute(value, AXES, pairs)  48.4 us
    ppermute x29, waiting for transfers between devices, send(): return lax.ppermute(value, AXES, pairs)  46.6 us
    dot_general x5, matrix products, inner(): lax.dot_general(left, right, (((0,), (0,)), ((), ())), preferred_element_...  6.74 us
  transfers between devices with their start and end apart: 29, of which 12 were waited for; matrix products, arithmetic and copies ran while one was open for 11% of the time, Pallas kernels for 0%

profile of v6, /device:TPU:25, one launch (start us, length us, event | category | flops | bytes accessed | tf_op | source)
XLA Modules:
  0.0 112.7 jit_solution(337291940133856719)
XLA Ops:
  0.7 1.5 %constant_dynamic-slice_fusion = (bf16[3,3,192,128]{3,2,1,0:T(8,128)(2,1)S(1)}, bf16[3,3,192,128]{3,2,1,0:T(8,128)(2,1)S(1)}, bf16[3,3,192,128]{3,2,1,0:T(8,128)(2,1)S(1)}, bf16[3,3,192,128]{3,2,1,0:T(8,128)(2,1)S(1)}) fusion(bf16[3,12,192,128]{3,2,1,0:T(8,128)(2,1)} %param.2, s32[]{:T(128)S(6)} %select_n.507, s32[]{:T(128)S(6)} %select_n.505, ...), kind=kLoop, calls=%fused_computation.126 | loop fusion | bytes 3538960 | tf_op jit(solution)/shard_map/rows/dynamic_slice | solution.py:65
  2.3 1.4 %collective-permute-start = (bf16[3,3,192,128]{3,2,1,0:T(8,128)(2,1)S(1)}, bf16[3,3,192,128]{3,2,1,0:T(8,128)(2,1)S(1)}, u32[]{:S(2)}, u32[]{:S(2)}) collective-permute-start(bf16[3,3,192,128]{3,2,1,0:T(8,128)(2,1)S(1)} %get-tuple-element.43), channel_id=1, source_target_pairs={{0,7},{1,6},{2,5},{3,4},{4,3},{5,2},{6,1},{7,0},{8,15},{9,14},{10,... | collective-permute-start | bytes 1327112 | tf_op jit(solution)/shard_map/rows/ppermute | solution.py:34
  4.1 2.5 %collective-permute-start.1 = (bf16[1728,128]{1,0:T(8,128)(2,1)S(1)}, bf16[1728,128]{1,0:T(8,128)(2,1)S(1)}, u32[]{:S(2)}, u32[]{:S(2)}) collective-permute-start(bf16[1728,128]{1,0:T(8,128)(2,1)S(1)} %bitcast.193), channel_id=1, source_target_pairs={{0,96},{1,97},{2,98},{3,99},{4,100},{5,101},{6,102},{7,103},{8,104... | collective-permute-start | bytes 1327112 | tf_op jit(solution)/shard_map/first/ppermute | solution.py:34
  7.3 5.4 %collective-permute-start.6 = (bf16[3,3,192,128]{3,2,1,0:T(8,128)(2,1)S(1)}, bf16[3,3,192,128]{3,2,1,0:T(8,128)(2,1)S(1)}, u32[]{:S(2)}, u32[]{:S(2)}) collective-permute-start(bf16[3,3,192,128]{3,2,1,0:T(8,128)(2,1)S(1)} %get-tuple-element.42), channel_id=1, source_target_pairs={{0,23},{1,22},{2,21},{3,20},{4,19},{5,18},{6,17},{7,16},{8,31},{9,... | collective-permute-start | bytes 1327112 | tf_op jit(solution)/shard_map/rows/ppermute | solution.py:34
  12.7 2.8 %collective-permute-done = bf16[3,3,192,128]{3,2,1,0:T(8,128)(2,1)S(1)} collective-permute-done((bf16[3,3,192,128]{3,2,1,0:T(8,128)(2,1)S(1)}, bf16[3,3,192,128]{3,2,1,0:T(8,128)(2,1)S(1)}, u32[]{:S(2)}, u32[]{:S(2)}) %collective-permute-start) | collective-permute-done | bytes 442400 | tf_op jit(solution)/shard_map/rows/ppermute | solution.py:34
  15.8 2.8 %collective-permute-start.2 = (bf16[1728,128]{1,0:T(8,128)(2,1)S(1)}, bf16[1728,128]{1,0:T(8,128)(2,1)S(1)}, u32[]{:S(2)}, u32[]{:S(2)}) collective-permute-start(bf16[1728,128]{1,0:T(8,128)(2,1)S(1)} %bitcast.201), channel_id=1, source_target_pairs={{0,96},{1,97},{2,98},{3,99},{4,100},{5,101},{6,102},{7,103},{8,104... | collective-permute-start | bytes 1327112 | tf_op jit(solution)/shard_map/first/ppermute | solution.py:34
  19.3 12.5 %collective-permute-done.6 = bf16[3,3,192,128]{3,2,1,0:T(8,128)(2,1)S(1)} collective-permute-done((bf16[3,3,192,128]{3,2,1,0:T(8,128)(2,1)S(1)}, bf16[3,3,192,128]{3,2,1,0:T(8,128)(2,1)S(1)}, u32[]{:S(2)}, u32[]{:S(2)}) %collective-permute-start.6) | collective-permute-done | bytes 442400 | tf_op jit(solution)/shard_map/rows/ppermute | solution.py:34
  32.1 5.2 %collective-permute-done.5 = bf16[3,3,192,128]{3,2,1,0:T(8,128)(2,1)S(1)} collective-permute-done((bf16[3,3,192,128]{3,2,1,0:T(8,128)(2,1)S(1)}, bf16[3,3,192,128]{3,2,1,0:T(8,128)(2,1)S(1)}, u32[]{:S(2)}, u32[]{:S(2)}) %collective-permute-start.5) | collective-permute-done | bytes 442400 | tf_op jit(solution)/shard_map/rows/ppermute | solution.py:34
  39.3 2.5 %collective-permute-start.17 = (bf16[3456,128]{1,0:T(8,128)(2,1)S(1)}, bf16[3456,128]{1,0:T(8,128)(2,1)S(1)}, u32[]{:S(2)}, u32[]{:S(2)}) collective-permute-start(bf16[3456,128]{1,0:T(8,128)(2,1)S(1)} %pad_maximum_fusion), channel_id=1, source_target_pairs={{0,96},{1,97},{2,98},{3,99},{4,100},{5,101},{6,102},{7,103},{8,104... | collective-permute-start | bytes 2654216 | tf_op jit(solution)/shard_map/second/ppermute | solution.py:34
  48.2 2.5 %collective-permute-start.14 = (f32[2,128,256]{2,1,0:T(8,128)S(1)}, f32[2,128,256]{2,1,0:T(8,128)S(1)}, u32[]{:S(2)}, u32[]{:S(2)}) collective-permute-start(f32[2,128,256]{2,1,0:T(8,128)S(1)} %get-tuple-element.55), channel_id=1, source_target_pairs={{0,17},{1,0},{2,19},{3,2},{4,21},{5,4},{6,23},{7,6},{8,25},{9,8},{... | collective-permute-start | bytes 786440 | tf_op jit(solution)/shard_map/same/ppermute | solution.py:34
  51.9 5.3 %collective-permute-done.15 = f32[2,128,256]{2,1,0:T(8,128)S(1)} collective-permute-done((f32[2,128,256]{2,1,0:T(8,128)S(1)}, f32[2,128,256]{2,1,0:T(8,128)S(1)}, u32[]{:S(2)}, u32[]{:S(2)}) %collective-permute-start.15) | collective-permute-done | bytes 262176 | tf_op jit(solution)/shard_map/same/ppermute | solution.py:34
  57.2 2.1 %collective-permute-start.10 = (bf16[1728,128]{1,0:T(8,128)(2,1)S(1)}, bf16[1728,128]{1,0:T(8,128)(2,1)S(1)}, u32[]{:S(2)}, u32[]{:S(2)}) collective-permute-start(bf16[1728,128]{1,0:T(8,128)(2,1)S(1)} %copy-done.1), channel_id=1, source_target_pairs={{0,8},{1,9},{2,10},{3,11},{4,12},{5,13},{6,14},{7,15},{8,0},{9,1},... | collective-permute-start | bytes 1327112 | tf_op jit(solution)/shard_map/second/ppermute | solution.py:34
  61.5 2.0 %collective-permute-done.13 = f32[2,128,256]{2,1,0:T(8,128)S(1)} collective-permute-done((f32[2,128,256]{2,1,0:T(8,128)S(1)}, f32[2,128,256]{2,1,0:T(8,128)S(1)}, u32[]{:S(2)}, u32[]{:S(2)}) %collective-permute-start.13) | collective-permute-done | bytes 262176 | tf_op jit(solution)/shard_map/same/ppermute | solution.py:34
  65.0 1.4 %collective-permute-start.23 = (f32[2,128,256]{2,1,0:T(8,128)S(1)}, f32[2,128,256]{2,1,0:T(8,128)S(1)}, u32[]{:S(2)}, u32[]{:S(2)}) collective-permute-start(f32[2,128,256]{2,1,0:T(8,128)S(1)} %get-tuple-element.53), channel_id=1, source_target_pairs={{0,16},{1,17},{2,18},{3,19},{4,20},{5,21},{6,22},{7,23},{8,24},{9,... | collective-permute-start | bytes 786440 | tf_op jit(solution)/shard_map/beside/ppermute | solution.py:34
  66.3 1.3 %collective-permute-start.22 = (f32[2,128,256]{2,1,0:T(8,128)S(1)}, f32[2,128,256]{2,1,0:T(8,128)S(1)}, u32[]{:S(2)}, u32[]{:S(2)}) collective-permute-start(f32[2,128,256]{2,1,0:T(8,128)S(1)} %get-tuple-element.52), channel_id=1, source_target_pairs={{0,17},{1,0},{2,19},{3,2},{4,21},{5,4},{6,23},{7,6},{8,25},{9,8},{... | collective-permute-start | bytes 786440 | tf_op jit(solution)/shard_map/beside/ppermute | solution.py:34
  70.9 2.1 %fusion = f32[512,512]{1,0:T(8,128)S(1)} fusion(bf16[3456,512]{1,0:T(8,128)(2,1)S(1)} %slice_dynamic-update-slice_fusion, bf16[1728,128]{1,0:T(8,128)(2,1)S(1)} %get-tuple-element.58, bf16[1728,128]{1,0:T(8,128)(2,1)S(1)} %get-tuple-element.57, bf16[1728,128]{1,0:T(8,128)(2,1)S(1)} %copy-done.6, bf16[1728,128]{1,0:T(8,128)(2,1)S(1)} %copy-done.8), kind=kOutput, calls=%fused_computation | convolution fusion | flops 1840250880 | bytes 6356992 | tf_op jit(solution)/shard_map/around/dot_general | solution.py:38
  75.3 2.2 %collective-permute-done.22 = f32[2,128,256]{2,1,0:T(8,128)S(1)} collective-permute-done((f32[2,128,256]{2,1,0:T(8,128)S(1)}, f32[2,128,256]{2,1,0:T(8,128)S(1)}, u32[]{:S(2)}, u32[]{:S(2)}) %collective-permute-start.22) | collective-permute-done | bytes 262176 | tf_op jit(solution)/shard_map/beside/ppermute | solution.py:34
  77.5 2.9 %collective-permute-done.21 = f32[2,128,256]{2,1,0:T(8,128)S(1)} collective-permute-done((f32[2,128,256]{2,1,0:T(8,128)S(1)}, f32[2,128,256]{2,1,0:T(8,128)S(1)}, u32[]{:S(2)}, u32[]{:S(2)}) %collective-permute-start.21) | collective-permute-done | bytes 262176 | tf_op jit(solution)/shard_map/beside/ppermute | solution.py:34
  80.9 11.6 %collective-permute-start.24 = (f32[2,128,256]{2,1,0:T(8,128)S(1)}, f32[2,128,256]{2,1,0:T(8,128)S(1)}, u32[]{:S(2)}, u32[]{:S(2)}) collective-permute-start(f32[2,128,256]{2,1,0:T(8,128)S(1)} %get-tuple-element.72), channel_id=1, source_target_pairs={{0,32},{1,48},{2,98},{3,99},{4,2},{5,18},{6,0},{7,1},{8,40},{9,56}... | collective-permute-start | bytes 786440 | tf_op jit(solution)/shard_map/over_y/ppermute | solution.py:34
  92.4 3.3 %collective-permute-start.25 = (f32[2,128,256]{2,1,0:T(8,128)S(1)}, f32[2,128,256]{2,1,0:T(8,128)S(1)}, u32[]{:S(2)}, u32[]{:S(2)}) collective-permute-start(f32[2,128,256]{2,1,0:T(8,128)S(1)} %get-tuple-element.40), channel_id=1, source_target_pairs={{0,98},{1,114},{2,0},{3,1},{4,32},{5,33},{6,2},{7,18},{8,106},{9,1... | collective-permute-start | bytes 786440 | tf_op jit(solution)/shard_map/over_y/ppermute | solution.py:34
  95.8 1.3 %collective-permute-start.27 = (f32[2,128,256]{2,1,0:T(8,128)S(1)}, f32[2,128,256]{2,1,0:T(8,128)S(1)}, u32[]{:S(2)}, u32[]{:S(2)}) collective-permute-start(f32[2,128,256]{2,1,0:T(8,128)S(1)} %get-tuple-element.74), channel_id=1, source_target_pairs={{0,38},{1,39},{2,32},{3,48},{8,46},{9,47},{10,40},{11,56},{16,54},... | collective-permute-start | bytes 786440 | tf_op jit(solution)/shard_map/over_y/ppermute | solution.py:34
  97.1 6.6 %collective-permute-done.24 = f32[2,128,256]{2,1,0:T(8,128)S(1)} collective-permute-done((f32[2,128,256]{2,1,0:T(8,128)S(1)}, f32[2,128,256]{2,1,0:T(8,128)S(1)}, u32[]{:S(2)}, u32[]{:S(2)}) %collective-permute-start.24) | collective-permute-done | bytes 262176 | tf_op jit(solution)/shard_map/over_y/ppermute | solution.py:34
  103.7 4.1 %collective-permute-done.27 = f32[2,128,256]{2,1,0:T(8,128)S(1)} collective-permute-done((f32[2,128,256]{2,1,0:T(8,128)S(1)}, f32[2,128,256]{2,1,0:T(8,128)S(1)}, u32[]{:S(2)}, u32[]{:S(2)}) %collective-permute-start.27) | collective-permute-done | bytes 262176 | tf_op jit(solution)/shard_map/over_y/ppermute | solution.py:34
  108.2 2.8 %collective-permute-start.28 = (f32[128,256]{1,0:T(8,128)S(1)}, f32[128,256]{1,0:T(8,128)S(1)}, u32[]{:S(2)}, u32[]{:S(2)}) collective-permute-start(f32[128,256]{1,0:T(8,128)S(1)} %get-tuple-element.69), channel_id=1, source_target_pairs={{0,8},{1,9},{2,10},{3,11},{4,12},{5,13},{6,14},{7,15},{8,0},{9,1},... | collective-permute-start | bytes 393224 | tf_op jit(solution)/shard_map/place/ppermute | solution.py:34
  (99 shorter events, 23.4 us)
Async XLA Ops:
  2.3 13.2 %collective-permute-start = (bf16[3,3,192,128]{3,2,1,0:T(8,128)(2,1)S(1)}, bf16[3,3,192,128]{3,2,1,0:T(8,128)(2,1)S(1)}, u32[]{:S(2)}, u32[]{:S(2)}) collective-permute-start(bf16[3,3,192,128]{3,2,1,0:T(8,128)(2,1)S(1)} %get-tuple-element.43), channel_id=1, source_target_pairs={{0,7},{1,6},{2,5},{3,4},{4,3},{5,2},{6,1},{7,0},{8,15},{9,14},{10,... | collective-permute-start | bytes 1327112 | tf_op jit(solution)/shard_map/rows/ppermute | solution.py:34
  4.1 11.7 %collective-permute-start.1 = (bf16[1728,128]{1,0:T(8,128)(2,1)S(1)}, bf16[1728,128]{1,0:T(8,128)(2,1)S(1)}, u32[]{:S(2)}, u32[]{:S(2)}) collective-permute-start(bf16[1728,128]{1,0:T(8,128)(2,1)S(1)} %bitcast.193), channel_id=1, source_target_pairs={{0,96},{1,97},{2,98},{3,99},{4,100},{5,101},{6,102},{7,103},{8,104... | collective-permute-start | bytes 1327112 | tf_op jit(solution)/shard_map/first/ppermute | solution.py:34
  6.7 11.9 %collective-permute-start.3 = (bf16[1728,128]{1,0:T(8,128)(2,1)S(1)}, bf16[1728,128]{1,0:T(8,128)(2,1)S(1)}, u32[]{:S(2)}, u32[]{:S(2)}) collective-permute-start(bf16[1728,128]{1,0:T(8,128)(2,1)S(1)} %bitcast.194), channel_id=1, source_target_pairs={{2,34},{3,35},{4,36},{5,37},{10,42},{11,43},{12,44},{13,45},{18,50... | collective-permute-start | bytes 1327112 | tf_op jit(solution)/shard_map/first/ppermute | solution.py:34
  7.3 24.5 %collective-permute-start.6 = (bf16[3,3,192,128]{3,2,1,0:T(8,128)(2,1)S(1)}, bf16[3,3,192,128]{3,2,1,0:T(8,128)(2,1)S(1)}, u32[]{:S(2)}, u32[]{:S(2)}) collective-permute-start(bf16[3,3,192,128]{3,2,1,0:T(8,128)(2,1)S(1)} %get-tuple-element.42), channel_id=1, source_target_pairs={{0,23},{1,22},{2,21},{3,20},{4,19},{5,18},{6,17},{7,16},{8,31},{9,... | collective-permute-start | bytes 1327112 | tf_op jit(solution)/shard_map/rows/ppermute | solution.py:34
  12.7 24.5 %collective-permute-start.5 = (bf16[3,3,192,128]{3,2,1,0:T(8,128)(2,1)S(1)}, bf16[3,3,192,128]{3,2,1,0:T(8,128)(2,1)S(1)}, u32[]{:S(2)}, u32[]{:S(2)}) collective-permute-start(bf16[3,3,192,128]{3,2,1,0:T(8,128)(2,1)S(1)} %get-tuple-element.45), channel_id=1, source_target_pairs={{0,16},{1,17},{2,18},{3,19},{4,20},{5,21},{6,22},{7,23},{8,24},{9,... | collective-permute-start | bytes 1327112 | tf_op jit(solution)/shard_map/rows/ppermute | solution.py:34
  15.8 22.1 %collective-permute-start.2 = (bf16[1728,128]{1,0:T(8,128)(2,1)S(1)}, bf16[1728,128]{1,0:T(8,128)(2,1)S(1)}, u32[]{:S(2)}, u32[]{:S(2)}) collective-permute-start(bf16[1728,128]{1,0:T(8,128)(2,1)S(1)} %bitcast.201), channel_id=1, source_target_pairs={{0,96},{1,97},{2,98},{3,99},{4,100},{5,101},{6,102},{7,103},{8,104... | collective-permute-start | bytes 1327112 | tf_op jit(solution)/shard_map/first/ppermute | solution.py:34
  18.6 19.4 %collective-permute-start.4 = (bf16[1728,128]{1,0:T(8,128)(2,1)S(1)}, bf16[1728,128]{1,0:T(8,128)(2,1)S(1)}, u32[]{:S(2)}, u32[]{:S(2)}) collective-permute-start(bf16[1728,128]{1,0:T(8,128)(2,1)S(1)} %bitcast.202), channel_id=1, source_target_pairs={{2,34},{3,35},{4,36},{5,37},{10,42},{11,43},{12,44},{13,45},{18,50... | collective-permute-start | bytes 1327112 | tf_op jit(solution)/shard_map/first/ppermute | solution.py:34
  39.3 24.3 %collective-permute-start.17 = (bf16[3456,128]{1,0:T(8,128)(2,1)S(1)}, bf16[3456,128]{1,0:T(8,128)(2,1)S(1)}, u32[]{:S(2)}, u32[]{:S(2)}) collective-permute-start(bf16[3456,128]{1,0:T(8,128)(2,1)S(1)} %pad_maximum_fusion), channel_id=1, source_target_pairs={{0,96},{1,97},{2,98},{3,99},{4,100},{5,101},{6,102},{7,103},{8,104... | collective-permute-start | bytes 2654216 | tf_op jit(solution)/shard_map/second/ppermute | solution.py:34
  41.7 25.9 %collective-permute-start.12 = (bf16[3456,128]{1,0:T(8,128)(2,1)S(1)}, bf16[3456,128]{1,0:T(8,128)(2,1)S(1)}, u32[]{:S(2)}, u32[]{:S(2)}) collective-permute-start(bf16[3456,128]{1,0:T(8,128)(2,1)S(1)} %pad_maximum_fusion), channel_id=1, source_target_pairs={{2,34},{3,35},{4,36},{5,37},{10,42},{11,43},{12,44},{13,45},{18,50... | collective-permute-start | bytes 2654216 | tf_op jit(solution)/shard_map/second/ppermute | solution.py:34
  48.1 9.1 %collective-permute-start.15 = (f32[2,128,256]{2,1,0:T(8,128)S(1)}, f32[2,128,256]{2,1,0:T(8,128)S(1)}, u32[]{:S(2)}, u32[]{:S(2)}) collective-permute-start(f32[2,128,256]{2,1,0:T(8,128)S(1)} %get-tuple-element.56), channel_id=1, source_target_pairs={{0,16},{1,17},{2,18},{3,19},{4,20},{5,21},{6,22},{7,23},{8,24},{9,... | collective-permute-start | bytes 786440 | tf_op jit(solution)/shard_map/same/ppermute | solution.py:34
  48.2 12.0 %collective-permute-start.14 = (f32[2,128,256]{2,1,0:T(8,128)S(1)}, f32[2,128,256]{2,1,0:T(8,128)S(1)}, u32[]{:S(2)}, u32[]{:S(2)}) collective-permute-start(f32[2,128,256]{2,1,0:T(8,128)S(1)} %get-tuple-element.55), channel_id=1, source_target_pairs={{0,17},{1,0},{2,19},{3,2},{4,21},{5,4},{6,23},{7,6},{8,25},{9,8},{... | collective-permute-start | bytes 786440 | tf_op jit(solution)/shard_map/same/ppermute | solution.py:34
  50.7 12.8 %collective-permute-start.13 = (f32[2,128,256]{2,1,0:T(8,128)S(1)}, f32[2,128,256]{2,1,0:T(8,128)S(1)}, u32[]{:S(2)}, u32[]{:S(2)}) collective-permute-start(f32[2,128,256]{2,1,0:T(8,128)S(1)} %get-tuple-element.54), channel_id=1, source_target_pairs={{0,1},{1,16},{2,3},{3,18},{4,5},{5,20},{6,7},{7,22},{8,9},{9,24},{... | collective-permute-start | bytes 786440 | tf_op jit(solution)/shard_map/same/ppermute | solution.py:34
  57.2 10.6 %collective-permute-start.10 = (bf16[1728,128]{1,0:T(8,128)(2,1)S(1)}, bf16[1728,128]{1,0:T(8,128)(2,1)S(1)}, u32[]{:S(2)}, u32[]{:S(2)}) collective-permute-start(bf16[1728,128]{1,0:T(8,128)(2,1)S(1)} %copy-done.1), channel_id=1, source_target_pairs={{0,8},{1,9},{2,10},{3,11},{4,12},{5,13},{6,14},{7,15},{8,0},{9,1},... | collective-permute-start | bytes 1327112 | tf_op jit(solution)/shard_map/second/ppermute | solution.py:34
  60.2 8.5 %collective-permute-start.11 = (bf16[1728,128]{1,0:T(8,128)(2,1)S(1)}, bf16[1728,128]{1,0:T(8,128)(2,1)S(1)}, u32[]{:S(2)}, u32[]{:S(2)}) collective-permute-start(bf16[1728,128]{1,0:T(8,128)(2,1)S(1)} %copy-done.3), channel_id=1, source_target_pairs={{0,8},{1,9},{2,10},{3,11},{4,12},{5,13},{6,14},{7,15},{8,0},{9,1},... | collective-permute-start | bytes 1327112 | tf_op jit(solution)/shard_map/second/ppermute | solution.py:34
  65.0 9.6 %collective-permute-start.23 = (f32[2,128,256]{2,1,0:T(8,128)S(1)}, f32[2,128,256]{2,1,0:T(8,128)S(1)}, u32[]{:S(2)}, u32[]{:S(2)}) collective-permute-start(f32[2,128,256]{2,1,0:T(8,128)S(1)} %get-tuple-element.53), channel_id=1, source_target_pairs={{0,16},{1,17},{2,18},{3,19},{4,20},{5,21},{6,22},{7,23},{8,24},{9,... | collective-permute-start | bytes 786440 | tf_op jit(solution)/shard_map/beside/ppermute | solution.py:34
  66.3 11.2 %collective-permute-start.22 = (f32[2,128,256]{2,1,0:T(8,128)S(1)}, f32[2,128,256]{2,1,0:T(8,128)S(1)}, u32[]{:S(2)}, u32[]{:S(2)}) collective-permute-start(f32[2,128,256]{2,1,0:T(8,128)S(1)} %get-tuple-element.52), channel_id=1, source_target_pairs={{0,17},{1,0},{2,19},{3,2},{4,21},{5,4},{6,23},{7,6},{8,25},{9,8},{... | collective-permute-start | bytes 786440 | tf_op jit(solution)/shard_map/beside/ppermute | solution.py:34
  67.6 12.8 %collective-permute-start.21 = (f32[2,128,256]{2,1,0:T(8,128)S(1)}, f32[2,128,256]{2,1,0:T(8,128)S(1)}, u32[]{:S(2)}, u32[]{:S(2)}) collective-permute-start(f32[2,128,256]{2,1,0:T(8,128)S(1)} %get-tuple-element.51), channel_id=1, source_target_pairs={{0,1},{1,16},{2,3},{3,18},{4,5},{5,20},{6,7},{7,22},{8,9},{9,24},{... | collective-permute-start | bytes 786440 | tf_op jit(solution)/shard_map/beside/ppermute | solution.py:34
  73.2 7.3 %collective-permute-start.20 = (f32[2,128,256]{2,1,0:T(8,128)S(1)}, f32[2,128,256]{2,1,0:T(8,128)S(1)}, u32[]{:S(2)}, u32[]{:S(2)}) collective-permute-start(f32[2,128,256]{2,1,0:T(8,128)S(1)} %get-tuple-element.48), channel_id=1, source_target_pairs={{0,16},{1,17},{2,18},{3,19},{8,24},{9,25},{10,26},{11,27},{16,0},{... | collective-permute-start | bytes 786440 | tf_op jit(solution)/shard_map/around/ppermute | solution.py:34
  73.9 6.7 %collective-permute-start.19 = (f32[2,128,256]{2,1,0:T(8,128)S(1)}, f32[2,128,256]{2,1,0:T(8,128)S(1)}, u32[]{:S(2)}, u32[]{:S(2)}) collective-permute-start(f32[2,128,256]{2,1,0:T(8,128)S(1)} %get-tuple-element.47), channel_id=1, source_target_pairs={{0,17},{1,0},{2,19},{3,2},{8,25},{9,8},{10,27},{11,10},{16,1},{17,... | collective-permute-start | bytes 786440 | tf_op jit(solution)/shard_map/around/ppermute | solution.py:34
  74.6 6.0 %collective-permute-start.18 = (f32[2,128,256]{2,1,0:T(8,128)S(1)}, f32[2,128,256]{2,1,0:T(8,128)S(1)}, u32[]{:S(2)}, u32[]{:S(2)}) collective-permute-start(f32[2,128,256]{2,1,0:T(8,128)S(1)} %get-tuple-element.46), channel_id=1, source_target_pairs={{0,1},{1,16},{2,3},{3,18},{8,9},{9,24},{10,11},{11,26},{16,17},{17... | collective-permute-start | bytes 786440 | tf_op jit(solution)/shard_map/around/ppermute | solution.py:34
  80.8 16.3 %collective-permute-start.26 = (f32[2,128,256]{2,1,0:T(8,128)S(1)}, f32[2,128,256]{2,1,0:T(8,128)S(1)}, u32[]{:S(2)}, u32[]{:S(2)}) collective-permute-start(f32[2,128,256]{2,1,0:T(8,128)S(1)} %get-tuple-element.73), channel_id=1, source_target_pairs={{0,2},{1,3},{2,38},{3,54},{4,0},{5,1},{6,32},{7,33},{8,10},{9,11},... | collective-permute-start | bytes 786440 | tf_op jit(solution)/shard_map/over_y/ppermute | solution.py:34
  80.9 22.8 %collective-permute-start.24 = (f32[2,128,256]{2,1,0:T(8,128)S(1)}, f32[2,128,256]{2,1,0:T(8,128)S(1)}, u32[]{:S(2)}, u32[]{:S(2)}) collective-permute-start(f32[2,128,256]{2,1,0:T(8,128)S(1)} %get-tuple-element.72), channel_id=1, source_target_pairs={{0,32},{1,48},{2,98},{3,99},{4,2},{5,18},{6,0},{7,1},{8,40},{9,56}... | collective-permute-start | bytes 786440 | tf_op jit(solution)/shard_map/over_y/ppermute | solution.py:34
  92.4 11.2 %collective-permute-start.25 = (f32[2,128,256]{2,1,0:T(8,128)S(1)}, f32[2,128,256]{2,1,0:T(8,128)S(1)}, u32[]{:S(2)}, u32[]{:S(2)}) collective-permute-start(f32[2,128,256]{2,1,0:T(8,128)S(1)} %get-tuple-element.40), channel_id=1, source_target_pairs={{0,98},{1,114},{2,0},{3,1},{4,32},{5,33},{6,2},{7,18},{8,106},{9,1... | collective-permute-start | bytes 786440 | tf_op jit(solution)/shard_map/over_y/ppermute | solution.py:34
  95.8 12.0 %collective-permute-start.27 = (f32[2,128,256]{2,1,0:T(8,128)S(1)}, f32[2,128,256]{2,1,0:T(8,128)S(1)}, u32[]{:S(2)}, u32[]{:S(2)}) collective-permute-start(f32[2,128,256]{2,1,0:T(8,128)S(1)} %get-tuple-element.74), channel_id=1, source_target_pairs={{0,38},{1,39},{2,32},{3,48},{8,46},{9,47},{10,40},{11,56},{16,54},... | collective-permute-start | bytes 786440 | tf_op jit(solution)/shard_map/over_y/ppermute | solution.py:34
  (14 other events, 99.7 us)

commit v7 on v5

--- a/solution.py
+++ b/solution.py
@@ -150,13 +150,13 @@
         )
 
     same, beside = lax.optimization_barrier((same, beside))
-    mixed = lax.optimization_barrier(tuple(jnp.where(d == at, same, beside) for at in (3, 2, 1)))
+    mixed = lax.optimization_barrier(tuple(jnp.where(d == at, same, beside) for at in (1, 3, 2)))
 
     rounds = (
+        ((2, False), (0, False), (1, True), (1, False)),
+        ((2, True), (1, True), None, None),
         ((1, True), (2, False), (1, False), (0, False)),
         ((1, False), (2, True), (0, False), (1, True)),
-        ((2, False), (0, False), (1, True), (1, False)),
-        ((2, True), (1, True), None, None),
     )
     with jax.named_scope("over_y"):
         got = []
@@ -171,12 +171,13 @@
                 if turn != ((y - x) % 4 in SWAPS[block]):
                     h, l = l, h
                 return row % 4, h, c, column, l
-            value = (mixed + (beside,))[len(got)]
+            value = (mixed[0], beside, mixed[1], mixed[2])[len(got)]
             for at, step in enumerate(plan):
                 if step is not None and step[0] == 2:
                     value = jnp.where(d == at, around, value)
             got.append(send(value, target))
         own_block = jnp.where(d == 0, same, beside)
+        got = got[2:] + got[:2]
         odd = got[0] + got[2]
         straight = odd + jnp.where(d == 2, 0, own_block + got[1])
         turned = jnp.where(d == 2, 0, odd) + got[1] + got[3]

time: 114 us -> 114 us (level)
  no operation moved by 1% of the time
where the time goes in v7:
time: 114 us; the launch traced here: 113 us
  starting transfers between devices  48.5 us (43%)
  waiting for transfers between devices  46.6 us (41%)
  matrix products  7.53 us (7%)
  local copies, waits for them, and re-layouts  7.26 us (6%)
  other arithmetic  1.78 us (2%)
  between operations  1.25 us (1%)
    ppermute x29, starting transfers between devices, send(): return lax.ppermute(value, AXES, pairs)  48.5 us
    ppermute x29, waiting for transfers between devices, send(): return lax.ppermute(value, AXES, pairs)  46.6 us
    dot_general x6, matrix products, inner(): lax.dot_general(left, right, (((0,), (0,)), ((), ())), preferred_element_...  6.95 us
  transfers between devices with their start and end apart: 29, of which 12 were waited for; matrix products, arithmetic and copies ran while one was open for 11% of the time, Pallas kernels for 0%

profile of v7, /device:TPU:25, one launch (start us, length us, event | category | flops | bytes accessed | tf_op | source)
XLA Modules:
  0.0 112.9 jit_solution(7918396175477704605)
XLA Ops:
  0.7 1.5 %constant_dynamic-slice_fusion = (bf16[3,3,192,128]{3,2,1,0:T(8,128)(2,1)S(1)}, bf16[3,3,192,128]{3,2,1,0:T(8,128)(2,1)S(1)}, bf16[3,3,192,128]{3,2,1,0:T(8,128)(2,1)S(1)}, bf16[3,3,192,128]{3,2,1,0:T(8,128)(2,1)S(1)}) fusion(bf16[3,12,192,128]{3,2,1,0:T(8,128)(2,1)} %param.2, s32[]{:T(128)S(6)} %select_n.507, s32[]{:T(128)S(6)} %select_n.505, ...), kind=kLoop, calls=%fused_computation.100 | loop fusion | bytes 3538960 | tf_op jit(solution)/shard_map/rows/dynamic_slice | solution.py:65
  2.3 1.4 %collective-permute-start = (bf16[3,3,192,128]{3,2,1,0:T(8,128)(2,1)S(1)}, bf16[3,3,192,128]{3,2,1,0:T(8,128)(2,1)S(1)}, u32[]{:S(2)}, u32[]{:S(2)}) collective-permute-start(bf16[3,3,192,128]{3,2,1,0:T(8,128)(2,1)S(1)} %get-tuple-element.43), channel_id=1, source_target_pairs={{0,7},{1,6},{2,5},{3,4},{4,3},{5,2},{6,1},{7,0},{8,15},{9,14},{10,... | collective-permute-start | bytes 1327112 | tf_op jit(solution)/shard_map/rows/ppermute | solution.py:34
  4.1 2.5 %collective-permute-start.1 = (bf16[1728,128]{1,0:T(8,128)(2,1)S(1)}, bf16[1728,128]{1,0:T(8,128)(2,1)S(1)}, u32[]{:S(2)}, u32[]{:S(2)}) collective-permute-start(bf16[1728,128]{1,0:T(8,128)(2,1)S(1)} %bitcast.194), channel_id=1, source_target_pairs={{0,96},{1,97},{2,98},{3,99},{4,100},{5,101},{6,102},{7,103},{8,104... | collective-permute-start | bytes 1327112 | tf_op jit(solution)/shard_map/first/ppermute | solution.py:34
  7.3 5.4 %collective-permute-start.6 = (bf16[3,3,192,128]{3,2,1,0:T(8,128)(2,1)S(1)}, bf16[3,3,192,128]{3,2,1,0:T(8,128)(2,1)S(1)}, u32[]{:S(2)}, u32[]{:S(2)}) collective-permute-start(bf16[3,3,192,128]{3,2,1,0:T(8,128)(2,1)S(1)} %get-tuple-element.42), channel_id=1, source_target_pairs={{0,23},{1,22},{2,21},{3,20},{4,19},{5,18},{6,17},{7,16},{8,31},{9,... | collective-permute-start | bytes 1327112 | tf_op jit(solution)/shard_map/rows/ppermute | solution.py:34
  12.7 2.8 %collective-permute-done = bf16[3,3,192,128]{3,2,1,0:T(8,128)(2,1)S(1)} collective-permute-done((bf16[3,3,192,128]{3,2,1,0:T(8,128)(2,1)S(1)}, bf16[3,3,192,128]{3,2,1,0:T(8,128)(2,1)S(1)}, u32[]{:S(2)}, u32[]{:S(2)}) %collective-permute-start) | collective-permute-done | bytes 442400 | tf_op jit(solution)/shard_map/rows/ppermute | solution.py:34
  15.8 2.8 %collective-permute-start.2 = (bf16[1728,128]{1,0:T(8,128)(2,1)S(1)}, bf16[1728,128]{1,0:T(8,128)(2,1)S(1)}, u32[]{:S(2)}, u32[]{:S(2)}) collective-permute-start(bf16[1728,128]{1,0:T(8,128)(2,1)S(1)} %bitcast.202), channel_id=1, source_target_pairs={{0,96},{1,97},{2,98},{3,99},{4,100},{5,101},{6,102},{7,103},{8,104... | collective-permute-start | bytes 1327112 | tf_op jit(solution)/shard_map/first/ppermute | solution.py:34
  19.3 12.5 %collective-permute-done.6 = bf16[3,3,192,128]{3,2,1,0:T(8,128)(2,1)S(1)} collective-permute-done((bf16[3,3,192,128]{3,2,1,0:T(8,128)(2,1)S(1)}, bf16[3,3,192,128]{3,2,1,0:T(8,128)(2,1)S(1)}, u32[]{:S(2)}, u32[]{:S(2)}) %collective-permute-start.6) | collective-permute-done | bytes 442400 | tf_op jit(solution)/shard_map/rows/ppermute | solution.py:34
  32.1 5.2 %collective-permute-done.5 = bf16[3,3,192,128]{3,2,1,0:T(8,128)(2,1)S(1)} collective-permute-done((bf16[3,3,192,128]{3,2,1,0:T(8,128)(2,1)S(1)}, bf16[3,3,192,128]{3,2,1,0:T(8,128)(2,1)S(1)}, u32[]{:S(2)}, u32[]{:S(2)}) %collective-permute-start.5) | collective-permute-done | bytes 442400 | tf_op jit(solution)/shard_map/rows/ppermute | solution.py:34
  39.3 2.5 %collective-permute-start.17 = (bf16[3456,128]{1,0:T(8,128)(2,1)S(1)}, bf16[3456,128]{1,0:T(8,128)(2,1)S(1)}, u32[]{:S(2)}, u32[]{:S(2)}) collective-permute-start(bf16[3456,128]{1,0:T(8,128)(2,1)S(1)} %pad_maximum_fusion), channel_id=1, source_target_pairs={{0,96},{1,97},{2,98},{3,99},{4,100},{5,101},{6,102},{7,103},{8,104... | collective-permute-start | bytes 2654216 | tf_op jit(solution)/shard_map/second/ppermute | solution.py:34
  48.2 2.5 %collective-permute-start.14 = (f32[2,128,256]{2,1,0:T(8,128)S(1)}, f32[2,128,256]{2,1,0:T(8,128)S(1)}, u32[]{:S(2)}, u32[]{:S(2)}) collective-permute-start(f32[2,128,256]{2,1,0:T(8,128)S(1)} %get-tuple-element.53), channel_id=1, source_target_pairs={{0,17},{1,0},{2,19},{3,2},{4,21},{5,4},{6,23},{7,6},{8,25},{9,8},{... | collective-permute-start | bytes 786440 | tf_op jit(solution)/shard_map/same/ppermute | solution.py:34
  51.9 5.3 %collective-permute-done.15 = f32[2,128,256]{2,1,0:T(8,128)S(1)} collective-permute-done((f32[2,128,256]{2,1,0:T(8,128)S(1)}, f32[2,128,256]{2,1,0:T(8,128)S(1)}, u32[]{:S(2)}, u32[]{:S(2)}) %collective-permute-start.15) | collective-permute-done | bytes 262176 | tf_op jit(solution)/shard_map/same/ppermute | solution.py:34
  57.2 2.1 %collective-permute-start.10 = (bf16[1728,128]{1,0:T(8,128)(2,1)S(1)}, bf16[1728,128]{1,0:T(8,128)(2,1)S(1)}, u32[]{:S(2)}, u32[]{:S(2)}) collective-permute-start(bf16[1728,128]{1,0:T(8,128)(2,1)S(1)} %copy-done.1), channel_id=1, source_target_pairs={{0,8},{1,9},{2,10},{3,11},{4,12},{5,13},{6,14},{7,15},{8,0},{9,1},... | collective-permute-start | bytes 1327112 | tf_op jit(solution)/shard_map/second/ppermute | solution.py:34
  60.2 1.3 %collective-permute-start.11 = (bf16[1728,128]{1,0:T(8,128)(2,1)S(1)}, bf16[1728,128]{1,0:T(8,128)(2,1)S(1)}, u32[]{:S(2)}, u32[]{:S(2)}) collective-permute-start(bf16[1728,128]{1,0:T(8,128)(2,1)S(1)} %copy-done.3), channel_id=1, source_target_pairs={{0,8},{1,9},{2,10},{3,11},{4,12},{5,13},{6,14},{7,15},{8,0},{9,1},... | collective-permute-start | bytes 1327112 | tf_op jit(solution)/shard_map/second/ppermute | solution.py:34
  61.5 2.0 %collective-permute-done.13 = f32[2,128,256]{2,1,0:T(8,128)S(1)} collective-permute-done((f32[2,128,256]{2,1,0:T(8,128)S(1)}, f32[2,128,256]{2,1,0:T(8,128)S(1)}, u32[]{:S(2)}, u32[]{:S(2)}) %collective-permute-start.13) | collective-permute-done | bytes 262176 | tf_op jit(solution)/shard_map/same/ppermute | solution.py:34
  65.0 1.4 %collective-permute-start.23 = (f32[2,128,256]{2,1,0:T(8,128)S(1)}, f32[2,128,256]{2,1,0:T(8,128)S(1)}, u32[]{:S(2)}, u32[]{:S(2)}) collective-permute-start(f32[2,128,256]{2,1,0:T(8,128)S(1)} %get-tuple-element.51), channel_id=1, source_target_pairs={{0,16},{1,17},{2,18},{3,19},{4,20},{5,21},{6,22},{7,23},{8,24},{9,... | collective-permute-start | bytes 786440 | tf_op jit(solution)/shard_map/beside/ppermute | solution.py:34
  66.3 1.3 %collective-permute-start.22 = (f32[2,128,256]{2,1,0:T(8,128)S(1)}, f32[2,128,256]{2,1,0:T(8,128)S(1)}, u32[]{:S(2)}, u32[]{:S(2)}) collective-permute-start(f32[2,128,256]{2,1,0:T(8,128)S(1)} %get-tuple-element.50), channel_id=1, source_target_pairs={{0,17},{1,0},{2,19},{3,2},{4,21},{5,4},{6,23},{7,6},{8,25},{9,8},{... | collective-permute-start | bytes 786440 | tf_op jit(solution)/shard_map/beside/ppermute | solution.py:34
  75.4 2.1 %collective-permute-done.22 = f32[2,128,256]{2,1,0:T(8,128)S(1)} collective-permute-done((f32[2,128,256]{2,1,0:T(8,128)S(1)}, f32[2,128,256]{2,1,0:T(8,128)S(1)}, u32[]{:S(2)}, u32[]{:S(2)}) %collective-permute-start.22) | collective-permute-done | bytes 262176 | tf_op jit(solution)/shard_map/beside/ppermute | solution.py:34
  77.5 2.9 %collective-permute-done.21 = f32[2,128,256]{2,1,0:T(8,128)S(1)} collective-permute-done((f32[2,128,256]{2,1,0:T(8,128)S(1)}, f32[2,128,256]{2,1,0:T(8,128)S(1)}, u32[]{:S(2)}, u32[]{:S(2)}) %collective-permute-start.21) | collective-permute-done | bytes 262176 | tf_op jit(solution)/shard_map/beside/ppermute | solution.py:34
  80.9 11.7 %collective-permute-start.24 = (f32[2,128,256]{2,1,0:T(8,128)S(1)}, f32[2,128,256]{2,1,0:T(8,128)S(1)}, u32[]{:S(2)}, u32[]{:S(2)}) collective-permute-start(f32[2,128,256]{2,1,0:T(8,128)S(1)} %get-tuple-element.70), channel_id=1, source_target_pairs={{0,32},{1,48},{2,98},{3,99},{4,2},{5,18},{6,0},{7,1},{8,40},{9,56}... | collective-permute-start | bytes 786440 | tf_op jit(solution)/shard_map/over_y/ppermute | solution.py:34
  92.6 3.2 %collective-permute-start.25 = (f32[2,128,256]{2,1,0:T(8,128)S(1)}, f32[2,128,256]{2,1,0:T(8,128)S(1)}, u32[]{:S(2)}, u32[]{:S(2)}) collective-permute-start(f32[2,128,256]{2,1,0:T(8,128)S(1)} %get-tuple-element.40), channel_id=1, source_target_pairs={{0,98},{1,114},{2,0},{3,1},{4,32},{5,33},{6,2},{7,18},{8,106},{9,1... | collective-permute-start | bytes 786440 | tf_op jit(solution)/shard_map/over_y/ppermute | solution.py:34
  95.8 1.3 %collective-permute-start.27 = (f32[2,128,256]{2,1,0:T(8,128)S(1)}, f32[2,128,256]{2,1,0:T(8,128)S(1)}, u32[]{:S(2)}, u32[]{:S(2)}) collective-permute-start(f32[2,128,256]{2,1,0:T(8,128)S(1)} %get-tuple-element.72), channel_id=1, source_target_pairs={{0,38},{1,39},{2,32},{3,48},{8,46},{9,47},{10,40},{11,56},{16,54},... | collective-permute-start | bytes 786440 | tf_op jit(solution)/shard_map/over_y/ppermute | solution.py:34
  97.1 6.7 %collective-permute-done.24 = f32[2,128,256]{2,1,0:T(8,128)S(1)} collective-permute-done((f32[2,128,256]{2,1,0:T(8,128)S(1)}, f32[2,128,256]{2,1,0:T(8,128)S(1)}, u32[]{:S(2)}, u32[]{:S(2)}) %collective-permute-start.24) | collective-permute-done | bytes 262176 | tf_op jit(solution)/shard_map/over_y/ppermute | solution.py:34
  103.8 4.1 %collective-permute-done.27 = f32[2,128,256]{2,1,0:T(8,128)S(1)} collective-permute-done((f32[2,128,256]{2,1,0:T(8,128)S(1)}, f32[2,128,256]{2,1,0:T(8,128)S(1)}, u32[]{:S(2)}, u32[]{:S(2)}) %collective-permute-start.27) | collective-permute-done | bytes 262176 | tf_op jit(solution)/shard_map/over_y/ppermute | solution.py:34
  108.3 2.8 %collective-permute-start.28 = (f32[128,256]{1,0:T(8,128)S(1)}, f32[128,256]{1,0:T(8,128)S(1)}, u32[]{:S(2)}, u32[]{:S(2)}) collective-permute-start(f32[128,256]{1,0:T(8,128)S(1)} %get-tuple-element.67), channel_id=1, source_target_pairs={{0,8},{1,9},{2,10},{3,11},{4,12},{5,13},{6,14},{7,15},{8,0},{9,1},... | collective-permute-start | bytes 393224 | tf_op jit(solution)/shard_map/place/ppermute | solution.py:34
  (99 shorter events, 24.4 us)
Async XLA Ops:
  2.3 13.2 %collective-permute-start = (bf16[3,3,192,128]{3,2,1,0:T(8,128)(2,1)S(1)}, bf16[3,3,192,128]{3,2,1,0:T(8,128)(2,1)S(1)}, u32[]{:S(2)}, u32[]{:S(2)}) collective-permute-start(bf16[3,3,192,128]{3,2,1,0:T(8,128)(2,1)S(1)} %get-tuple-element.43), channel_id=1, source_target_pairs={{0,7},{1,6},{2,5},{3,4},{4,3},{5,2},{6,1},{7,0},{8,15},{9,14},{10,... | collective-permute-start | bytes 1327112 | tf_op jit(solution)/shard_map/rows/ppermute | solution.py:34
  4.1 11.7 %collective-permute-start.1 = (bf16[1728,128]{1,0:T(8,128)(2,1)S(1)}, bf16[1728,128]{1,0:T(8,128)(2,1)S(1)}, u32[]{:S(2)}, u32[]{:S(2)}) collective-permute-start(bf16[1728,128]{1,0:T(8,128)(2,1)S(1)} %bitcast.194), channel_id=1, source_target_pairs={{0,96},{1,97},{2,98},{3,99},{4,100},{5,101},{6,102},{7,103},{8,104... | collective-permute-start | bytes 1327112 | tf_op jit(solution)/shard_map/first/ppermute | solution.py:34
  6.7 11.9 %collective-permute-start.3 = (bf16[1728,128]{1,0:T(8,128)(2,1)S(1)}, bf16[1728,128]{1,0:T(8,128)(2,1)S(1)}, u32[]{:S(2)}, u32[]{:S(2)}) collective-permute-start(bf16[1728,128]{1,0:T(8,128)(2,1)S(1)} %bitcast.195), channel_id=1, source_target_pairs={{2,34},{3,35},{4,36},{5,37},{10,42},{11,43},{12,44},{13,45},{18,50... | collective-permute-start | bytes 1327112 | tf_op jit(solution)/shard_map/first/ppermute | solution.py:34
  7.3 24.5 %collective-permute-start.6 = (bf16[3,3,192,128]{3,2,1,0:T(8,128)(2,1)S(1)}, bf16[3,3,192,128]{3,2,1,0:T(8,128)(2,1)S(1)}, u32[]{:S(2)}, u32[]{:S(2)}) collective-permute-start(bf16[3,3,192,128]{3,2,1,0:T(8,128)(2,1)S(1)} %get-tuple-element.42), channel_id=1, source_target_pairs={{0,23},{1,22},{2,21},{3,20},{4,19},{5,18},{6,17},{7,16},{8,31},{9,... | collective-permute-start | bytes 1327112 | tf_op jit(solution)/shard_map/rows/ppermute | solution.py:34
  12.7 24.5 %collective-permute-start.5 = (bf16[3,3,192,128]{3,2,1,0:T(8,128)(2,1)S(1)}, bf16[3,3,192,128]{3,2,1,0:T(8,128)(2,1)S(1)}, u32[]{:S(2)}, u32[]{:S(2)}) collective-permute-start(bf16[3,3,192,128]{3,2,1,0:T(8,128)(2,1)S(1)} %get-tuple-element.45), channel_id=1, source_target_pairs={{0,16},{1,17},{2,18},{3,19},{4,20},{5,21},{6,22},{7,23},{8,24},{9,... | collective-permute-start | bytes 1327112 | tf_op jit(solution)/shard_map/rows/ppermute | solution.py:34
  15.8 22.1 %collective-permute-start.2 = (bf16[1728,128]{1,0:T(8,128)(2,1)S(1)}, bf16[1728,128]{1,0:T(8,128)(2,1)S(1)}, u32[]{:S(2)}, u32[]{:S(2)}) collective-permute-start(bf16[1728,128]{1,0:T(8,128)(2,1)S(1)} %bitcast.202), channel_id=1, source_target_pairs={{0,96},{1,97},{2,98},{3,99},{4,100},{5,101},{6,102},{7,103},{8,104... | collective-permute-start | bytes 1327112 | tf_op jit(solution)/shard_map/first/ppermute | solution.py:34
  18.6 19.4 %collective-permute-start.4 = (bf16[1728,128]{1,0:T(8,128)(2,1)S(1)}, bf16[1728,128]{1,0:T(8,128)(2,1)S(1)}, u32[]{:S(2)}, u32[]{:S(2)}) collective-permute-start(bf16[1728,128]{1,0:T(8,128)(2,1)S(1)} %bitcast.203), channel_id=1, source_target_pairs={{2,34},{3,35},{4,36},{5,37},{10,42},{11,43},{12,44},{13,45},{18,50... | collective-permute-start | bytes 1327112 | tf_op jit(solution)/shard_map/first/ppermute | solution.py:34
  39.3 24.3 %collective-permute-start.17 = (bf16[3456,128]{1,0:T(8,128)(2,1)S(1)}, bf16[3456,128]{1,0:T(8,128)(2,1)S(1)}, u32[]{:S(2)}, u32[]{:S(2)}) collective-permute-start(bf16[3456,128]{1,0:T(8,128)(2,1)S(1)} %pad_maximum_fusion), channel_id=1, source_target_pairs={{0,96},{1,97},{2,98},{3,99},{4,100},{5,101},{6,102},{7,103},{8,104... | collective-permute-start | bytes 2654216 | tf_op jit(solution)/shard_map/second/ppermute | solution.py:34
  41.7 25.9 %collective-permute-start.12 = (bf16[3456,128]{1,0:T(8,128)(2,1)S(1)}, bf16[3456,128]{1,0:T(8,128)(2,1)S(1)}, u32[]{:S(2)}, u32[]{:S(2)}) collective-permute-start(bf16[3456,128]{1,0:T(8,128)(2,1)S(1)} %pad_maximum_fusion), channel_id=1, source_target_pairs={{2,34},{3,35},{4,36},{5,37},{10,42},{11,43},{12,44},{13,45},{18,50... | collective-permute-start | bytes 2654216 | tf_op jit(solution)/shard_map/second/ppermute | solution.py:34
  48.1 9.1 %collective-permute-start.15 = (f32[2,128,256]{2,1,0:T(8,128)S(1)}, f32[2,128,256]{2,1,0:T(8,128)S(1)}, u32[]{:S(2)}, u32[]{:S(2)}) collective-permute-start(f32[2,128,256]{2,1,0:T(8,128)S(1)} %get-tuple-element.54), channel_id=1, source_target_pairs={{0,16},{1,17},{2,18},{3,19},{4,20},{5,21},{6,22},{7,23},{8,24},{9,... | collective-permute-start | bytes 786440 | tf_op jit(solution)/shard_map/same/ppermute | solution.py:34
  48.2 12.0 %collective-permute-start.14 = (f32[2,128,256]{2,1,0:T(8,128)S(1)}, f32[2,128,256]{2,1,0:T(8,128)S(1)}, u32[]{:S(2)}, u32[]{:S(2)}) collective-permute-start(f32[2,128,256]{2,1,0:T(8,128)S(1)} %get-tuple-element.53), channel_id=1, source_target_pairs={{0,17},{1,0},{2,19},{3,2},{4,21},{5,4},{6,23},{7,6},{8,25},{9,8},{... | collective-permute-start | bytes 786440 | tf_op jit(solution)/shard_map/same/ppermute | solution.py:34
  50.7 12.8 %collective-permute-start.13 = (f32[2,128,256]{2,1,0:T(8,128)S(1)}, f32[2,128,256]{2,1,0:T(8,128)S(1)}, u32[]{:S(2)}, u32[]{:S(2)}) collective-permute-start(f32[2,128,256]{2,1,0:T(8,128)S(1)} %get-tuple-element.52), channel_id=1, source_target_pairs={{0,1},{1,16},{2,3},{3,18},{4,5},{5,20},{6,7},{7,22},{8,9},{9,24},{... | collective-permute-start | bytes 786440 | tf_op jit(solution)/shard_map/same/ppermute | solution.py:34
  57.2 10.6 %collective-permute-start.10 = (bf16[1728,128]{1,0:T(8,128)(2,1)S(1)}, bf16[1728,128]{1,0:T(8,128)(2,1)S(1)}, u32[]{:S(2)}, u32[]{:S(2)}) collective-permute-start(bf16[1728,128]{1,0:T(8,128)(2,1)S(1)} %copy-done.1), channel_id=1, source_target_pairs={{0,8},{1,9},{2,10},{3,11},{4,12},{5,13},{6,14},{7,15},{8,0},{9,1},... | collective-permute-start | bytes 1327112 | tf_op jit(solution)/shard_map/second/ppermute | solution.py:34
  60.2 8.5 %collective-permute-start.11 = (bf16[1728,128]{1,0:T(8,128)(2,1)S(1)}, bf16[1728,128]{1,0:T(8,128)(2,1)S(1)}, u32[]{:S(2)}, u32[]{:S(2)}) collective-permute-start(bf16[1728,128]{1,0:T(8,128)(2,1)S(1)} %copy-done.3), channel_id=1, source_target_pairs={{0,8},{1,9},{2,10},{3,11},{4,12},{5,13},{6,14},{7,15},{8,0},{9,1},... | collective-permute-start | bytes 1327112 | tf_op jit(solution)/shard_map/second/ppermute | solution.py:34
  65.0 9.8 %collective-permute-start.23 = (f32[2,128,256]{2,1,0:T(8,128)S(1)}, f32[2,128,256]{2,1,0:T(8,128)S(1)}, u32[]{:S(2)}, u32[]{:S(2)}) collective-permute-start(f32[2,128,256]{2,1,0:T(8,128)S(1)} %get-tuple-element.51), channel_id=1, source_target_pairs={{0,16},{1,17},{2,18},{3,19},{4,20},{5,21},{6,22},{7,23},{8,24},{9,... | collective-permute-start | bytes 786440 | tf_op jit(solution)/shard_map/beside/ppermute | solution.py:34
  66.3 11.2 %collective-permute-start.22 = (f32[2,128,256]{2,1,0:T(8,128)S(1)}, f32[2,128,256]{2,1,0:T(8,128)S(1)}, u32[]{:S(2)}, u32[]{:S(2)}) collective-permute-start(f32[2,128,256]{2,1,0:T(8,128)S(1)} %get-tuple-element.50), channel_id=1, source_target_pairs={{0,17},{1,0},{2,19},{3,2},{4,21},{5,4},{6,23},{7,6},{8,25},{9,8},{... | collective-permute-start | bytes 786440 | tf_op jit(solution)/shard_map/beside/ppermute | solution.py:34
  67.6 12.8 %collective-permute-start.21 = (f32[2,128,256]{2,1,0:T(8,128)S(1)}, f32[2,128,256]{2,1,0:T(8,128)S(1)}, u32[]{:S(2)}, u32[]{:S(2)}) collective-permute-start(f32[2,128,256]{2,1,0:T(8,128)S(1)} %get-tuple-element.49), channel_id=1, source_target_pairs={{0,1},{1,16},{2,3},{3,18},{4,5},{5,20},{6,7},{7,22},{8,9},{9,24},{... | collective-permute-start | bytes 786440 | tf_op jit(solution)/shard_map/beside/ppermute | solution.py:34
  73.4 7.2 %collective-permute-start.20 = (f32[2,128,256]{2,1,0:T(8,128)S(1)}, f32[2,128,256]{2,1,0:T(8,128)S(1)}, u32[]{:S(2)}, u32[]{:S(2)}) collective-permute-start(f32[2,128,256]{2,1,0:T(8,128)S(1)} %get-tuple-element.48), channel_id=1, source_target_pairs={{0,16},{1,17},{2,18},{3,19},{8,24},{9,25},{10,26},{11,27},{16,0},{... | collective-permute-start | bytes 786440 | tf_op jit(solution)/shard_map/around/ppermute | solution.py:34
  74.1 6.5 %collective-permute-start.19 = (f32[2,128,256]{2,1,0:T(8,128)S(1)}, f32[2,128,256]{2,1,0:T(8,128)S(1)}, u32[]{:S(2)}, u32[]{:S(2)}) collective-permute-start(f32[2,128,256]{2,1,0:T(8,128)S(1)} %get-tuple-element.47), channel_id=1, source_target_pairs={{0,17},{1,0},{2,19},{3,2},{8,25},{9,8},{10,27},{11,10},{16,1},{17,... | collective-permute-start | bytes 786440 | tf_op jit(solution)/shard_map/around/ppermute | solution.py:34
  74.7 5.8 %collective-permute-start.18 = (f32[2,128,256]{2,1,0:T(8,128)S(1)}, f32[2,128,256]{2,1,0:T(8,128)S(1)}, u32[]{:S(2)}, u32[]{:S(2)}) collective-permute-start(f32[2,128,256]{2,1,0:T(8,128)S(1)} %get-tuple-element.46), channel_id=1, source_target_pairs={{0,1},{1,16},{2,3},{3,18},{8,9},{9,24},{10,11},{11,26},{16,17},{17... | collective-permute-start | bytes 786440 | tf_op jit(solution)/shard_map/around/ppermute | solution.py:34
  80.8 16.3 %collective-permute-start.26 = (f32[2,128,256]{2,1,0:T(8,128)S(1)}, f32[2,128,256]{2,1,0:T(8,128)S(1)}, u32[]{:S(2)}, u32[]{:S(2)}) collective-permute-start(f32[2,128,256]{2,1,0:T(8,128)S(1)} %get-tuple-element.71), channel_id=1, source_target_pairs={{0,2},{1,3},{2,38},{3,54},{4,0},{5,1},{6,32},{7,33},{8,10},{9,11},... | collective-permute-start | bytes 786440 | tf_op jit(solution)/shard_map/over_y/ppermute | solution.py:34
  80.9 22.9 %collective-permute-start.24 = (f32[2,128,256]{2,1,0:T(8,128)S(1)}, f32[2,128,256]{2,1,0:T(8,128)S(1)}, u32[]{:S(2)}, u32[]{:S(2)}) collective-permute-start(f32[2,128,256]{2,1,0:T(8,128)S(1)} %get-tuple-element.70), channel_id=1, source_target_pairs={{0,32},{1,48},{2,98},{3,99},{4,2},{5,18},{6,0},{7,1},{8,40},{9,56}... | collective-permute-start | bytes 786440 | tf_op jit(solution)/shard_map/over_y/ppermute | solution.py:34
  92.6 11.2 %collective-permute-start.25 = (f32[2,128,256]{2,1,0:T(8,128)S(1)}, f32[2,128,256]{2,1,0:T(8,128)S(1)}, u32[]{:S(2)}, u32[]{:S(2)}) collective-permute-start(f32[2,128,256]{2,1,0:T(8,128)S(1)} %get-tuple-element.40), channel_id=1, source_target_pairs={{0,98},{1,114},{2,0},{3,1},{4,32},{5,33},{6,2},{7,18},{8,106},{9,1... | collective-permute-start | bytes 786440 | tf_op jit(solution)/shard_map/over_y/ppermute | solution.py:34
  95.8 12.1 %collective-permute-start.27 = (f32[2,128,256]{2,1,0:T(8,128)S(1)}, f32[2,128,256]{2,1,0:T(8,128)S(1)}, u32[]{:S(2)}, u32[]{:S(2)}) collective-permute-start(f32[2,128,256]{2,1,0:T(8,128)S(1)} %get-tuple-element.72), channel_id=1, source_target_pairs={{0,38},{1,39},{2,32},{3,48},{8,46},{9,47},{10,40},{11,56},{16,54},... | collective-permute-start | bytes 786440 | tf_op jit(solution)/shard_map/over_y/ppermute | solution.py:34
  (14 other events, 99.8 us)

commit v8 on v7

--- a/solution.py
+++ b/solution.py
@@ -125,7 +125,7 @@
             return jnp.where(column ^ h == 0, pick(first), pick(second))
 
         total = block(0)
-        for k in (1, 3, 2):
+        for k in (1, 3, 2) if active(0, 0, 0, 2, 0) else (3, 1, 2):
             def target(x, h, c, y, l, k=k):
                 to = (2 * h + l + k) % 4
                 return (x, to // 2, c, y, to % 2) if active(x, h, c, y, l) else None

time: 114 us -> 114 us (level)
  no operation moved by 1% of the time
where the time goes in v8:
time: 114 us
  starting transfers between devices  48.3 us (42%)
  waiting for transfers between devices  47.7 us (42%)
  matrix products  7.53 us (7%)
  local copies, waits for them, and re-layouts  7.26 us (6%)
  other arithmetic  1.78 us (2%)
  between operations  1.25 us (1%)
    ppermute x29, starting transfers between devices, send(): return lax.ppermute(value, AXES, pairs)  48.3 us
    ppermute x29, waiting for transfers between devices, send(): return lax.ppermute(value, AXES, pairs)  47.7 us
    dot_general x6, matrix products, inner(): lax.dot_general(left, right, (((0,), (0,)), ((), ())), preferred_element_...  6.95 us
  transfers between devices with their start and end apart: 29, of which 12 were waited for; matrix products, arithmetic and copies ran while one was open for 11% of the time, Pallas kernels for 0%

profile of v8, /device:TPU:25, one launch (start us, length us, event | category | flops | bytes accessed | tf_op | source)
XLA Modules:
  0.0 113.8 jit_solution(5596509094318147758)
XLA Ops:
  0.7 1.5 %constant_dynamic-slice_fusion = (bf16[3,3,192,128]{3,2,1,0:T(8,128)(2,1)S(1)}, bf16[3,3,192,128]{3,2,1,0:T(8,128)(2,1)S(1)}, bf16[3,3,192,128]{3,2,1,0:T(8,128)(2,1)S(1)}, bf16[3,3,192,128]{3,2,1,0:T(8,128)(2,1)S(1)}) fusion(bf16[3,12,192,128]{3,2,1,0:T(8,128)(2,1)} %param.2, s32[]{:T(128)S(6)} %select_n.507, s32[]{:T(128)S(6)} %select_n.505, ...), kind=kLoop, calls=%fused_computation.100 | loop fusion | bytes 3538960 | tf_op jit(solution)/shard_map/rows/dynamic_slice | solution.py:65
  2.3 1.4 %collective-permute-start = (bf16[3,3,192,128]{3,2,1,0:T(8,128)(2,1)S(1)}, bf16[3,3,192,128]{3,2,1,0:T(8,128)(2,1)S(1)}, u32[]{:S(2)}, u32[]{:S(2)}) collective-permute-start(bf16[3,3,192,128]{3,2,1,0:T(8,128)(2,1)S(1)} %get-tuple-element.43), channel_id=1, source_target_pairs={{0,7},{1,6},{2,5},{3,4},{4,3},{5,2},{6,1},{7,0},{8,15},{9,14},{10,... | collective-permute-start | bytes 1327112 | tf_op jit(solution)/shard_map/rows/ppermute | solution.py:34
  4.1 2.5 %collective-permute-start.1 = (bf16[1728,128]{1,0:T(8,128)(2,1)S(1)}, bf16[1728,128]{1,0:T(8,128)(2,1)S(1)}, u32[]{:S(2)}, u32[]{:S(2)}) collective-permute-start(bf16[1728,128]{1,0:T(8,128)(2,1)S(1)} %bitcast.194), channel_id=1, source_target_pairs={{0,96},{1,97},{2,98},{3,99},{4,100},{5,101},{6,102},{7,103},{8,104... | collective-permute-start | bytes 1327112 | tf_op jit(solution)/shard_map/first/ppermute | solution.py:34
  7.3 5.4 %collective-permute-start.6 = (bf16[3,3,192,128]{3,2,1,0:T(8,128)(2,1)S(1)}, bf16[3,3,192,128]{3,2,1,0:T(8,128)(2,1)S(1)}, u32[]{:S(2)}, u32[]{:S(2)}) collective-permute-start(bf16[3,3,192,128]{3,2,1,0:T(8,128)(2,1)S(1)} %get-tuple-element.42), channel_id=1, source_target_pairs={{0,23},{1,22},{2,21},{3,20},{4,19},{5,18},{6,17},{7,16},{8,31},{9,... | collective-permute-start | bytes 1327112 | tf_op jit(solution)/shard_map/rows/ppermute | solution.py:34
  12.7 2.8 %collective-permute-done = bf16[3,3,192,128]{3,2,1,0:T(8,128)(2,1)S(1)} collective-permute-done((bf16[3,3,192,128]{3,2,1,0:T(8,128)(2,1)S(1)}, bf16[3,3,192,128]{3,2,1,0:T(8,128)(2,1)S(1)}, u32[]{:S(2)}, u32[]{:S(2)}) %collective-permute-start) | collective-permute-done | bytes 442400 | tf_op jit(solution)/shard_map/rows/ppermute | solution.py:34
  15.8 2.8 %collective-permute-start.2 = (bf16[1728,128]{1,0:T(8,128)(2,1)S(1)}, bf16[1728,128]{1,0:T(8,128)(2,1)S(1)}, u32[]{:S(2)}, u32[]{:S(2)}) collective-permute-start(bf16[1728,128]{1,0:T(8,128)(2,1)S(1)} %bitcast.202), channel_id=1, source_target_pairs={{0,96},{1,97},{2,98},{3,99},{4,100},{5,101},{6,102},{7,103},{8,104... | collective-permute-start | bytes 1327112 | tf_op jit(solution)/shard_map/first/ppermute | solution.py:34
  19.3 12.5 %collective-permute-done.6 = bf16[3,3,192,128]{3,2,1,0:T(8,128)(2,1)S(1)} collective-permute-done((bf16[3,3,192,128]{3,2,1,0:T(8,128)(2,1)S(1)}, bf16[3,3,192,128]{3,2,1,0:T(8,128)(2,1)S(1)}, u32[]{:S(2)}, u32[]{:S(2)}) %collective-permute-start.6) | collective-permute-done | bytes 442400 | tf_op jit(solution)/shard_map/rows/ppermute | solution.py:34
  32.1 5.2 %collective-permute-done.5 = bf16[3,3,192,128]{3,2,1,0:T(8,128)(2,1)S(1)} collective-permute-done((bf16[3,3,192,128]{3,2,1,0:T(8,128)(2,1)S(1)}, bf16[3,3,192,128]{3,2,1,0:T(8,128)(2,1)S(1)}, u32[]{:S(2)}, u32[]{:S(2)}) %collective-permute-start.5) | collective-permute-done | bytes 442400 | tf_op jit(solution)/shard_map/rows/ppermute | solution.py:34
  39.3 2.5 %collective-permute-start.17 = (bf16[3456,128]{1,0:T(8,128)(2,1)S(1)}, bf16[3456,128]{1,0:T(8,128)(2,1)S(1)}, u32[]{:S(2)}, u32[]{:S(2)}) collective-permute-start(bf16[3456,128]{1,0:T(8,128)(2,1)S(1)} %pad_maximum_fusion), channel_id=1, source_target_pairs={{0,96},{1,97},{2,98},{3,99},{4,100},{5,101},{6,102},{7,103},{8,104... | collective-permute-start | bytes 2654216 | tf_op jit(solution)/shard_map/second/ppermute | solution.py:34
  48.2 2.5 %collective-permute-start.14 = (f32[2,128,256]{2,1,0:T(8,128)S(1)}, f32[2,128,256]{2,1,0:T(8,128)S(1)}, u32[]{:S(2)}, u32[]{:S(2)}) collective-permute-start(f32[2,128,256]{2,1,0:T(8,128)S(1)} %get-tuple-element.53), channel_id=1, source_target_pairs={{0,17},{1,0},{2,19},{3,2},{4,21},{5,4},{6,23},{7,6},{8,25},{9,8},{... | collective-permute-start | bytes 786440 | tf_op jit(solution)/shard_map/same/ppermute | solution.py:34
  51.9 5.3 %collective-permute-done.15 = f32[2,128,256]{2,1,0:T(8,128)S(1)} collective-permute-done((f32[2,128,256]{2,1,0:T(8,128)S(1)}, f32[2,128,256]{2,1,0:T(8,128)S(1)}, u32[]{:S(2)}, u32[]{:S(2)}) %collective-permute-start.15) | collective-permute-done | bytes 262176 | tf_op jit(solution)/shard_map/same/ppermute | solution.py:34
  57.2 2.1 %collective-permute-start.10 = (bf16[1728,128]{1,0:T(8,128)(2,1)S(1)}, bf16[1728,128]{1,0:T(8,128)(2,1)S(1)}, u32[]{:S(2)}, u32[]{:S(2)}) collective-permute-start(bf16[1728,128]{1,0:T(8,128)(2,1)S(1)} %copy-done.1), channel_id=1, source_target_pairs={{0,8},{1,9},{2,10},{3,11},{4,12},{5,13},{6,14},{7,15},{8,0},{9,1},... | collective-permute-start | bytes 1327112 | tf_op jit(solution)/shard_map/second/ppermute | solution.py:34
  60.2 1.3 %collective-permute-start.11 = (bf16[1728,128]{1,0:T(8,128)(2,1)S(1)}, bf16[1728,128]{1,0:T(8,128)(2,1)S(1)}, u32[]{:S(2)}, u32[]{:S(2)}) collective-permute-start(bf16[1728,128]{1,0:T(8,128)(2,1)S(1)} %copy-done.3), channel_id=1, source_target_pairs={{0,8},{1,9},{2,10},{3,11},{4,12},{5,13},{6,14},{7,15},{8,0},{9,1},... | collective-permute-start | bytes 1327112 | tf_op jit(solution)/shard_map/second/ppermute | solution.py:34
  61.5 2.0 %collective-permute-done.13 = f32[2,128,256]{2,1,0:T(8,128)S(1)} collective-permute-done((f32[2,128,256]{2,1,0:T(8,128)S(1)}, f32[2,128,256]{2,1,0:T(8,128)S(1)}, u32[]{:S(2)}, u32[]{:S(2)}) %collective-permute-start.13) | collective-permute-done | bytes 262176 | tf_op jit(solution)/shard_map/same/ppermute | solution.py:34
  65.0 1.4 %collective-permute-start.23 = (f32[2,128,256]{2,1,0:T(8,128)S(1)}, f32[2,128,256]{2,1,0:T(8,128)S(1)}, u32[]{:S(2)}, u32[]{:S(2)}) collective-permute-start(f32[2,128,256]{2,1,0:T(8,128)S(1)} %get-tuple-element.51), channel_id=1, source_target_pairs={{0,16},{1,17},{2,18},{3,19},{4,20},{5,21},{6,22},{7,23},{8,24},{9,... | collective-permute-start | bytes 786440 | tf_op jit(solution)/shard_map/beside/ppermute | solution.py:34
  66.3 1.3 %collective-permute-start.22 = (f32[2,128,256]{2,1,0:T(8,128)S(1)}, f32[2,128,256]{2,1,0:T(8,128)S(1)}, u32[]{:S(2)}, u32[]{:S(2)}) collective-permute-start(f32[2,128,256]{2,1,0:T(8,128)S(1)} %get-tuple-element.50), channel_id=1, source_target_pairs={{0,17},{1,0},{2,19},{3,2},{4,21},{5,4},{6,23},{7,6},{8,25},{9,8},{... | collective-permute-start | bytes 786440 | tf_op jit(solution)/shard_map/beside/ppermute | solution.py:34
  75.4 2.1 %collective-permute-done.22 = f32[2,128,256]{2,1,0:T(8,128)S(1)} collective-permute-done((f32[2,128,256]{2,1,0:T(8,128)S(1)}, f32[2,128,256]{2,1,0:T(8,128)S(1)}, u32[]{:S(2)}, u32[]{:S(2)}) %collective-permute-start.22) | collective-permute-done | bytes 262176 | tf_op jit(solution)/shard_map/beside/ppermute | solution.py:34
  77.5 2.9 %collective-permute-done.21 = f32[2,128,256]{2,1,0:T(8,128)S(1)} collective-permute-done((f32[2,128,256]{2,1,0:T(8,128)S(1)}, f32[2,128,256]{2,1,0:T(8,128)S(1)}, u32[]{:S(2)}, u32[]{:S(2)}) %collective-permute-start.21) | collective-permute-done | bytes 262176 | tf_op jit(solution)/shard_map/beside/ppermute | solution.py:34
  80.9 12.6 %collective-permute-start.24 = (f32[2,128,256]{2,1,0:T(8,128)S(1)}, f32[2,128,256]{2,1,0:T(8,128)S(1)}, u32[]{:S(2)}, u32[]{:S(2)}) collective-permute-start(f32[2,128,256]{2,1,0:T(8,128)S(1)} %get-tuple-element.70), channel_id=1, source_target_pairs={{0,32},{1,48},{2,98},{3,99},{4,2},{5,18},{6,0},{7,1},{8,40},{9,56}... | collective-permute-start | bytes 786440 | tf_op jit(solution)/shard_map/over_y/ppermute | solution.py:34
  93.5 2.8 %collective-permute-start.25 = (f32[2,128,256]{2,1,0:T(8,128)S(1)}, f32[2,128,256]{2,1,0:T(8,128)S(1)}, u32[]{:S(2)}, u32[]{:S(2)}) collective-permute-start(f32[2,128,256]{2,1,0:T(8,128)S(1)} %get-tuple-element.40), channel_id=1, source_target_pairs={{0,98},{1,114},{2,0},{3,1},{4,32},{5,33},{6,2},{7,18},{8,106},{9,1... | collective-permute-start | bytes 786440 | tf_op jit(solution)/shard_map/over_y/ppermute | solution.py:34
  96.3 1.3 %collective-permute-start.27 = (f32[2,128,256]{2,1,0:T(8,128)S(1)}, f32[2,128,256]{2,1,0:T(8,128)S(1)}, u32[]{:S(2)}, u32[]{:S(2)}) collective-permute-start(f32[2,128,256]{2,1,0:T(8,128)S(1)} %get-tuple-element.72), channel_id=1, source_target_pairs={{0,38},{1,39},{2,32},{3,48},{8,46},{9,47},{10,40},{11,56},{16,54},... | collective-permute-start | bytes 786440 | tf_op jit(solution)/shard_map/over_y/ppermute | solution.py:34
  97.6 7.0 %collective-permute-done.24 = f32[2,128,256]{2,1,0:T(8,128)S(1)} collective-permute-done((f32[2,128,256]{2,1,0:T(8,128)S(1)}, f32[2,128,256]{2,1,0:T(8,128)S(1)}, u32[]{:S(2)}, u32[]{:S(2)}) %collective-permute-start.24) | collective-permute-done | bytes 262176 | tf_op jit(solution)/shard_map/over_y/ppermute | solution.py:34
  104.7 4.9 %collective-permute-done.27 = f32[2,128,256]{2,1,0:T(8,128)S(1)} collective-permute-done((f32[2,128,256]{2,1,0:T(8,128)S(1)}, f32[2,128,256]{2,1,0:T(8,128)S(1)}, u32[]{:S(2)}, u32[]{:S(2)}) %collective-permute-start.27) | collective-permute-done | bytes 262176 | tf_op jit(solution)/shard_map/over_y/ppermute | solution.py:34
  109.9 2.1 %collective-permute-start.28 = (f32[128,256]{1,0:T(8,128)S(1)}, f32[128,256]{1,0:T(8,128)S(1)}, u32[]{:S(2)}, u32[]{:S(2)}) collective-permute-start(f32[128,256]{1,0:T(8,128)S(1)} %get-tuple-element.67), channel_id=1, source_target_pairs={{0,8},{1,9},{2,10},{3,11},{4,12},{5,13},{6,14},{7,15},{8,0},{9,1},... | collective-permute-start | bytes 393224 | tf_op jit(solution)/shard_map/place/ppermute | solution.py:34
  (99 shorter events, 24.4 us)
Async XLA Ops:
  2.3 13.2 %collective-permute-start = (bf16[3,3,192,128]{3,2,1,0:T(8,128)(2,1)S(1)}, bf16[3,3,192,128]{3,2,1,0:T(8,128)(2,1)S(1)}, u32[]{:S(2)}, u32[]{:S(2)}) collective-permute-start(bf16[3,3,192,128]{3,2,1,0:T(8,128)(2,1)S(1)} %get-tuple-element.43), channel_id=1, source_target_pairs={{0,7},{1,6},{2,5},{3,4},{4,3},{5,2},{6,1},{7,0},{8,15},{9,14},{10,... | collective-permute-start | bytes 1327112 | tf_op jit(solution)/shard_map/rows/ppermute | solution.py:34
  4.1 11.7 %collective-permute-start.1 = (bf16[1728,128]{1,0:T(8,128)(2,1)S(1)}, bf16[1728,128]{1,0:T(8,128)(2,1)S(1)}, u32[]{:S(2)}, u32[]{:S(2)}) collective-permute-start(bf16[1728,128]{1,0:T(8,128)(2,1)S(1)} %bitcast.194), channel_id=1, source_target_pairs={{0,96},{1,97},{2,98},{3,99},{4,100},{5,101},{6,102},{7,103},{8,104... | collective-permute-start | bytes 1327112 | tf_op jit(solution)/shard_map/first/ppermute | solution.py:34
  6.7 11.9 %collective-permute-start.3 = (bf16[1728,128]{1,0:T(8,128)(2,1)S(1)}, bf16[1728,128]{1,0:T(8,128)(2,1)S(1)}, u32[]{:S(2)}, u32[]{:S(2)}) collective-permute-start(bf16[1728,128]{1,0:T(8,128)(2,1)S(1)} %bitcast.195), channel_id=1, source_target_pairs={{2,34},{3,35},{4,36},{5,37},{10,42},{11,43},{12,44},{13,45},{18,50... | collective-permute-start | bytes 1327112 | tf_op jit(solution)/shard_map/first/ppermute | solution.py:34
  7.3 24.5 %collective-permute-start.6 = (bf16[3,3,192,128]{3,2,1,0:T(8,128)(2,1)S(1)}, bf16[3,3,192,128]{3,2,1,0:T(8,128)(2,1)S(1)}, u32[]{:S(2)}, u32[]{:S(2)}) collective-permute-start(bf16[3,3,192,128]{3,2,1,0:T(8,128)(2,1)S(1)} %get-tuple-element.42), channel_id=1, source_target_pairs={{0,23},{1,22},{2,21},{3,20},{4,19},{5,18},{6,17},{7,16},{8,31},{9,... | collective-permute-start | bytes 1327112 | tf_op jit(solution)/shard_map/rows/ppermute | solution.py:34
  12.7 24.5 %collective-permute-start.5 = (bf16[3,3,192,128]{3,2,1,0:T(8,128)(2,1)S(1)}, bf16[3,3,192,128]{3,2,1,0:T(8,128)(2,1)S(1)}, u32[]{:S(2)}, u32[]{:S(2)}) collective-permute-start(bf16[3,3,192,128]{3,2,1,0:T(8,128)(2,1)S(1)} %get-tuple-element.45), channel_id=1, source_target_pairs={{0,16},{1,17},{2,18},{3,19},{4,20},{5,21},{6,22},{7,23},{8,24},{9,... | collective-permute-start | bytes 1327112 | tf_op jit(solution)/shard_map/rows/ppermute | solution.py:34
  15.8 22.1 %collective-permute-start.2 = (bf16[1728,128]{1,0:T(8,128)(2,1)S(1)}, bf16[1728,128]{1,0:T(8,128)(2,1)S(1)}, u32[]{:S(2)}, u32[]{:S(2)}) collective-permute-start(bf16[1728,128]{1,0:T(8,128)(2,1)S(1)} %bitcast.202), channel_id=1, source_target_pairs={{0,96},{1,97},{2,98},{3,99},{4,100},{5,101},{6,102},{7,103},{8,104... | collective-permute-start | bytes 1327112 | tf_op jit(solution)/shard_map/first/ppermute | solution.py:34
  18.6 19.4 %collective-permute-start.4 = (bf16[1728,128]{1,0:T(8,128)(2,1)S(1)}, bf16[1728,128]{1,0:T(8,128)(2,1)S(1)}, u32[]{:S(2)}, u32[]{:S(2)}) collective-permute-start(bf16[1728,128]{1,0:T(8,128)(2,1)S(1)} %bitcast.203), channel_id=1, source_target_pairs={{2,34},{3,35},{4,36},{5,37},{10,42},{11,43},{12,44},{13,45},{18,50... | collective-permute-start | bytes 1327112 | tf_op jit(solution)/shard_map/first/ppermute | solution.py:34
  39.3 24.3 %collective-permute-start.17 = (bf16[3456,128]{1,0:T(8,128)(2,1)S(1)}, bf16[3456,128]{1,0:T(8,128)(2,1)S(1)}, u32[]{:S(2)}, u32[]{:S(2)}) collective-permute-start(bf16[3456,128]{1,0:T(8,128)(2,1)S(1)} %pad_maximum_fusion), channel_id=1, source_target_pairs={{0,96},{1,97},{2,98},{3,99},{4,100},{5,101},{6,102},{7,103},{8,104... | collective-permute-start | bytes 2654216 | tf_op jit(solution)/shard_map/second/ppermute | solution.py:34
  41.7 25.9 %collective-permute-start.12 = (bf16[3456,128]{1,0:T(8,128)(2,1)S(1)}, bf16[3456,128]{1,0:T(8,128)(2,1)S(1)}, u32[]{:S(2)}, u32[]{:S(2)}) collective-permute-start(bf16[3456,128]{1,0:T(8,128)(2,1)S(1)} %pad_maximum_fusion), channel_id=1, source_target_pairs={{2,34},{3,35},{4,36},{5,37},{10,42},{11,43},{12,44},{13,45},{18,50... | collective-permute-start | bytes 2654216 | tf_op jit(solution)/shard_map/second/ppermute | solution.py:34
  48.1 9.1 %collective-permute-start.15 = (f32[2,128,256]{2,1,0:T(8,128)S(1)}, f32[2,128,256]{2,1,0:T(8,128)S(1)}, u32[]{:S(2)}, u32[]{:S(2)}) collective-permute-start(f32[2,128,256]{2,1,0:T(8,128)S(1)} %get-tuple-element.54), channel_id=1, source_target_pairs={{0,16},{1,17},{2,18},{3,19},{4,20},{5,21},{6,22},{7,23},{8,24},{9,... | collective-permute-start | bytes 786440 | tf_op jit(solution)/shard_map/same/ppermute | solution.py:34
  48.2 12.0 %collective-permute-start.14 = (f32[2,128,256]{2,1,0:T(8,128)S(1)}, f32[2,128,256]{2,1,0:T(8,128)S(1)}, u32[]{:S(2)}, u32[]{:S(2)}) collective-permute-start(f32[2,128,256]{2,1,0:T(8,128)S(1)} %get-tuple-element.53), channel_id=1, source_target_pairs={{0,17},{1,0},{2,19},{3,2},{4,21},{5,4},{6,23},{7,6},{8,25},{9,8},{... | collective-permute-start | bytes 786440 | tf_op jit(solution)/shard_map/same/ppermute | solution.py:34
  50.7 12.8 %collective-permute-start.13 = (f32[2,128,256]{2,1,0:T(8,128)S(1)}, f32[2,128,256]{2,1,0:T(8,128)S(1)}, u32[]{:S(2)}, u32[]{:S(2)}) collective-permute-start(f32[2,128,256]{2,1,0:T(8,128)S(1)} %get-tuple-element.52), channel_id=1, source_target_pairs={{0,1},{1,16},{2,3},{3,18},{4,5},{5,20},{6,7},{7,22},{8,9},{9,24},{... | collective-permute-start | bytes 786440 | tf_op jit(solution)/shard_map/same/ppermute | solution.py:34
  57.2 10.6 %collective-permute-start.10 = (bf16[1728,128]{1,0:T(8,128)(2,1)S(1)}, bf16[1728,128]{1,0:T(8,128)(2,1)S(1)}, u32[]{:S(2)}, u32[]{:S(2)}) collective-permute-start(bf16[1728,128]{1,0:T(8,128)(2,1)S(1)} %copy-done.1), channel_id=1, source_target_pairs={{0,8},{1,9},{2,10},{3,11},{4,12},{5,13},{6,14},{7,15},{8,0},{9,1},... | collective-permute-start | bytes 1327112 | tf_op jit(solution)/shard_map/second/ppermute | solution.py:34
  60.2 8.5 %collective-permute-start.11 = (bf16[1728,128]{1,0:T(8,128)(2,1)S(1)}, bf16[1728,128]{1,0:T(8,128)(2,1)S(1)}, u32[]{:S(2)}, u32[]{:S(2)}) collective-permute-start(bf16[1728,128]{1,0:T(8,128)(2,1)S(1)} %copy-done.3), channel_id=1, source_target_pairs={{0,8},{1,9},{2,10},{3,11},{4,12},{5,13},{6,14},{7,15},{8,0},{9,1},... | collective-permute-start | bytes 1327112 | tf_op jit(solution)/shard_map/second/ppermute | solution.py:34
  65.0 9.8 %collective-permute-start.23 = (f32[2,128,256]{2,1,0:T(8,128)S(1)}, f32[2,128,256]{2,1,0:T(8,128)S(1)}, u32[]{:S(2)}, u32[]{:S(2)}) collective-permute-start(f32[2,128,256]{2,1,0:T(8,128)S(1)} %get-tuple-element.51), channel_id=1, source_target_pairs={{0,16},{1,17},{2,18},{3,19},{4,20},{5,21},{6,22},{7,23},{8,24},{9,... | collective-permute-start | bytes 786440 | tf_op jit(solution)/shard_map/beside/ppermute | solution.py:34
  66.3 11.2 %collective-permute-start.22 = (f32[2,128,256]{2,1,0:T(8,128)S(1)}, f32[2,128,256]{2,1,0:T(8,128)S(1)}, u32[]{:S(2)}, u32[]{:S(2)}) collective-permute-start(f32[2,128,256]{2,1,0:T(8,128)S(1)} %get-tuple-element.50), channel_id=1, source_target_pairs={{0,17},{1,0},{2,19},{3,2},{4,21},{5,4},{6,23},{7,6},{8,25},{9,8},{... | collective-permute-start | bytes 786440 | tf_op jit(solution)/shard_map/beside/ppermute | solution.py:34
  67.6 12.8 %collective-permute-start.21 = (f32[2,128,256]{2,1,0:T(8,128)S(1)}, f32[2,128,256]{2,1,0:T(8,128)S(1)}, u32[]{:S(2)}, u32[]{:S(2)}) collective-permute-start(f32[2,128,256]{2,1,0:T(8,128)S(1)} %get-tuple-element.49), channel_id=1, source_target_pairs={{0,1},{1,16},{2,3},{3,18},{4,5},{5,20},{6,7},{7,22},{8,9},{9,24},{... | collective-permute-start | bytes 786440 | tf_op jit(solution)/shard_map/beside/ppermute | solution.py:34
  73.4 7.2 %collective-permute-start.20 = (f32[2,128,256]{2,1,0:T(8,128)S(1)}, f32[2,128,256]{2,1,0:T(8,128)S(1)}, u32[]{:S(2)}, u32[]{:S(2)}) collective-permute-start(f32[2,128,256]{2,1,0:T(8,128)S(1)} %get-tuple-element.48), channel_id=1, source_target_pairs={{0,16},{1,17},{2,18},{3,19},{8,24},{9,25},{10,26},{11,27},{16,0},{... | collective-permute-start | bytes 786440 | tf_op jit(solution)/shard_map/around/ppermute | solution.py:34
  74.1 6.5 %collective-permute-start.19 = (f32[2,128,256]{2,1,0:T(8,128)S(1)}, f32[2,128,256]{2,1,0:T(8,128)S(1)}, u32[]{:S(2)}, u32[]{:S(2)}) collective-permute-start(f32[2,128,256]{2,1,0:T(8,128)S(1)} %get-tuple-element.47), channel_id=1, source_target_pairs={{0,1},{1,16},{2,3},{3,18},{8,9},{9,24},{10,11},{11,26},{16,17},{17... | collective-permute-start | bytes 786440 | tf_op jit(solution)/shard_map/around/ppermute | solution.py:34
  74.7 5.8 %collective-permute-start.18 = (f32[2,128,256]{2,1,0:T(8,128)S(1)}, f32[2,128,256]{2,1,0:T(8,128)S(1)}, u32[]{:S(2)}, u32[]{:S(2)}) collective-permute-start(f32[2,128,256]{2,1,0:T(8,128)S(1)} %get-tuple-element.46), channel_id=1, source_target_pairs={{0,17},{1,0},{2,19},{3,2},{8,25},{9,8},{10,27},{11,10},{16,1},{17,... | collective-permute-start | bytes 786440 | tf_op jit(solution)/shard_map/around/ppermute | solution.py:34
  80.8 16.8 %collective-permute-start.26 = (f32[2,128,256]{2,1,0:T(8,128)S(1)}, f32[2,128,256]{2,1,0:T(8,128)S(1)}, u32[]{:S(2)}, u32[]{:S(2)}) collective-permute-start(f32[2,128,256]{2,1,0:T(8,128)S(1)} %get-tuple-element.71), channel_id=1, source_target_pairs={{0,2},{1,3},{2,38},{3,54},{4,0},{5,1},{6,32},{7,33},{8,10},{9,11},... | collective-permute-start | bytes 786440 | tf_op jit(solution)/shard_map/over_y/ppermute | solution.py:34
  80.9 23.8 %collective-permute-start.24 = (f32[2,128,256]{2,1,0:T(8,128)S(1)}, f32[2,128,256]{2,1,0:T(8,128)S(1)}, u32[]{:S(2)}, u32[]{:S(2)}) collective-permute-start(f32[2,128,256]{2,1,0:T(8,128)S(1)} %get-tuple-element.70), channel_id=1, source_target_pairs={{0,32},{1,48},{2,98},{3,99},{4,2},{5,18},{6,0},{7,1},{8,40},{9,56}... | collective-permute-start | bytes 786440 | tf_op jit(solution)/shard_map/over_y/ppermute | solution.py:34
  93.5 11.2 %collective-permute-start.25 = (f32[2,128,256]{2,1,0:T(8,128)S(1)}, f32[2,128,256]{2,1,0:T(8,128)S(1)}, u32[]{:S(2)}, u32[]{:S(2)}) collective-permute-start(f32[2,128,256]{2,1,0:T(8,128)S(1)} %get-tuple-element.40), channel_id=1, source_target_pairs={{0,98},{1,114},{2,0},{3,1},{4,32},{5,33},{6,2},{7,18},{8,106},{9,1... | collective-permute-start | bytes 786440 | tf_op jit(solution)/shard_map/over_y/ppermute | solution.py:34
  96.3 13.2 %collective-permute-start.27 = (f32[2,128,256]{2,1,0:T(8,128)S(1)}, f32[2,128,256]{2,1,0:T(8,128)S(1)}, u32[]{:S(2)}, u32[]{:S(2)}) collective-permute-start(f32[2,128,256]{2,1,0:T(8,128)S(1)} %get-tuple-element.72), channel_id=1, source_target_pairs={{0,38},{1,39},{2,32},{3,48},{8,46},{9,47},{10,40},{11,56},{16,54},... | collective-permute-start | bytes 786440 | tf_op jit(solution)/shard_map/over_y/ppermute | solution.py:34
  (14 other events, 99.0 us)
